TPU v7x, 32 devices: a whole 2x2x4 slice. The times are simulated.
32 devices in a mesh: dp: 4 (over x, core), expert: 8 (over z, y).
Axes of the slice: x: 2, y: 2, z: 4, core: 2. Of those that a mesh axis runs over, the one named last changes fastest.
Arguments:
- tokens: bfloat16 [32768, 768], P(('dp', 'expert')), may hold values from -6 to 6
- segments: int32 [32, 1024], P(('dp', 'expert')), may hold values from 0 to 7, never falling along the last dimension, each value on 1 to 512 neighbouring positions
- routes: int32 [32768, 1], P(('dp', 'expert')), may hold values from 0 to 7
- cotangent: bfloat16 [32768, 768], P(('dp', 'expert')), may hold values from -6 to 6
- attn_gain: float32 [768], replicated, may hold values from 0.5 to 1.5
- ffn_gain: float32 [768], replicated, may hold values from 0.5 to 1.5
- query_weight: bfloat16 [768, 768], replicated, may hold values from -0.21875 to 0.21875
- key_weight: bfloat16 [768, 768], replicated, may hold values from -0.21875 to 0.21875
- value_weight: bfloat16 [768, 768], replicated, may hold values from -0.21875 to 0.21875
- output_weight: bfloat16 [768, 768], replicated, may hold values from -0.875 to 0.875
- position_bias_grid: float32 [32, 12], replicated, may hold values from -6 to 6
- router_weight: float32 [768, 8], replicated, may hold values from -0.15625 to 0.15625
- expert_in: bfloat16 [8, 768, 3072], P('expert'), may hold values from -0.21875 to 0.21875
- expert_out: bfloat16 [8, 3072, 768], P('expert'), may hold values from -0.875 to 0.875
Outputs:
- mixed: bfloat16 [32768, 768], P(('dp', 'expert'))
- grad_tokens: bfloat16 [32768, 768], P(('dp', 'expert'))
- grad_attn_gain: float32 [768], replicated
- grad_ffn_gain: float32 [768], replicated
- grad_query: float32 [768, 768], replicated
- grad_key: float32 [768, 768], replicated
- grad_value: float32 [768, 768], replicated
- grad_output: float32 [768, 768], replicated
- grad_bias: float32 [32, 12], replicated
- grad_router: float32 [768, 8], replicated
- grad_expert_in: float32 [8, 768, 3072], P('expert', None, 'dp')
- grad_expert_out: float32 [8, 3072, 768], P('expert', 'dp')
All inputs are finite; a program needn't handle non-finite values.
Results may differ from a plain program's by a relative error of at most 0.017.
Values may be sent and summed in bfloat16 or wider, within the bound.
A program may use at most 320 MiB of HBM per device.

v0:
```python
from functools import partial

import jax
import jax.numpy as jnp
from jax import lax
from jax.sharding import PartitionSpec as P

epsilon = 1e-06
masked_score = -1e30
bucket_bounds = (12, 16, 23, 32, 46, 64, 91)
precise_setting = lax.Precision.HIGHEST


def bucket_of(relative):
    distance = jnp.abs(relative)
    beyond = jnp.zeros_like(distance)
    for threshold in bucket_bounds:
        beyond = beyond + (distance >= threshold).astype(jnp.int32)
    inside = jnp.where(distance < 8, distance, 8 + beyond)
    return inside + 16 * (relative > 0).astype(jnp.int32)


def bucket_table(first_row, row_count, length, bucket_count):
    relative = (
        lax.iota(jnp.int32, length)[None, :] - (first_row + lax.iota(jnp.int32, row_count))[:, None]
    )
    bucket_ids = lax.iota(jnp.int32, bucket_count)
    return (bucket_of(relative)[None, :, :] == bucket_ids[:, None, None]).astype(jnp.bfloat16)


def rms_forward(values, norm_gain):
    inverse = lax.rsqrt(jnp.mean(values * values, -1, keepdims=True) + epsilon)
    return (values * inverse * norm_gain, inverse)


def rms_backward(values, inverse, norm_gain, upstream):
    scaled = upstream * norm_gain
    gain_grad = jnp.sum(upstream * values * inverse, 0)
    input_grad = inverse * (
        scaled - values * inverse * inverse * jnp.mean(scaled * values, -1, keepdims=True)
    )
    return (input_grad, gain_grad)


def block_scores(query_block, key_seq, bias_block, segment_row, first_row, row_count, score_scale):
    scores = (
        jnp.einsum("hqc,hkc->hqk", query_block, key_seq, preferred_element_type=jnp.float32)
        * score_scale
    )
    scores = scores + bias_block
    same_doc = segment_row[first_row : first_row + row_count, None] == segment_row[None, :]
    return jnp.where(same_doc[None], scores, masked_score)


def with_zero_row(rows):
    return jnp.concatenate([rows, jnp.zeros((1, rows.shape[1]), rows.dtype)], 0)


def per_device(
    tokens,
    segments,
    routes,
    cotangent,
    attn_gain,
    ffn_gain,
    query_weight,
    key_weight,
    value_weight,
    output_weight,
    position_bias_grid,
    router_weight,
    expert_in,
    expert_out,
):
    token_count, model_width = tokens.shape
    seq_count, length = segments.shape
    bucket_count, head_count = position_bias_grid.shape
    head_width = model_width // head_count
    score_scale = head_width ** (-0.5)
    block_rows = min(512, length)
    experts_all = router_weight.shape[1]
    local_experts = expert_in.shape[0]
    groups = lax.axis_size("expert")
    capacity = (5 * token_count + 4 * experts_all - 1) // (4 * experts_all)
    head_weight_shape = (model_width, head_count, head_width)
    per_head_queries = query_weight.reshape(head_weight_shape)
    per_head_keys = key_weight.reshape(head_weight_shape)
    per_head_values = value_weight.reshape(head_weight_shape)
    output_heads = output_weight.reshape(head_count, head_width, model_width)
    inputs = tokens.astype(jnp.float32)
    normed, inverse_one = rms_forward(inputs, attn_gain)
    normed_low = normed.astype(jnp.bfloat16)
    normalized_sequence = normed_low.reshape(seq_count, length, model_width)
    queries = jnp.einsum(
        "ifr,rma->imfa", normalized_sequence, per_head_queries, preferred_element_type=jnp.float32
    ).astype(jnp.bfloat16)
    key_rows = jnp.einsum(
        "ifr,rma->imfa", normalized_sequence, per_head_keys, preferred_element_type=jnp.float32
    ).astype(jnp.bfloat16)
    value_rows = jnp.einsum(
        "ifr,rma->imfa", normalized_sequence, per_head_values, preferred_element_type=jnp.float32
    ).astype(jnp.bfloat16)
    block_starts = list(range(0, length, block_rows))
    onehot_bucket_grids = [
        bucket_table(first_row, block_rows, length, bucket_count) for first_row in block_starts
    ]
    bias_blocks = [
        jnp.einsum(
            "gps,gv->vps",
            onehot_bucket.astype(jnp.float32),
            position_bias_grid,
            precision=precise_setting,
        )
        for onehot_bucket in onehot_bucket_grids
    ]
    log_sums = []
    seq_index = 0
    seq_outputs = []
    for block_ordinal, first_row in enumerate(block_starts):
        query_block = queries[seq_index, :, first_row : first_row + block_rows]
        scores = block_scores(
            query_block,
            key_rows[seq_index],
            bias_blocks[block_ordinal],
            segments[seq_index],
            first_row,
            block_rows,
            score_scale,
        )
        highest = jnp.max(scores, -1, keepdims=True)
        exponents = jnp.exp(scores - highest)
        totals = jnp.sum(exponents, -1, keepdims=True)
        attention = exponents / totals
        log_sums.append(highest + jnp.log(totals))
        seq_outputs.append(
            jnp.einsum(
                "hqk,hkc->hqc",
                attention.astype(jnp.bfloat16),
                value_rows[seq_index],
                preferred_element_type=jnp.float32,
            )
        )
    outputs = [jnp.concatenate(seq_outputs, 1)]
    attended = jnp.stack(outputs, 0).astype(jnp.bfloat16)
    projected = jnp.einsum(
        "shlc,hcm->slm", attended, output_heads, preferred_element_type=jnp.float32
    )
    middle = inputs + projected.reshape(token_count, model_width)
    hidden_two, inverse_two = rms_forward(middle, ffn_gain)
    logits = jnp.dot(hidden_two, router_weight, precision=precise_setting)
    top_logit = jnp.max(logits, -1, keepdims=True)
    exponents_router = jnp.exp(logits - top_logit)
    router_probs = exponents_router / jnp.sum(exponents_router, -1, keepdims=True)
    chosen = routes[:, 0]
    expert_hot = (chosen[:, None] == lax.iota(jnp.int32, experts_all)[None, :]).astype(jnp.int32)
    expert_float = expert_hot.astype(jnp.float32)
    slot_rank = jnp.sum((jnp.cumsum(expert_hot, 0) - expert_hot) * expert_hot, 1)
    dump_slot = experts_all * capacity
    token_slot = jnp.where(slot_rank < capacity, chosen * capacity + slot_rank, dump_slot)
    slot_token = (
        jnp.full((dump_slot + 1,), token_count, jnp.int32)
        .at[token_slot]
        .set(lax.iota(jnp.int32, token_count))[:dump_slot]
    )
    gate_values = jnp.sum(router_probs * expert_float, 1)
    slots_out = jnp.take(with_zero_row(hidden_two.astype(jnp.bfloat16)), slot_token, axis=0)
    slots_out = slots_out.reshape(experts_all, capacity, model_width)
    arrived = lax.all_to_all(slots_out, "expert", split_axis=0, concat_axis=0, tiled=True)
    arrived = arrived.reshape(groups, local_experts, capacity, model_width)
    pre_act = jnp.einsum("secd,edf->secf", arrived, expert_in, preferred_element_type=jnp.float32)
    activated = jax.nn.gelu(pre_act, approximate=False).astype(jnp.bfloat16)
    produced = jnp.einsum(
        "secf,efd->secd", activated, expert_out, preferred_element_type=jnp.float32
    )
    produced = produced.astype(jnp.bfloat16).reshape(experts_all, capacity, model_width)
    returned = lax.all_to_all(produced, "expert", split_axis=0, concat_axis=0, tiled=True)
    expert_rows = jnp.take(
        with_zero_row(returned.reshape(dump_slot, model_width)), token_slot, axis=0
    )
    expert_rows = expert_rows.astype(jnp.float32)
    mixed = (middle + gate_values[:, None] * expert_rows).astype(jnp.bfloat16)
    upstream = cotangent.astype(jnp.float32)
    gate_grad = jnp.sum(upstream * expert_rows, 1)
    out_grad_rows = with_zero_row((gate_values[:, None] * upstream).astype(jnp.bfloat16))
    grad_slots = jnp.take(out_grad_rows, slot_token, axis=0).reshape(
        experts_all, capacity, model_width
    )
    grad_arrived, inputs_again = (
        lax.all_to_all(grad_slots, "expert", split_axis=0, concat_axis=0, tiled=True),
        lax.all_to_all(slots_out, "expert", split_axis=0, concat_axis=0, tiled=True),
    )
    inputs_again = inputs_again.reshape(groups, local_experts, capacity, model_width)
    pre_again = jnp.einsum(
        "secd,edf->secf", inputs_again, expert_in, preferred_element_type=jnp.float32
    )
    activated_again = jax.nn.gelu(pre_again, approximate=False).astype(jnp.bfloat16)
    grad_arrived = grad_arrived.reshape(groups, local_experts, capacity, model_width)
    act_grad = jnp.einsum(
        "secd,efd->secf", grad_arrived, expert_out, preferred_element_type=jnp.float32
    )
    _, gelu_pull = jax.vjp(partial(jax.nn.gelu, approximate=False), pre_again)
    pre_grad = gelu_pull(act_grad)[0].astype(jnp.bfloat16)
    out_weight_grad = jnp.einsum(
        "secf,secd->efd", activated_again, grad_arrived, preferred_element_type=jnp.float32
    )
    in_weight_grad = jnp.einsum(
        "secd,secf->edf", inputs_again, pre_grad, preferred_element_type=jnp.float32
    )
    input_slot_grad = jnp.einsum(
        "secf,edf->secd", pre_grad, expert_in, preferred_element_type=jnp.float32
    )
    input_slot_grad = input_slot_grad.astype(jnp.bfloat16).reshape(
        experts_all, capacity, model_width
    )
    home_grad = lax.all_to_all(input_slot_grad, "expert", split_axis=0, concat_axis=0, tiled=True)
    in_weight_grad, out_weight_grad = (
        lax.psum_scatter(
            in_weight_grad.astype(jnp.bfloat16), "dp", scatter_dimension=2, tiled=True
        ).astype(jnp.float32),
        lax.psum_scatter(
            out_weight_grad.astype(jnp.bfloat16), "dp", scatter_dimension=1, tiled=True
        ).astype(jnp.float32),
    )
    expert_input_grad = jnp.take(
        with_zero_row(home_grad.reshape(dump_slot, model_width)), token_slot, axis=0
    )
    logit_grad = router_probs * (
        expert_float * gate_grad[:, None] - (gate_values * gate_grad)[:, None]
    )
    router_grad = jnp.dot(hidden_two.T, logit_grad, precision=precise_setting)
    hidden_grad = expert_input_grad.astype(jnp.float32) + jnp.dot(
        logit_grad, router_weight.T, precision=precise_setting
    )
    middle_part, ffn_gain_grad = rms_backward(middle, inverse_two, ffn_gain, hidden_grad)
    middle_grad = upstream + middle_part
    branch_grad = middle_grad.astype(jnp.bfloat16).reshape(seq_count, length, model_width)
    output_weight_grad = jnp.einsum(
        "shlc,slm->hcm", attended, branch_grad, preferred_element_type=jnp.float32
    ).reshape(model_width, model_width)
    attended_grad = jnp.einsum(
        "slm,hcm->shlc", branch_grad, output_heads, preferred_element_type=jnp.float32
    ).astype(jnp.bfloat16)
    table_grad = jnp.zeros((bucket_count, head_count), jnp.float32)
    block_index = 0
    seq_index = 0
    key_sum = jnp.zeros((head_count, length, head_width), jnp.float32)
    value_sum = jnp.zeros((head_count, length, head_width), jnp.float32)
    seq_query_grads = []
    for block_ordinal, first_row in enumerate(block_starts):
        query_block = queries[seq_index, :, first_row : first_row + block_rows]
        grad_block = attended_grad[seq_index, :, first_row : first_row + block_rows]
        scores = block_scores(
            query_block,
            key_rows[seq_index],
            bias_blocks[block_ordinal],
            segments[seq_index],
            first_row,
            block_rows,
            score_scale,
        )
        attention = jnp.exp(scores - log_sums[block_index])
        block_index = block_index + 1
        prob_grad = jnp.einsum(
            "hqc,hkc->hqk", grad_block, value_rows[seq_index], preferred_element_type=jnp.float32
        )
        inner = jnp.sum(attention * prob_grad, -1, keepdims=True)
        scores_gradient = (attention * (prob_grad - inner)).astype(jnp.bfloat16)
        seq_query_grads.append(
            (
                jnp.einsum(
                    "hqk,hkc->hqc",
                    scores_gradient,
                    key_rows[seq_index],
                    preferred_element_type=jnp.float32,
                )
                * score_scale
            ).astype(jnp.bfloat16)
        )
        key_sum = (
            key_sum
            + jnp.einsum(
                "hqk,hqc->hkc", scores_gradient, query_block, preferred_element_type=jnp.float32
            )
            * score_scale
        )
        value_sum = value_sum + jnp.einsum(
            "hqk,hqc->hkc",
            attention.astype(jnp.bfloat16),
            grad_block,
            preferred_element_type=jnp.float32,
        )
        table_grad = table_grad + jnp.einsum(
            "avx,ovx->ao",
            onehot_bucket_grids[block_ordinal],
            scores_gradient,
            preferred_element_type=jnp.float32,
        )
    query_grads = [jnp.concatenate(seq_query_grads, 1)]
    key_grads = [key_sum.astype(jnp.bfloat16)]
    value_grads = [value_sum.astype(jnp.bfloat16)]
    full_query_gradient = jnp.stack(query_grads, 0)
    full_key_gradient = jnp.stack(key_grads, 0)
    full_value_gradient = jnp.stack(value_grads, 0)
    query_weight_grad = jnp.einsum(
        "fwn,fbwy->nby",
        normalized_sequence,
        full_query_gradient,
        preferred_element_type=jnp.float32,
    ).reshape(model_width, model_width)
    key_weight_grad = jnp.einsum(
        "fwn,fbwy->nby", normalized_sequence, full_key_gradient, preferred_element_type=jnp.float32
    ).reshape(model_width, model_width)
    value_weight_grad = jnp.einsum(
        "fwn,fbwy->nby",
        normalized_sequence,
        full_value_gradient,
        preferred_element_type=jnp.float32,
    ).reshape(model_width, model_width)
    normed_grad = jnp.einsum(
        "orxq,prq->oxp", full_query_gradient, per_head_queries, preferred_element_type=jnp.float32
    )
    normed_grad = normed_grad + jnp.einsum(
        "orxq,prq->oxp", full_key_gradient, per_head_keys, preferred_element_type=jnp.float32
    )
    normed_grad = normed_grad + jnp.einsum(
        "orxq,prq->oxp", full_value_gradient, per_head_values, preferred_element_type=jnp.float32
    )
    normed_grad = normed_grad.reshape(token_count, model_width)
    input_part, attn_gain_grad = rms_backward(inputs, inverse_one, attn_gain, normed_grad)
    token_grad = (middle_grad + input_part).astype(jnp.bfloat16)
    summed = lax.psum(
        (
            query_weight_grad,
            key_weight_grad,
            value_weight_grad,
            output_weight_grad,
            table_grad,
            router_grad,
            attn_gain_grad,
            ffn_gain_grad,
        ),
        ("dp", "expert"),
    )
    return (
        mixed,
        token_grad,
        summed[6],
        summed[7],
        summed[0],
        summed[1],
        summed[2],
        summed[3],
        summed[4],
        summed[5],
        in_weight_grad,
        out_weight_grad,
    )


def solution(mesh):
    return jax.shard_map(
        per_device,
        mesh=mesh,
        in_specs=(
            P(("dp", "expert"), None),
            P(("dp", "expert"), None),
            P(("dp", "expert"), None),
            P(("dp", "expert"), None),
            P(),
            P(),
            P(),
            P(),
            P(),
            P(),
            P(),
            P(),
            P("expert", None, None),
            P("expert", None, None),
        ),
        out_specs=(
            P(("dp", "expert"), None),
            P(("dp", "expert"), None),
            P(),
            P(),
            P(),
            P(),
            P(),
            P(),
            P(),
            P(),
            P("expert", None, "dp"),
            P("expert", "dp", None),
        ),
        check_vma=False,
    )
```

profile of v0, /device:TPU:1, one launch (start us, length us, event | category | flops | bytes accessed | tf_op | source)
XLA Modules:
  0.0 934.9 jit_solution(17707192600387234811)
XLA Ops:
  13.1 4.3 scatter_custom_fusion
  30.2 23.8 %fusion.3 = f32[512,1024,12]{1,2,0:T(8,128)} fusion(s32[512,1024]{1,0:T(8,128)S(1)} %fusion.78, f32[32,12]{0,1:T(8,128)S(1)} %copy-done.79), kind=kOutput, calls=%fused_computation.10 | convolution fusion | flops 2432696320 | bytes 27264512 | tf_op jit(solution)/shard_map/gps,gv->vps/dot_general | solution.py:108
  54.0 23.6 %fusion.1 = f32[512,1024,12]{1,2,0:T(8,128)} fusion(s32[512,1024]{1,0:T(8,128)S(1)} %fusion.79, f32[32,12]{0,1:T(8,128)S(1)} %copy-done.79), kind=kOutput, calls=%fused_computation.7 | convolution fusion | flops 2432696320 | bytes 27264512 | tf_op jit(solution)/shard_map/gps,gv->vps/dot_general | solution.py:108
  78.3 29.2 %fusion.192 = (f32[12,512]{1,0:T(8,128)S(1)}, f32[12,512,1024]{2,1,0:T(8,128)}) fusion(f32[512,1024,12]{1,2,0:T(8,128)} %fusion.3, bf16[1024,12,64]{0,2,1:T(8,128)(2,1)S(1)} %convert_element_type.306, bf16[1,12,1024,64]{2,3,1,0:T(8,128)(2,1)S(1)} %convert_bitcast_fusion, pred[512,1024]{1,0:T(8,128)(4,1)S(1)} %get-tuple-element.30), kind=kOutput, calls=%fused_computation.240 | convolution fusion | flops 830466048 | bytes 53239808 | tf_op jit(solution)/shard_map/hqc,hkc->hqk/dot_general | solution.py:47
  107.5 10.9 %fusion.10 = f32[12,512]{1,0:T(8,128)S(1)} fusion(f32[12,512,1024]{2,1,0:T(8,128)} %get-tuple-element.37, f32[12,512]{1,0:T(8,128)S(1)} %get-tuple-element.36), kind=kLoop, calls=%fused_computation.30 | loop fusion | flops 12576768 | bytes 25214976 | tf_op jit(solution)/shard_map/reduce_sum | solution.py:132
  118.5 10.4 %fusion.135 = bf16[12,512,64]{1,2,0:T(8,128)(2,1)S(1)} fusion(bf16[1024,12,64]{0,2,1:T(8,128)(2,1)S(1)} %convert_element_type.318, f32[12,512,1024]{2,1,0:T(8,128)} %get-tuple-element.37, f32[12,512]{1,0:T(8,128)S(1)} %fusion.10, f32[12,512]{1,0:T(8,128)S(1)} %get-tuple-element.36), kind=kOutput, calls=%fused_computation.174 | convolution fusion | flops 824573952 | bytes 27574272 | tf_op jit(solution)/shard_map/hqk,hkc->hqc/dot_general | solution.py:136
  128.9 29.1 %fusion.191 = (f32[12,512]{1,0:T(8,128)S(1)}, f32[12,512,1024]{2,1,0:T(8,128)}) fusion(f32[512,1024,12]{1,2,0:T(8,128)} %fusion.1, bf16[1024,12,64]{0,2,1:T(8,128)(2,1)S(1)} %convert_element_type.306, bf16[1,12,1024,64]{2,3,1,0:T(8,128)(2,1)S(1)} %convert_bitcast_fusion, pred[512,1024]{1,0:T(8,128)(4,1)S(1)} %get-tuple-element.31), kind=kOutput, calls=%fused_computation.239 | convolution fusion | flops 830466048 | bytes 53239808 | tf_op jit(solution)/shard_map/hqc,hkc->hqk/dot_general | solution.py:47
  158.0 10.9 %fusion.11 = f32[12,512]{1,0:T(8,128)S(1)} fusion(f32[12,512,1024]{2,1,0:T(8,128)} %get-tuple-element.35, f32[12,512]{1,0:T(8,128)S(1)} %get-tuple-element.34), kind=kLoop, calls=%fused_computation.31 | loop fusion | flops 12576768 | bytes 25214976 | tf_op jit(solution)/shard_map/reduce_sum | solution.py:132
  169.0 10.4 %fusion.132 = bf16[12,512,64]{1,2,0:T(8,128)(2,1)S(1)} fusion(bf16[1024,12,64]{0,2,1:T(8,128)(2,1)S(1)} %convert_element_type.318, f32[12,512,1024]{2,1,0:T(8,128)} %get-tuple-element.35, f32[12,512]{1,0:T(8,128)S(1)} %fusion.11, f32[12,512]{1,0:T(8,128)S(1)} %get-tuple-element.34), kind=kOutput, calls=%fused_computation.173 | convolution fusion | flops 824573952 | bytes 27574272 | tf_op jit(solution)/shard_map/hqk,hkc->hqc/dot_general | solution.py:136
  183.5 4.9 gather_fusion
  190.3 51.1 %all_to_all.21 = bf16[8,160,768]{2,1,0:T(8,128)(2,1)S(1)} all-to-all(bf16[8,160,768]{2,1,0:T(8,128)(2,1)S(1)} %bitcast.331), channel_id=1, replica_groups=mesh['dp'=4,'expert'=8] {'expert'}, dimensions={0} | all-to-all | bytes 3932160 | tf_op jit(solution)/shard_map/all_to_all | solution.py:168
  241.4 8.9 fusion.53
  250.3 5.4 copy-done.90
  255.7 40.1 %fusion.98 = bf16[8,160,768]{2,1,0:T(8,128)(2,1)} fusion(bf16[1,3072,768]{2,1,0:T(8,128)(2,1)S(1)} %bitcast.356, f32[8,160,3072]{2,1,0:T(8,128)S(1)} %fusion.53), kind=kOutput, calls=%fused_computation.146 | convolution fusion | flops 6296371200 | bytes 22413312 | tf_op jit(solution)/shard_map/secf,efd->secd/dot_general | solution.py:172
  295.8 4.5 all-to-all-start.1
  300.4 4.9 fusion.193
  305.9 38.4 %all-to-all-done.1 = bf16[8,160,768]{2,1,0:T(8,128)(2,1)S(1)} async-done(((bf16[8,160,768]{2,1,0:T(8,128)(2,1)}), bf16[8,160,768]{2,1,0:T(8,128)(2,1)S(1)}, u32[]{:S(2)}, u32[]{:S(2)}) %all-to-all-start.1) | async-done | bytes 1966112 | tf_op jit(solution)/shard_map/all_to_all | solution.py:176
  347.3 5.2 gather_fusion.1
  352.5 3.3 fusion.70
  356.0 4.9 gather_fusion.2
  362.7 49.6 %all_to_all.22 = bf16[8,160,768]{2,1,0:T(8,128)(2,1)S(1)} all-to-all(bf16[8,160,768]{2,1,0:T(8,128)(2,1)S(1)} %bitcast.330), channel_id=1, replica_groups=mesh['dp'=4,'expert'=8] {'expert'}, dimensions={0} | all-to-all | bytes 3932160 | tf_op jit(solution)/shard_map/all_to_all | solution.py:189
  412.3 40.1 %fusion.58 = bf16[1,3072,768]{2,1,0:T(8,128)(2,1)} fusion(bf16[8,160,768]{2,1,0:T(8,128)(2,1)S(1)} %all_to_all.22, f32[8,160,3072]{2,1,0:T(8,128)} %copy-done.90), kind=kOutput, calls=%fused_computation.92 | convolution fusion | flops 6297747456 | bytes 22413312 | tf_op jit(solution)/shard_map/secf,secd->efd/dot_general | solution.py:203
  452.5 42.8 %fusion.22 = bf16[8,1,160,3072]{3,2,0,1:T(8,128)(2,1)S(1)} fusion(f32[8,160,3072]{2,1,0:T(8,128)} %copy-done.90, bf16[8,160,768]{2,1,0:T(8,128)(2,1)S(1)} %all_to_all.22, bf16[1,3072,768]{2,1,0:T(8,128)(2,1)} %param.31), kind=kOutput, calls=%fused_computation.44 | convolution fusion | flops 6322913280 | bytes 30277632 | tf_op jit(solution)/shard_map/secd,efd->secf/dot_general | solution.py:198
  498.3 7.5 fusion.101
  505.8 4.4 all-to-all-start.3
  523.8 11.2 %fusion.55 = bf16[1,768,3072]{2,1,0:T(8,128)(2,1)} fusion(bf16[8,160,768]{2,1,0:T(8,128)(2,1)S(1)} %copy-done.32, bf16[8,1,160,3072]{3,2,0,1:T(8,128)(2,1)} %copy-done.91), kind=kOutput, calls=%fused_computation.91 | convolution fusion | flops 6042157056 | bytes 14548992 | tf_op jit(solution)/shard_map/secd,secf->edf/dot_general | solution.py:206
  535.0 19.3 %all-to-all-done.3 = bf16[8,160,768]{2,1,0:T(8,128)(2,1)S(1)} async-done(((bf16[8,160,768]{2,1,0:T(8,128)(2,1)}), bf16[8,160,768]{2,1,0:T(8,128)(2,1)S(1)}, u32[]{:S(2)}, u32[]{:S(2)}) %all-to-all-start.3) | async-done | bytes 1966112 | tf_op jit(solution)/shard_map/all_to_all | solution.py:215
  557.6 5.2 gather_fusion.3
  562.9 6.4 multiply_reduce_fusion.2
  576.3 15.9 %multiply_reduce_fusion = (f32[12,512]{1,0:T(8,128)S(1)}, f32[12,512,1024]{2,1,0:T(8,128)}) fusion(f32[12,512,1024]{2,1,0:T(8,128)} %get-tuple-element.35, f32[12,512]{1,0:T(8,128)S(1)} %log_add_fusion, bf16[1024,12,64]{0,2,1:T(8,128)(2,1)S(1)} %copy-done.7, bf16[1,12,1024,64]{2,3,1,0:T(8,128)(2,1)} %fusion.125), kind=kOutput, calls=%fused_computation.20 | convolution fusion | flops 824174592 | bytes 52740096 | tf_op jit(solution)/shard_map/hqc,hkc->hqk/dot_general | solution.py:263
  592.2 15.8 %multiply_reduce_fusion.1 = (f32[12,512]{1,0:T(8,128)S(1)}, f32[12,512,1024]{2,1,0:T(8,128)}) fusion(f32[12,512,1024]{2,1,0:T(8,128)} %get-tuple-element.37, f32[12,512]{1,0:T(8,128)S(1)} %log_add_fusion.1, bf16[1024,12,64]{0,2,1:T(8,128)(2,1)S(1)} %copy-done.7, bf16[1,12,1024,64]{2,3,1,0:T(8,128)(2,1)} %fusion.125), kind=kOutput, calls=%fused_computation.23 | convolution fusion | flops 824174592 | bytes 52740096 | tf_op jit(solution)/shard_map/hqc,hkc->hqk/dot_general | solution.py:263
  608.1 22.6 %multiply_convert_fusion = bf16[12,512,1024]{2,1,0:T(8,128)(2,1)} fusion(f32[12,512,1024]{2,1,0:T(8,128)} %get-tuple-element.46, f32[12,512,1024]{2,1,0:T(8,128)} %get-tuple-element.35, f32[12,512]{1,0:T(8,128)S(1)} %get-tuple-element.45, f32[12,512]{1,0:T(8,128)S(1)} %log_add_fusion), kind=kLoop, calls=%fused_computation.19 | loop fusion | flops 25165824 | bytes 62963712 | tf_op jit(solution)/shard_map/convert_element_type | solution.py:267
  635.2 15.3 %multiply_convert_fusion.1 = bf16[12,512,1024]{2,1,0:T(8,128)(2,1)} fusion(f32[12,512,1024]{2,1,0:T(8,128)} %get-tuple-element.44, f32[12,512,1024]{2,1,0:T(8,128)S(1)} %bitcast.323, f32[12,512]{1,0:T(8,128)S(1)} %get-tuple-element.43, f32[12,512]{1,0:T(8,128)S(1)} %log_add_fusion.1), kind=kLoop, calls=%fused_computation.22 | loop fusion | flops 25165824 | bytes 62963712 | tf_op jit(solution)/shard_map/convert_element_type | solution.py:267
  650.5 8.5 multiply_convert_fusion.3
  659.0 9.4 %multiply_convert_fusion.4 = bf16[12,512,64]{1,2,0:T(8,128)(2,1)} fusion(bf16[12,512,1024]{2,1,0:T(8,128)(2,1)} %multiply_convert_fusion.1, bf16[1024,12,64]{0,2,1:T(8,128)(2,1)S(1)} %copy-done.10), kind=kOutput, calls=%fused_computation.165 | convolution fusion | flops 806092800 | bytes 14942208 | tf_op jit(solution)/shard_map/hqk,hkc->hqc/dot_general | solution.py:270
  671.0 10.3 %fusion.34 = f32[12,1024,64]{1,2,0:T(8,128)S(1)} fusion(f32[12,512,1024]{2,1,0:T(8,128)} %get-tuple-element.35, f32[12,512]{1,0:T(8,128)S(1)} %copy-done.49, bf16[1,12,1024,64]{2,3,1,0:T(8,128)(2,1)S(1)} %copy-done.25), kind=kOutput, calls=%fused_computation.62 | convolution fusion | flops 817889280 | bytes 29130752 | tf_op jit(solution)/shard_map/hqk,hqc->hkc/dot_general | solution.py:286
  681.4 12.5 %add_convert_fusion = bf16[12,1024,64]{1,2,0:T(8,128)(2,1)} fusion(f32[12,1024,64]{1,2,0:T(8,128)S(1)} %fusion.34, f32[12,512,1024]{2,1,0:T(8,128)} %get-tuple-element.37, f32[12,512]{1,0:T(8,128)S(1)} %copy-done.47, bf16[1,12,1024,64]{2,3,1,0:T(8,128)(2,1)} %fusion.125), kind=kOutput, calls=%fused_computation.113 | convolution fusion | flops 819462144 | bytes 30695424 | tf_op jit(solution)/shard_map/hqk,hqc->hkc/dot_general | solution.py:286
  693.9 5.1 fusion.178
  699.0 3.1 fusion.182
  705.6 3.6 multiply_convert_fusion.2
  709.3 3.1 fusion.180
  720.6 3.9 fusion.74
  726.1 22.9 %fusion.138 = f32[32,12]{0,1:T(8,128)S(1)} fusion(bf16[12,512,1024]{2,1,0:T(8,128)(2,1)} %multiply_convert_fusion.1, s32[512,1024]{1,0:T(8,128)S(1)} %copy-done.14), kind=kOutput, calls=%fused_computation.175 | convolution fusion | flops 419430400 | bytes 14681600 | tf_op jit(solution)/shard_map/avx,ovx->ao/dot_general | solution.py:292
  749.0 23.7 %fusion.144 = f32[32,12]{0,1:T(8,128)S(1)} fusion(f32[32,12]{0,1:T(8,128)S(1)} %fusion.138, bf16[12,512,1024]{2,1,0:T(8,128)(2,1)} %multiply_convert_fusion, s32[512,1024]{1,0:T(8,128)S(1)} %copy-done.16), kind=kOutput, calls=%fused_computation.177 | convolution fusion | flops 419430784 | bytes 14683136 | tf_op jit(solution)/shard_map/avx,ovx->ao/dot_general | solution.py:292
  772.7 40.9 %all-reduce.4 = (f32[768]{0:T(1024)}, f32[768]{0:T(1024)}, f32[32,12]{0,1:T(8,128)}, f32[768,8]{0,1:T(8,128)}) all-reduce(f32[768]{0:T(1024)S(1)} %get-tuple-element.16, f32[768]{0:T(1024)S(1)} %copy-done.83, f32[32,12]{0,1:T(8,128)S(1)} %fusion.144, f32[768,8]{0,1:T(8,128)S(1)} %copy-done.68), channel_id=1, replica_groups=mesh['dp'=4,'expert'=8] {'dp','expert'}, use_global_device_ids=true, to_apply=%region_19.22 | all-reduce | flops 8064 | bytes 64512 | tf_op jit(solution)/shard_map/psum | solution.py:331
  813.6 5.0 fusion.66
  824.3 92.8 %all-reduce.8.cloned.1.call-done = (f32[768,768]{1,0:T(8,128)}, f32[768,768]{1,0:T(8,128)}, f32[768,768]{1,0:T(8,128)}, f32[768,768]{1,0:T(8,128)}) async-done(((f32[768,768]{1,0:T(8,128)}, f32[768,768]{1,0:T(8,128)}, f32[768,768]{1,0:T(8,128)}, f32[768,768]{1,0:T(8,128)}), (f32[768,768]{1,0:T(8,128)}, f32[768,768]{1,0:T(8,128)}, f32[768,768]{1,0:T(8,128)}, ...) | async-done | bytes 9437200 | tf_op jit(solution)/shard_map/psum | solution.py:331
  917.1 3.4 copy.61
  (282 shorter events, 89.1 us)
Async XLA Ops:
  8.0 171.4 %copy-start = (bf16[768,768]{1,0:T(8,128)(2,1)S(1)}, bf16[768,768]{1,0:T(8,128)(2,1)}, u32[]{:S(2)}) copy-start(bf16[768,768]{1,0:T(8,128)(2,1)} %param.27) | copy-start | bytes 3538948
  8.0 10.6 %copy-start.19 = (bf16[1024,768]{1,0:T(8,128)(2,1)S(1)}, bf16[1024,768]{1,0:T(8,128)(2,1)}, u32[]{:S(2)}) copy-start(bf16[1024,768]{1,0:T(8,128)(2,1)} %param.18) | copy-start | bytes 4718596
  8.0 11.0 %copy-start.84 = (s32[1,1024]{1,0:T(1,128)S(1)}, s32[1,1024]{1,0:T(1,128)}, u32[]{:S(2)}) copy-start(s32[1,1024]{1,0:T(1,128)} %param.19) | copy-start | bytes 12292
  8.0 14.0 %copy-start.87 = (f32[768]{0:T(1024)S(1)}, f32[768]{0:T(1024)}, u32[]{:S(2)}) copy-start(f32[768]{0:T(1024)} %param.22) | copy-start | bytes 9220
  18.6 11.1 %copy-start.13 = (s32[512,1024]{1,0:T(8,128)}, s32[512,1024]{1,0:T(8,128)S(1)}, u32[]{:S(2)}) copy-start(s32[512,1024]{1,0:T(8,128)S(1)} %fusion.78) | copy-start | bytes 6291460
  22.1 31.9 %copy-start.15 = (s32[512,1024]{1,0:T(8,128)}, s32[512,1024]{1,0:T(8,128)S(1)}, u32[]{:S(2)}) copy-start(s32[512,1024]{1,0:T(8,128)S(1)} %fusion.79) | copy-start | bytes 6291460
  25.0 103.9 %copy-start.9 = (bf16[1024,12,64]{0,2,1:T(8,128)(2,1)}, bf16[1024,12,64]{0,2,1:T(8,128)(2,1)S(1)}, u32[]{:S(2)}) copy-start(bf16[1024,12,64]{0,2,1:T(8,128)(2,1)S(1)} %convert_element_type.306) | copy-start | bytes 4718596
  27.9 141.0 %copy-start.6 = (bf16[1024,12,64]{0,2,1:T(8,128)(2,1)}, bf16[1024,12,64]{0,2,1:T(8,128)(2,1)S(1)}, u32[]{:S(2)}) copy-start(bf16[1024,12,64]{0,2,1:T(8,128)(2,1)S(1)} %convert_element_type.318) | copy-start | bytes 4718596
  30.2 98.7 %copy-start.4 = (bf16[1,12,1024,64]{2,3,1,0:T(8,128)(2,1)}, bf16[1,12,1024,64]{2,3,1,0:T(8,128)(2,1)S(1)}, u32[]{:S(2)}) copy-start(bf16[1,12,1024,64]{2,3,1,0:T(8,128)(2,1)S(1)} %convert_bitcast_fusion) | copy-start | bytes 4718596
  107.5 10.9 %copy-start.50 = (f32[12,512]{1,0:T(8,128)}, f32[12,512]{1,0:T(8,128)S(1)}, u32[]{:S(2)}) copy-start(f32[12,512]{1,0:T(8,128)S(1)} %get-tuple-element.36) | copy-start | bytes 73732
  118.5 10.4 %copy-start.58 = (f32[12,512]{1,0:T(8,128)}, f32[12,512]{1,0:T(8,128)S(1)}, u32[]{:S(2)}) copy-start(f32[12,512]{1,0:T(8,128)S(1)} %fusion.10) | copy-start | bytes 73732
  128.9 50.5 %copy-start.44 = (bf16[12,512,64]{1,2,0:T(8,128)(2,1)}, bf16[12,512,64]{1,2,0:T(8,128)(2,1)S(1)}, u32[]{:S(2)}) copy-start(bf16[12,512,64]{1,2,0:T(8,128)(2,1)S(1)} %fusion.135) | copy-start | bytes 2359300
  158.0 10.9 %copy-start.52 = (f32[12,512]{1,0:T(8,128)}, f32[12,512]{1,0:T(8,128)S(1)}, u32[]{:S(2)}) copy-start(f32[12,512]{1,0:T(8,128)S(1)} %get-tuple-element.34) | copy-start | bytes 73732
  168.9 10.4 %copy-start.60 = (f32[12,512]{1,0:T(8,128)}, f32[12,512]{1,0:T(8,128)S(1)}, u32[]{:S(2)}) copy-start(f32[12,512]{1,0:T(8,128)S(1)} %fusion.11) | copy-start | bytes 73732
  181.1 119.2 %copy-start.56 = (f32[1024]{0:T(1024)}, f32[1024]{0:T(1024)S(1)}, u32[]{:S(2)}) copy-start(f32[1024]{0:T(1024)S(1)} %add_rsqrt_fusion) | copy-start | bytes 12292
  188.3 67.4 %slice-start.12 = ((s8[4718592]{0:T(1024)(128)(4,1)}), s8[4194304]{0:T(1024)(128)(4,1)S(1)}, s32[]{:S(2)}) async-start(s8[4718592]{0:T(1024)(128)(4,1)} %bitcast.355), calls=%async_computation.21 | async-start | bytes 8388608
  241.4 14.3 %slice-start.13 = ((s8[4718592]{0:T(1024)(128)(4,1)}), s8[524288]{0:T(1024)(128)(4,1)S(1)}, s32[]{:S(2)}) async-start(s8[4718592]{0:T(1024)(128)(4,1)} %bitcast.355), calls=%async_computation.22 | async-start | bytes 1048576
  295.8 9.5 %copy-start.54 = (s32[1024,1]{0,1:T(1,128)S(1)}, s32[1024,1]{0,1:T(1,128)}, u32[]{:S(2)}) copy-start(s32[1024,1]{0,1:T(1,128)} %param.20) | copy-start | bytes 12292
  295.8 9.6 %copy-start.73 = (s32[1024]{0:T(1024)S(1)}, s32[1024]{0:T(1024)}, u32[]{:S(2)}) copy-start(s32[1024]{0:T(1024)} %copy-done.72) | copy-start | bytes 12292
  295.8 48.5 %all-to-all-start.1 = ((bf16[8,160,768]{2,1,0:T(8,128)(2,1)}), bf16[8,160,768]{2,1,0:T(8,128)(2,1)S(1)}, u32[]{:S(2)}, u32[]{:S(2)}) async-start(bf16[8,160,768]{2,1,0:T(8,128)(2,1)} %fusion.98), calls=%async_computation.1 | async-start | bytes 3932160 | tf_op jit(solution)/shard_map/all_to_all | solution.py:176
  300.3 518.3 %reduce-scatter.5.cloned.1.call-start = ((), (), s32[]{:S(2)}) async-start(), calls=%async_computation.7 | async-start | bytes 5898240 | tf_op jit(solution)/shard_map/reduce_scatter | solution.py:220
  305.3 39.0 %copy-start.70 = (f32[1024]{0:T(1024)}, f32[1024]{0:T(1024)S(1)}, u32[]{:S(2)}) copy-start(f32[1024]{0:T(1024)S(1)} %fusion.160) | copy-start | bytes 12292
  305.4 47.1 %copy-start.75 = (f32[1024]{0:T(1024)}, f32[1024]{0:T(1024)S(1)}, u32[]{:S(2)}) copy-start(f32[1024]{0:T(1024)S(1)} %fusion.155) | copy-start | bytes 12292
  305.9 46.6 %copy-start.85 = (pred[1024]{0:T(1024)(128)(4,1)}, pred[1024]{0:T(1024)(128)(4,1)S(1)}, u32[]{:S(2)}) copy-start(pred[1024]{0:T(1024)(128)(4,1)S(1)} %compare_and_fusion.1) | copy-start | bytes 3076
  305.9 49.9 %copy-start.77 = (s32[1024]{0:T(1024)}, s32[1024]{0:T(1024)S(1)}, u32[]{:S(2)}) copy-start(s32[1024]{0:T(1024)S(1)} %broadcast_clamp_fusion) | copy-start | bytes 12292
  452.4 45.9 %copy-start.89 = (bf16[1,768,3072]{2,1,0:T(8,128)(2,1)S(1)}, bf16[1,768,3072]{2,1,0:T(8,128)(2,1)}, u32[]{:S(2)}) copy-start(bf16[1,768,3072]{2,1,0:T(8,128)(2,1)} %param.30) | copy-start | bytes 14155780
  505.8 48.5 %all-to-all-start.3 = ((bf16[8,160,768]{2,1,0:T(8,128)(2,1)}), bf16[8,160,768]{2,1,0:T(8,128)(2,1)S(1)}, u32[]{:S(2)}, u32[]{:S(2)}) async-start(bf16[8,160,768]{2,1,0:T(8,128)(2,1)} %fusion.101), calls=%async_computation.3 | async-start | bytes 3932160 | tf_op jit(solution)/shard_map/all_to_all | solution.py:215
  510.2 311.3 %reduce-scatter.3.cloned.1.call-start = ((), (), s32[]{:S(2)}) async-start(), calls=%async_computation.6 | async-start | bytes 5898240 | tf_op jit(solution)/shard_map/reduce_scatter | solution.py:217
  521.0 109.7 %copy-start.46 = (f32[12,512]{1,0:T(8,128)}, f32[12,512]{1,0:T(8,128)S(1)}, u32[]{:S(2)}) copy-start(f32[12,512]{1,0:T(8,128)S(1)} %log_add_fusion.1) | copy-start | bytes 73732
  521.0 87.0 %copy-start.48 = (f32[12,512]{1,0:T(8,128)}, f32[12,512]{1,0:T(8,128)S(1)}, u32[]{:S(2)}) copy-start(f32[12,512]{1,0:T(8,128)S(1)} %log_add_fusion) | copy-start | bytes 73732
  534.9 22.7 %copy-start.78 = (s32[1024]{0:T(1024)S(1)}, s32[1024]{0:T(1024)}, u32[]{:S(2)}) copy-start(s32[1024]{0:T(1024)} %copy-done.77) | copy-start | bytes 12292
  535.0 382.1 %all-reduce.8.cloned.1.call-start = ((), (), s32[]{:S(2)}) async-start(), calls=%async_computation.8 | async-start | bytes 18874368 | tf_op jit(solution)/shard_map/psum | solution.py:331
  608.0 22.6 %slice-start = ((s8[25165824]{0:T(1024)(128)(4,1)}), s8[4194304]{0:T(1024)(128)(4,1)S(1)}, s32[]{:S(2)}) async-start(s8[25165824]{0:T(1024)(128)(4,1)} %bitcast.322), calls=%async_computation.9 | async-start | bytes 8388608
  608.0 22.6 %slice-start.1 = ((s8[25165824]{0:T(1024)(128)(4,1)}), s8[4194304]{0:T(1024)(128)(4,1)S(1)}, s32[]{:S(2)}) async-start(s8[25165824]{0:T(1024)(128)(4,1)} %bitcast.322), calls=%async_computation.10 | async-start | bytes 8388608
  608.0 23.6 %slice-start.2 = ((s8[25165824]{0:T(1024)(128)(4,1)}), s8[4194304]{0:T(1024)(128)(4,1)S(1)}, s32[]{:S(2)}) async-start(s8[25165824]{0:T(1024)(128)(4,1)} %bitcast.322), calls=%async_computation.11 | async-start | bytes 8388608
  608.1 24.8 %slice-start.3 = ((s8[25165824]{0:T(1024)(128)(4,1)}), s8[4194304]{0:T(1024)(128)(4,1)S(1)}, s32[]{:S(2)}) async-start(s8[25165824]{0:T(1024)(128)(4,1)} %bitcast.322), calls=%async_computation.12 | async-start | bytes 8388608
  608.1 26.0 %slice-start.4 = ((s8[25165824]{0:T(1024)(128)(4,1)}), s8[4194304]{0:T(1024)(128)(4,1)S(1)}, s32[]{:S(2)}) async-start(s8[25165824]{0:T(1024)(128)(4,1)} %bitcast.322), calls=%async_computation.13 | async-start | bytes 8388608
  608.1 27.1 %slice-start.5 = ((s8[25165824]{0:T(1024)(128)(4,1)}), s8[4194304]{0:T(1024)(128)(4,1)S(1)}, s32[]{:S(2)}) async-start(s8[25165824]{0:T(1024)(128)(4,1)} %bitcast.322), calls=%async_computation.14 | async-start | bytes 8388608
  635.2 15.3 %copy-start.10 = (bf16[1024,12,64]{0,2,1:T(8,128)(2,1)S(1)}, bf16[1024,12,64]{0,2,1:T(8,128)(2,1)}, u32[]{:S(2)}) copy-start(bf16[1024,12,64]{0,2,1:T(8,128)(2,1)} %copy-done.9) | copy-start | bytes 4718596
  671.0 10.3 %copy-start.47 = (f32[12,512]{1,0:T(8,128)S(1)}, f32[12,512]{1,0:T(8,128)}, u32[]{:S(2)}) copy-start(f32[12,512]{1,0:T(8,128)} %copy-done.46) | copy-start | bytes 73732
  681.3 12.6 %copy-start.82 = (f32[1024]{0:T(1024)S(1)}, f32[1024]{0:T(1024)}, u32[]{:S(2)}) copy-start(f32[1024]{0:T(1024)} %copy-done.81) | copy-start | bytes 12292
  681.3 12.6 %copy-start.88 = (f32[768]{0:T(1024)S(1)}, f32[768]{0:T(1024)}, u32[]{:S(2)}) copy-start(f32[768]{0:T(1024)} %param.22) | copy-start | bytes 9220
  681.3 20.8 %slice-start.9 = ((s8[12582912]{0:T(1024)(128)(4,1)}), s8[4194304]{0:T(1024)(128)(4,1)S(1)}, s32[]{:S(2)}) async-start(s8[12582912]{0:T(1024)(128)(4,1)} %bitcast.326), calls=%async_computation.18 | async-start | bytes 8388608
  681.4 20.8 %slice-start.10 = ((s8[12582912]{0:T(1024)(128)(4,1)}), s8[4194304]{0:T(1024)(128)(4,1)S(1)}, s32[]{:S(2)}) async-start(s8[12582912]{0:T(1024)(128)(4,1)} %bitcast.326), calls=%async_computation.19 | async-start | bytes 8388608
  726.1 22.9 %copy-start.16 = (s32[512,1024]{1,0:T(8,128)S(1)}, s32[512,1024]{1,0:T(8,128)}, u32[]{:S(2)}) copy-start(s32[512,1024]{1,0:T(8,128)} %copy-done.15) | copy-start | bytes 6291460
  749.0 23.7 %copy-start.68 = (f32[768,8]{0,1:T(8,128)S(1)}, f32[768,8]{0,1:T(8,128)}, u32[]{:S(2)}) copy-start(f32[768,8]{0,1:T(8,128)} %fusion.75) | copy-start | bytes 73732
  749.0 23.7 %copy-start.83 = (f32[768]{0:T(1024)S(1)}, f32[768]{0:T(1024)}, u32[]{:S(2)}) copy-start(f32[768]{0:T(1024)} %get-tuple-element.14) | copy-start | bytes 9220
  749.0 64.6 %copy-start.23 = (bf16[1024,768]{1,0:T(8,128)(2,1)S(1)}, bf16[1024,768]{1,0:T(8,128)(2,1)}, u32[]{:S(2)}) copy-start(bf16[1024,768]{1,0:T(8,128)(2,1)} %param.18) | copy-start | bytes 4718596
  (63 other events, 238.8 us)
Sparse Core Ops, SparseCore 0:
  452.6 48.0 reduce-scatter.4
  535.1 49.9 reduce-scatter.2
Sparse Core Ops, SparseCore 1:
  724.7 192.4 all-reduce.7
where the time goes:
time: 944 us; the launch traced here: 935 us
  matrix products  448 us (47%)
  waiting for transfers between devices  151 us (16%)
  blocking collectives  142 us (15%)
  other arithmetic  96.7 us (10%)
  local copies, waits for them, and re-layouts  71.8 us (8%)
  between operations  17.3 us (2%)
    psum x1, waiting for transfers between devices, per_device(): lax.psum((query_weight_grad, key_weight_grad, value_weight_grad, output_w...  92.8 us
    dot_general x2, matrix products, block_scores(): jnp.einsum('hqc,hkc->hqk', query_block, key_seq, preferred_element_type=j...  58.3 us
    all_to_all x1, blocking collectives, per_device(): lax.all_to_all(slots_out, 'expert', split_axis=0, concat_axis=0, tiled=True)  51.1 us
    all_to_all x1, blocking collectives, per_device(): lax.all_to_all(grad_slots, 'expert', split_axis=0, concat_axis=0, tiled=T...  49.6 us
    dot_general x2, matrix products, per_device(): jnp.einsum('gps,gv->vps', onehot_bucket.astype(jnp.float32), position_bia...  47.4 us
    dot_general x2, matrix products, per_device(): jnp.einsum('avx,ovx->ao', onehot_bucket_grids[block_ordinal], scores_grad...  46.5 us
    unnamed x219, local copies, waits for them, and re-layouts  43.1 us
    dot_general x1, matrix products, per_device(): jnp.einsum('secd,efd->secf', grad_arrived, expert_out, preferred_element_...  42.8 us
  transfers between devices with their start and end apart: 5, of which 3 were waited for; matrix products, arithmetic and copies ran while one was open for 32% of the time, Pallas kernels for 0%

commit v1 on v0

v1 whole, which is shorter than its diff:
```python
import functools

import jax
import jax.numpy as jnp
from jax import lax
from jax.experimental import pallas as pl
from jax.experimental.pallas import tpu as pltpu
from jax.sharding import PartitionSpec as P

epsilon = 1e-06
precise_setting = lax.Precision.HIGHEST
bucket_bounds = (12, 16, 23, 32, 46, 64, 91)
masked_score = -1e30
LANES = 128
BLOCK = 128
NEAR = 5


def bucket_of(relative):
    distance = jnp.abs(relative)
    beyond = jnp.zeros_like(distance)
    for threshold in bucket_bounds:
        beyond = beyond + (distance >= threshold).astype(jnp.int32)
    inside = jnp.where(distance < 8, distance, 8 + beyond)
    return inside + 16 * (relative > 0).astype(jnp.int32)


def dot_nt(a, b):
    return lax.dot_general(a, b, (((1,), (1,)), ((), ())), preferred_element_type=jnp.float32)


def dot_nn(a, b):
    return lax.dot_general(a, b, (((1,), (0,)), ((), ())), preferred_element_type=jnp.float32)


def split3(x):
    a = x.astype(jnp.bfloat16)
    r = x - a.astype(jnp.float32)
    b = r.astype(jnp.bfloat16)
    c = (r - b.astype(jnp.float32)).astype(jnp.bfloat16)
    return a, b, c


def attn_fwd_kernel(lo_ref, hi_ref, q_ref, k_ref, v_ref, qm_ref, km_ref, diag_ref, o_ref, qx_ref,
                    kext, vext, bias, sc, mx, acc, *, heads):
    pairs = heads // 2
    length = q_ref.shape[0]
    nblk = length // BLOCK
    lane = lax.broadcasted_iota(jnp.int32, (1, LANES), 1)
    low = lane < 64
    for h in range(heads):
        for d in range(NEAR):
            if d in (0, 4):
                col = diag_ref[h : h + 1, 0:1] if d == 0 else diag_ref[h : h + 1, 511:512]
                bias[h, d] = jnp.broadcast_to(col, (BLOCK, BLOCK))
            else:
                v = jnp.broadcast_to(diag_ref[h : h + 1, (d - 1) * 128 : (d - 1) * 128 + 256], (BLOCK, 256))
                bias[h, d] = pltpu.roll(v, 128, 1, stride=1, stride_axis=0)[:, :BLOCK]
    zero = jnp.zeros((BLOCK, LANES), jnp.bfloat16)

    def build(j, _):
        rows = pl.ds(pl.multiple_of(j * BLOCK, BLOCK), BLOCK)
        km = km_ref[rows, :]
        km0 = jnp.where(low, km, 0).astype(jnp.bfloat16)
        km1 = jnp.where((lane < 8) | (lane >= 64), km, 0).astype(jnp.bfloat16)
        one0 = jnp.broadcast_to(low.astype(jnp.bfloat16), (BLOCK, LANES))
        one1 = jnp.broadcast_to((~low).astype(jnp.bfloat16), (BLOCK, LANES))
        for p in range(pairs):
            cols = pl.ds(p * LANES, LANES)
            kk = k_ref[rows, cols]
            vv = v_ref[rows, cols]
            kext[p, j] = jnp.concatenate([
                jnp.concatenate([jnp.where(low, kk, zero), km0], 1),
                jnp.concatenate([jnp.where(low, zero, kk), km1], 1)], 0)
            vext[p, j] = jnp.concatenate([
                jnp.concatenate([jnp.where(low, vv, zero), one0], 1),
                jnp.concatenate([jnp.where(low, zero, vv), one1], 1)], 0)
        return 0
    lax.fori_loop(0, nblk, build, 0)

    def q_block(i, _):
        lo = lo_ref[i]
        hi = hi_ref[i]
        rows = pl.ds(pl.multiple_of(i * BLOCK, BLOCK), BLOCK)
        qm = qm_ref[rows, :]
        mx[...] = jnp.full(mx.shape, -3e38, jnp.float32)

        def pass1(j, _):
            d = jnp.clip(j - i, -2, 2) + 2
            for p in range(pairs):
                qe = jnp.concatenate([q_ref[rows, pl.ds(p * LANES, LANES)], qm], 1)
                s = dot_nt(qe, kext[p, j])
                s0 = s[:, :BLOCK] + bias[2 * p, d]
                s1 = s[:, BLOCK:] + bias[2 * p + 1, d]
                sc[p, j, :, :BLOCK] = s0
                sc[p, j, :, BLOCK:] = s1
                mx[2 * p] = jnp.maximum(mx[2 * p], s0)
                mx[2 * p + 1] = jnp.maximum(mx[2 * p + 1], s1)
            return 0
        lax.fori_loop(lo, hi, pass1, 0)
        for h in range(heads):
            mx[h] = jnp.broadcast_to(jnp.max(mx[h], 1, keepdims=True), (BLOCK, LANES))
        acc[...] = jnp.zeros_like(acc)

        def pass2(j, _):
            for p in range(pairs):
                p0 = jnp.exp(sc[p, j, :, :BLOCK] - mx[2 * p]).astype(jnp.bfloat16)
                p1 = jnp.exp(sc[p, j, :, BLOCK:] - mx[2 * p + 1]).astype(jnp.bfloat16)
                acc[p] += dot_nn(jnp.concatenate([p0, p1], 1), vext[p, j])
            return 0
        lax.fori_loop(lo, hi, pass2, 0)
        m64 = lane % 64
        for p in range(pairs):
            cols = pl.ds(p * LANES, LANES)
            total = acc[p, :, LANES:]
            o_ref[rows, cols] = (acc[p, :, :LANES] / total).astype(jnp.bfloat16)
            lse = jnp.where(low, mx[2 * p], mx[2 * p + 1]) + jnp.log(total)
            a, b, c = split3(lse)
            ext = jnp.where(m64 == 8, -a, jnp.where(m64 == 9, -b, jnp.where(m64 == 10, -c, qm)))
            qx_ref[rows, cols] = ext.astype(jnp.bfloat16)
        return 0
    lax.fori_loop(0, nblk, q_block, 0)


def attn_fwd(lo, hi, q, k, v, qm, km, diag):
    length, width = q.shape
    heads = diag.shape[0]
    pairs = heads // 2
    nblk = length // BLOCK
    smem = pl.BlockSpec(memory_space=pltpu.SMEM)
    vmem = pl.BlockSpec(memory_space=pltpu.VMEM)
    f32, bf16 = jnp.float32, jnp.bfloat16
    return pl.pallas_call(
        functools.partial(attn_fwd_kernel, heads=heads),
        out_shape=(jax.ShapeDtypeStruct((length, width), bf16), jax.ShapeDtypeStruct((length, width), bf16)),
        in_specs=[smem, smem] + [vmem] * 6,
        out_specs=(vmem, vmem),
        scratch_shapes=[
            pltpu.VMEM((pairs, nblk, 2 * BLOCK, 2 * LANES), bf16),
            pltpu.VMEM((pairs, nblk, 2 * BLOCK, 2 * LANES), bf16),
            pltpu.VMEM((heads, NEAR, BLOCK, BLOCK), f32),
            pltpu.VMEM((pairs, nblk, BLOCK, 2 * BLOCK), f32),
            pltpu.VMEM((heads, BLOCK, LANES), f32),
            pltpu.VMEM((pairs, BLOCK, 2 * LANES), f32),
        ],
        compiler_params=pltpu.CompilerParams(vmem_limit_bytes=60 << 20),
        cost_estimate=pl.CostEstimate(flops=4 * length * length * width, bytes_accessed=10 * length * width, transcendentals=length * length * heads),
    )(lo, hi, q, k, v, qm, km, diag)


def attn_bwd_kernel(lo_ref, hi_ref, q_ref, k_ref, v_ref, qx_ref, do_ref, o_ref, km_ref, diag_ref,
                    dq_ref, dk_ref, dv_ref, gsum_ref,
                    qst, dost, bias, gacc, dkacc, dvacc, dqacc, *, heads, scale):
    pairs = heads // 2
    length = q_ref.shape[0]
    nblk = length // BLOCK
    lane = lax.broadcasted_iota(jnp.int32, (1, LANES), 1)
    low = lane < 64
    m64 = lane % 64
    f32, bf16 = jnp.float32, jnp.bfloat16
    for h in range(heads):
        for d in range(NEAR):
            if d in (0, 4):
                col = diag_ref[h : h + 1, 0:1] if d == 0 else diag_ref[h : h + 1, 511:512]
                bias[h, d] = jnp.broadcast_to(col, (BLOCK, BLOCK))
            else:
                base = (3 - d) * BLOCK
                v = jnp.broadcast_to(diag_ref[heads + h : heads + h + 1, base : base + 256], (BLOCK, 256))
                bias[h, d] = pltpu.roll(v, 128, 1, stride=1, stride_axis=0)[:, :BLOCK]
    zero = jnp.zeros((BLOCK, LANES), bf16)
    gacc[...] = jnp.zeros_like(gacc)
    dkacc[...] = jnp.zeros_like(dkacc)
    dvacc[...] = jnp.zeros_like(dvacc)

    def q_block(i, _):
        lo = lo_ref[i]
        hi = hi_ref[i]
        rows = pl.ds(pl.multiple_of(i * BLOCK, BLOCK), BLOCK)
        for p in range(pairs):
            cols = pl.ds(p * LANES, LANES)
            qq = q_ref[rows, cols]
            qx = qx_ref[rows, cols]
            qst[p] = jnp.concatenate([
                jnp.concatenate([jnp.where(low, qq, zero), jnp.where(low, qx, zero)], 1),
                jnp.concatenate([jnp.where(low, zero, qq), jnp.where((lane < 8) | ~low, qx, zero)], 1)], 0)
            dd = do_ref[rows, cols]
            prod = dd.astype(f32) * o_ref[rows, cols].astype(f32)
            in0 = jnp.sum(jnp.where(low, prod, 0.0), 1, keepdims=True)
            in1 = jnp.sum(jnp.where(low, 0.0, prod), 1, keepdims=True)
            inner = jnp.where(low, in0, in1)
            a, b, c = split3(inner)
            ext = jnp.where(m64 == 8, -a, jnp.where(m64 == 9, -b, jnp.where(m64 == 10, -c, zero)))
            dost[p] = jnp.concatenate([
                jnp.concatenate([jnp.where(low, dd, zero), jnp.where(low, ext, zero)], 1),
                jnp.concatenate([jnp.where(low, zero, dd), jnp.where(low, zero, ext)], 1)], 0)
        dqacc[...] = jnp.zeros_like(dqacc)

        def k_block(j, _):
            d = jnp.clip(j - i, -2, 2) + 2
            krows = pl.ds(pl.multiple_of(j * BLOCK, BLOCK), BLOCK)
            km = km_ref[krows, :]
            for p in range(pairs):
                cols = pl.ds(p * LANES, LANES)
                kk = k_ref[krows, cols]
                vv = v_ref[krows, cols]
                qs = qst[p]
                ds_ = dost[p]
                st = dot_nt(jnp.concatenate([kk, km], 1), qs)
                dpt = dot_nt(jnp.concatenate([vv, km], 1), ds_)
                p0 = jnp.exp(st[:, :BLOCK] + bias[2 * p, d])
                p1 = jnp.exp(st[:, BLOCK:] + bias[2 * p + 1, d])
                d0 = p0 * dpt[:, :BLOCK]
                d1 = p1 * dpt[:, BLOCK:]
                gacc[2 * p, d] += d0
                gacc[2 * p + 1, d] += d1
                pb = jnp.concatenate([p0.astype(bf16), p1.astype(bf16)], 1)
                d0b = d0.astype(bf16)
                d1b = d1.astype(bf16)
                db = jnp.concatenate([d0b, d1b], 1)
                dvacc[krows, cols] += dot_nn(pb, ds_[:, :LANES])
                dkacc[krows, cols] += dot_nn(db, qs[:, :LANES])
                dst = jnp.concatenate([d0b.T, d1b.T], 1)
                kz = jnp.concatenate([jnp.where(low, kk, zero), jnp.where(low, zero, kk)], 0)
                dqacc[:, cols] += dot_nn(dst, kz)
            return 0
        lax.fori_loop(lo, hi, k_block, 0)
        dq_ref[rows, :] = (dqacc[...] * scale).astype(bf16)
        return 0
    lax.fori_loop(0, nblk, q_block, 0)
    dk_ref[...] = dkacc[...].astype(bf16)
    dv_ref[...] = dvacc[...].astype(bf16)
    pad = jnp.zeros((BLOCK, LANES), f32)
    sub = lax.broadcasted_iota(jnp.int32, (8, 2 * LANES), 0)
    for h in range(heads):
        for d in range(NEAR):
            t = gacc[h, d]
            if d in (0, 4):
                s = jnp.concatenate([jnp.sum(t, 0, keepdims=True), jnp.zeros((1, LANES), f32)], 1)
            else:
                wide = jnp.concatenate([t, pad], 1)
                s = jnp.zeros((8, 2 * LANES), f32)
                for a in range(BLOCK // 8):
                    s = s + pltpu.roll(wide[8 * a : 8 * a + 8], BLOCK - 8 * a, 1)
                for bit in (1, 2, 4):
                    s = jnp.where((sub & bit) > 0, pltpu.roll(s, 2 * LANES - bit, 1), s)
                s = jnp.sum(s, 0, keepdims=True)
            gsum_ref[h * NEAR + d : h * NEAR + d + 1, :] = s


def attn_bwd(lo, hi, q, k, v, qx, do, o, km, diag, scale):
    length, width = q.shape
    heads = diag.shape[0] // 2
    pairs = heads // 2
    nblk = length // BLOCK
    smem = pl.BlockSpec(memory_space=pltpu.SMEM)
    vmem = pl.BlockSpec(memory_space=pltpu.VMEM)
    f32, bf16 = jnp.float32, jnp.bfloat16
    act = jax.ShapeDtypeStruct((length, width), bf16)
    return pl.pallas_call(
        functools.partial(attn_bwd_kernel, heads=heads, scale=scale),
        out_shape=(act, act, act, jax.ShapeDtypeStruct((heads * NEAR, 256), f32)),
        in_specs=[smem, smem] + [vmem] * 8,
        out_specs=(vmem,) * 4,
        scratch_shapes=[
            pltpu.VMEM((pairs, 2 * BLOCK, 2 * LANES), bf16),
            pltpu.VMEM((pairs, 2 * BLOCK, 2 * LANES), bf16),
            pltpu.VMEM((heads, NEAR, BLOCK, BLOCK), f32),
            pltpu.VMEM((heads, NEAR, BLOCK, BLOCK), f32),
            pltpu.VMEM((length, width), f32),
            pltpu.VMEM((length, width), f32),
            pltpu.VMEM((BLOCK, width), f32),
        ],
        compiler_params=pltpu.CompilerParams(vmem_limit_bytes=60 << 20),
        cost_estimate=pl.CostEstimate(flops=10 * length * length * width, bytes_accessed=20 * length * width, transcendentals=length * length * heads),
    )(lo, hi, q, k, v, qx, do, o, km, diag)


def rms_forward(values, norm_gain):
    inverse = lax.rsqrt(jnp.mean(values * values, -1, keepdims=True) + epsilon)
    return (values * inverse * norm_gain, inverse)


def rms_backward(values, inverse, norm_gain, upstream):
    scaled = upstream * norm_gain
    gain_grad = jnp.sum(upstream * values * inverse, 0)
    input_grad = inverse * (
        scaled - values * inverse * inverse * jnp.mean(scaled * values, -1, keepdims=True)
    )
    return (input_grad, gain_grad)


def matmul(left, right):
    return jnp.dot(left, right, preferred_element_type=jnp.float32)


def matmul_tn(left, right):
    return lax.dot_general(left, right, (((0,), (0,)), ((), ())), preferred_element_type=jnp.float32)


def matmul_nt(left, right):
    return lax.dot_general(left, right, (((1,), (1,)), ((), ())), preferred_element_type=jnp.float32)


def attention_operands(segment_row, bias_grid):
    f32 = jnp.float32
    first, last = segment_row[::BLOCK], segment_row[BLOCK - 1 :: BLOCK]
    lo = jnp.sum(segment_row[None, :] < first[:, None], 1) // BLOCK
    hi = (jnp.sum(segment_row[None, :] <= last[:, None], 1) + BLOCK - 1) // BLOCK
    lane = lax.iota(jnp.int32, LANES)[None, :]
    same = segment_row[:, None] == lane
    query_mask = jnp.where(same, masked_score, 0.0).astype(jnp.bfloat16)
    ones = ((lane % 64 >= 8) & (lane % 64 <= 10)).astype(f32)
    key_mask = jnp.where(lane < 8, 1.0 - same.astype(f32), ones).astype(jnp.bfloat16)
    relative = lax.iota(jnp.int32, 512) - 256
    buckets = bucket_of(jnp.concatenate([relative, 256 - lax.iota(jnp.int32, 512)]))
    hot = (lax.iota(jnp.int32, bias_grid.shape[0])[:, None] == buckets[None, :]).astype(f32)
    along = lax.dot_general(
        bias_grid, hot, (((0,), (0,)), ((), ())), precision=precise_setting
    )
    diag = jnp.concatenate([along[:, :512], along[:, 512:]], 0)
    return lo.astype(jnp.int32), hi.astype(jnp.int32), query_mask, key_mask, diag


def bias_grad(sums, heads, bucket_count):
    near = lax.broadcasted_iota(jnp.int32, (NEAR, 2 * LANES), 0)
    place = lax.broadcasted_iota(jnp.int32, (NEAR, 2 * LANES), 1)
    bucket = bucket_of((near - 2) * BLOCK + BLOCK - place)
    bucket = jnp.where(near == 0, 15, jnp.where(near == NEAR - 1, 31, bucket))
    hot = (bucket.reshape(-1)[:, None] == lax.iota(jnp.int32, bucket_count)[None, :]).astype(jnp.float32)
    return jnp.dot(sums.reshape(heads, -1), hot, precision=precise_setting).T


def per_device(
    tokens,
    segments,
    routes,
    cotangent,
    attn_gain,
    ffn_gain,
    query_weight,
    key_weight,
    value_weight,
    output_weight,
    position_bias_grid,
    router_weight,
    expert_in,
    expert_out,
):
    f32, bf16 = jnp.float32, jnp.bfloat16
    token_count, model_width = tokens.shape
    bucket_count, head_count = position_bias_grid.shape
    head_width = model_width // head_count
    score_scale = head_width ** (-0.5)
    experts_all = router_weight.shape[1]
    capacity = (5 * token_count + 4 * experts_all - 1) // (4 * experts_all)
    slots = experts_all * capacity

    chosen = routes[:, 0]
    expert_hot = chosen[:, None] == lax.iota(jnp.int32, experts_all)[None, :]
    expert_float = expert_hot.astype(f32)
    before = lax.iota(jnp.int32, token_count)[:, None] > lax.iota(jnp.int32, token_count)[None, :]
    ranks = matmul(before.astype(bf16), expert_hot.astype(bf16))
    slot_rank = jnp.sum(ranks * expert_float, 1).astype(jnp.int32)
    token_slot = jnp.where(slot_rank < capacity, chosen * capacity + slot_rank, slots)
    to_slots = (lax.iota(jnp.int32, slots)[:, None] == token_slot[None, :]).astype(bf16)

    inputs = tokens.astype(f32)
    normed, inverse_one = rms_forward(inputs, attn_gain)
    normed_low = normed.astype(bf16)
    queries = (matmul(normed_low, query_weight).astype(bf16) * score_scale).astype(bf16)
    key_rows = matmul(normed_low, key_weight).astype(bf16)
    value_rows = matmul(normed_low, value_weight).astype(bf16)
    lo, hi, query_mask, key_mask, diag = attention_operands(segments[0], position_bias_grid)
    attended, query_extra = attn_fwd(
        lo, hi, queries, key_rows, value_rows, query_mask, key_mask, diag[:head_count]
    )
    middle = inputs + matmul(attended, output_weight)
    hidden_two, inverse_two = rms_forward(middle, ffn_gain)
    logits = jnp.dot(hidden_two, router_weight, precision=precise_setting)
    top_logit = jnp.max(logits, -1, keepdims=True)
    exponents_router = jnp.exp(logits - top_logit)
    router_probs = exponents_router / jnp.sum(exponents_router, -1, keepdims=True)
    gate_values = jnp.sum(router_probs * expert_float, 1)
    upstream = cotangent.astype(f32)

    def exchange(rows):
        rows = rows.reshape(experts_all, capacity, model_width)
        rows = lax.all_to_all(rows, "expert", split_axis=0, concat_axis=0, tiled=True)
        return rows.reshape(slots, model_width)

    arrived = exchange(matmul(to_slots, hidden_two.astype(bf16)).astype(bf16))
    out_grad_rows = (gate_values[:, None] * upstream).astype(bf16)
    grad_arrived = exchange(matmul(to_slots, out_grad_rows).astype(bf16))
    weight_in, weight_out = expert_in[0], expert_out[0]
    pre_act = matmul(arrived, weight_in)
    activated = jax.nn.gelu(pre_act, approximate=False).astype(bf16)
    produced = matmul(activated, weight_out).astype(bf16)
    returned = exchange(produced)
    expert_rows = matmul_tn(to_slots, returned)
    mixed = (middle + gate_values[:, None] * expert_rows).astype(bf16)
    gate_grad = jnp.sum(upstream * expert_rows, 1)

    act_grad = matmul_nt(grad_arrived, weight_out)
    _, gelu_pull = jax.vjp(functools.partial(jax.nn.gelu, approximate=False), pre_act)
    pre_grad = gelu_pull(act_grad)[0].astype(bf16)
    out_weight_grad = matmul_tn(activated, grad_arrived)
    in_weight_grad = matmul_tn(arrived, pre_grad)
    home_grad = exchange(matmul_nt(pre_grad, weight_in).astype(bf16))
    in_weight_grad = lax.psum_scatter(
        in_weight_grad.astype(bf16), "dp", scatter_dimension=1, tiled=True
    ).astype(f32)
    out_weight_grad = lax.psum_scatter(
        out_weight_grad.astype(bf16), "dp", scatter_dimension=0, tiled=True
    ).astype(f32)
    expert_input_grad = matmul_tn(to_slots, home_grad)
    logit_grad = router_probs * (
        expert_float * gate_grad[:, None] - (gate_values * gate_grad)[:, None]
    )
    router_grad = jnp.dot(hidden_two.T, logit_grad, precision=precise_setting)
    hidden_grad = expert_input_grad + jnp.dot(
        logit_grad, router_weight.T, precision=precise_setting
    )
    middle_part, ffn_gain_grad = rms_backward(middle, inverse_two, ffn_gain, hidden_grad)
    middle_grad = upstream + middle_part
    branch_grad = middle_grad.astype(bf16)
    output_weight_grad = matmul_tn(attended, branch_grad)
    attended_grad = matmul_nt(branch_grad, output_weight).astype(bf16)
    query_grad, key_grad, value_grad, diag_sums = attn_bwd(
        lo, hi, queries, key_rows, value_rows, query_extra, attended_grad, attended, key_mask,
        diag, score_scale,
    )
    table_grad = bias_grad(diag_sums, head_count, bucket_count)
    query_weight_grad = matmul_tn(normed_low, query_grad)
    key_weight_grad = matmul_tn(normed_low, key_grad)
    value_weight_grad = matmul_tn(normed_low, value_grad)
    normed_grad = (
        matmul_nt(query_grad, query_weight)
        + matmul_nt(key_grad, key_weight)
        + matmul_nt(value_grad, value_weight)
    )
    input_part, attn_gain_grad = rms_backward(inputs, inverse_one, attn_gain, normed_grad)
    token_grad = (middle_grad + input_part).astype(bf16)
    weights = jnp.concatenate(
        [query_weight_grad, key_weight_grad, value_weight_grad, output_weight_grad], 1
    ).astype(bf16)
    weights = lax.psum(weights, ("dp", "expert")).astype(f32)
    weights = [weights[:, i * model_width : (i + 1) * model_width] for i in range(4)]
    small = lax.psum((table_grad, router_grad, attn_gain_grad, ffn_gain_grad), ("dp", "expert"))
    return (
        mixed,
        token_grad,
        small[2],
        small[3],
        *weights,
        small[0],
        small[1],
        in_weight_grad[None],
        out_weight_grad[None],
    )


def solution(mesh):
    rows = P(("dp", "expert"), None)
    return jax.shard_map(
        per_device,
        mesh=mesh,
        in_specs=(rows,) * 4 + (P(),) * 8 + (P("expert", None, None),) * 2,
        out_specs=(rows,) * 2 + (P(),) * 8 + (P("expert", None, "dp"), P("expert", "dp", None)),
        check_vma=False,
    )
```

time: 944 us -> 620 us (0.66)
  matrix products: 448 us -> 174 us
  Pallas kernels: 0 us -> 98.1 us
  blocking collectives: 142 us -> 56.9 us
  other arithmetic: 96.7 us -> 18.4 us
  local copies, waits for them, and re-layouts: 71.8 us -> 28.4 us
  waiting for transfers between devices: 151 us -> 192 us
  starting transfers between devices: 9.35 us -> 28.1 us
    dot_general x31 -> x25, matrix products: 429 us -> 160 us  [the longest x9 77 us: matmul(): return jnp.dot(left, right, preferred_element_type=jnp.float32)]
    all_to_all x2 -> x0, blocking collectives: 101 us -> none  [the longest x1 51.1 us: per_device(): lax.all_to_all(slots_out, 'expert', split_axis=0, concat_axis=0, tiled=True)]
    pallas_call x0 -> x2, Pallas kernels: none -> 98.1 us  [the longest x1 67.9 us: attn_bwd(): pl.pallas_call(functools.partial(attn_bwd_kernel, heads=heads, scale=scal...]
    convert_element_type x10 -> x4, other arithmetic: 50.4 us -> 4.56 us  [the longest x1 2.06 us: per_device(): token_grad = (middle_grad + input_part).astype(bf16)]
    all_to_all x2 -> x4, waiting for transfers between devices: 57.7 us -> 103 us  [exchange(): lax.all_to_all(rows, 'expert', split_axis=0, concat_axis=0, tiled=True)]
    reduce_sum x4 -> x1, other arithmetic: 25.8 us -> 0.22 us  [attention_operands(): jnp.sum(segment_row[None, :] <= last[:, None], 1) + BLOCK - 1]
    unnamed x219 -> x100, local copies, waits for them, and re-layouts: 43.1 us -> 20.5 us
    gather x4 -> x0, local copies, waits for them, and re-layouts: 20.2 us -> none  [the longest x1 5.21 us: per_device(): jnp.take(with_zero_row(returned.reshape(dump_slot, model_width)), token_s...]
  transfers between devices with their start and end apart: 5 -> 7, of which waited for: 3 -> 4; matrix products, arithmetic and copies ran while one was open for 32% -> 22% of each run, Pallas kernels for 0% -> 0%
where the time goes in v1:
time: 620 us; the launch traced here: 613 us
  waiting for transfers between devices  192 us (31%)
  matrix products  174 us (28%)
  Pallas kernels  98.1 us (16%)
  blocking collectives  56.9 us (9%)
  local copies, waits for them, and re-layouts  28.4 us (5%)
  starting transfers between devices  28.1 us (5%)
  other arithmetic  18.4 us (3%)
  between operations  16.3 us (3%)
    all_to_all x4, waiting for transfers between devices, exchange(): lax.all_to_all(rows, 'expert', split_axis=0, concat_axis=0, tiled=True)  103 us
    psum x1, waiting for transfers between devices, per_device(): weights = lax.psum(weights, ('dp', 'expert')).astype(f32)  89.6 us
    dot_general x9, matrix products, matmul(): return jnp.dot(left, right, preferred_element_type=jnp.float32)  77 us
    pallas_call x1, Pallas kernels, attn_bwd(): pl.pallas_call(functools.partial(attn_bwd_kernel, heads=heads, scale=scal...  67.9 us
    psum x1, blocking collectives, per_device(): lax.psum((table_grad, router_grad, attn_gain_grad, ffn_gain_grad), ('dp',...  56.9 us
    dot_general x6, matrix products, matmul_nt(): lax.dot_general(left, right, (((1,), (1,)), ((), ())), preferred_element_...  41.8 us
    dot_general x8, matrix products, matmul_tn(): lax.dot_general(left, right, (((0,), (0,)), ((), ())), preferred_element_...  40.2 us
    pallas_call x1, Pallas kernels, attn_fwd(): pl.pallas_call(functools.partial(attn_fwd_kernel, heads=heads), out_shape...  30.1 us
  transfers between devices with their start and end apart: 7, of which 4 were waited for; matrix products, arithmetic and copies ran while one was open for 22% of the time, Pallas kernels for 0%

profile of v1, /device:TPU:1, one launch (start us, length us, event | category | flops | bytes accessed | tf_op | source)
XLA Modules:
  0.0 612.7 jit_solution(10903402465187239287)
XLA Ops:
  14.7 1.7 copy.39
  16.9 4.1 convolution_convert_fusion.4.k_ref
  21.0 2.7 convolution_convert_fusion.3.v_ref
  23.7 2.7 fusion.56.q_ref
  28.0 30.1 %shard_map.229 = (bf16[1024,768]{1,0:T(8,128)(2,1)}, bf16[1024,768]{1,0:T(8,128)(2,1)}) custom-call(s32[8]{0:T(128)} %get-tuple-element.80.lo_ref, s32[8]{0:T(128)} %get-tuple-element.79.hi_ref, bf16[1024,768]{1,0:T(8,128)(2,1)} %fusion.56.q_ref, bf16[1024,768]{1,0:T(8,128)(2,1)} %convolution_convert_fusion.4.k_ref, ...), custom_call_target="tpu_custom_call" | custom-call | flops 3221225472 | bytes 7864320 | tf_op jit(solution)/shard_map/pallas_call | solution.py:133
  58.2 3.3 multiply_reduce_fusion.2
  61.5 3.9 fusion.26
  65.4 9.7 %all-to-all-start = ((bf16[8,160,768]{2,1,0:T(8,128)(2,1)}), bf16[8,160,768]{2,1,0:T(8,128)(2,1)}, u32[]{:S(2)}, u32[]{:S(2)}) async-start(bf16[8,160,768]{2,1,0:T(8,128)(2,1)} %bitcast.3), calls=%async_computation | async-start | bytes 3932160 | tf_op jit(solution)/shard_map/all_to_all | solution.py:388
  75.1 1.7 copy.40
  76.9 4.4 fusion.97
  82.0 3.8 fusion.27
  85.8 32.4 %all-to-all-done = bf16[8,160,768]{2,1,0:T(8,128)(2,1)} async-done(((bf16[8,160,768]{2,1,0:T(8,128)(2,1)}), bf16[8,160,768]{2,1,0:T(8,128)(2,1)}, u32[]{:S(2)}, u32[]{:S(2)}) %all-to-all-start) | async-done | bytes 1966112 | tf_op jit(solution)/shard_map/all_to_all | solution.py:388
  118.2 6.7 %all-to-all-start.2 = ((bf16[8,160,768]{2,1,0:T(8,128)(2,1)}), bf16[8,160,768]{2,1,0:T(8,128)(2,1)}, u32[]{:S(2)}, u32[]{:S(2)}) async-start(bf16[8,160,768]{2,1,0:T(8,128)(2,1)} %bitcast.66), calls=%async_computation.2 | async-start | bytes 3932160 | tf_op jit(solution)/shard_map/all_to_all | solution.py:388
  124.9 44.4 %multiply_convert_fusion = (bf16[1280,3072]{1,0:T(8,128)(2,1)}, f32[1280,3072]{1,0:T(8,128)}, f32[1280,3072]{1,0:T(8,128)}) fusion(bf16[1280,768]{1,0:T(8,128)(2,1)} %bitcast.4, bf16[1,768,3072]{2,1,0:T(8,128)(2,1)} %param.26), kind=kOutput, calls=%fused_computation.3 | convolution fusion | flops 6295388160 | bytes 46006272 | tf_op jit(solution)/shard_map/dot_general | solution.py:293
  169.3 21.4 %add_convert_fusion = bf16[1280,3072]{1,0:T(8,128)(2,1)} fusion(f32[1280,3072]{1,0:T(8,128)} %get-tuple-element.59, bf16[1280,768]{1,0:T(8,128)(2,1)} %bitcast.10, f32[1280,3072]{1,0:T(8,128)} %get-tuple-element.72, bf16[1,3072,768]{2,1,0:T(8,128)(2,1)} %param.27), kind=kOutput, calls=%fused_computation.2 | convolution fusion | flops 6094848000 | bytes 46006272 | tf_op jit(solution)/shard_map/dot_general | solution.py:301
  190.7 11.0 %fusion.20 = bf16[1280,768]{1,0:T(8,128)(2,1)} fusion(bf16[1280,3072]{1,0:T(8,128)(2,1)} %add_convert_fusion, bf16[1,768,3072]{2,1,0:T(8,128)(2,1)} %param.26), kind=kOutput, calls=%fused_computation.44 | convolution fusion | flops 6040780800 | bytes 14548992 | tf_op jit(solution)/shard_map/dot_general | solution.py:301
  201.6 5.4 all-to-all-start.3
  207.1 10.9 %fusion.23 = bf16[1280,768]{1,0:T(8,128)(2,1)} fusion(bf16[1280,3072]{1,0:T(8,128)(2,1)} %get-tuple-element.58, bf16[1,3072,768]{2,1,0:T(8,128)(2,1)} %param.27), kind=kOutput, calls=%fused_computation.45 | convolution fusion | flops 6040780800 | bytes 14548992 | tf_op jit(solution)/shard_map/dot_general | solution.py:293
  218.0 32.5 %all-to-all-done.3 = bf16[8,160,768]{2,1,0:T(8,128)(2,1)S(1)} async-done(((bf16[8,160,768]{2,1,0:T(8,128)(2,1)}), bf16[8,160,768]{2,1,0:T(8,128)(2,1)S(1)}, u32[]{:S(2)}, u32[]{:S(2)}) %all-to-all-start.3) | async-done | bytes 1966112 | tf_op jit(solution)/shard_map/all_to_all | solution.py:388
  250.5 5.8 all-to-all-start.1
  257.2 5.6 fusion.6
  262.8 37.8 %all-to-all-done.1 = bf16[8,160,768]{2,1,0:T(8,128)(2,1)} async-done(((bf16[8,160,768]{2,1,0:T(8,128)(2,1)}), bf16[8,160,768]{2,1,0:T(8,128)(2,1)}, u32[]{:S(2)}, u32[]{:S(2)}) %all-to-all-start.1) | async-done | bytes 1966112 | tf_op jit(solution)/shard_map/all_to_all | solution.py:388
  300.7 4.1 fusion.35
  304.9 3.6 multiply_reduce_fusion
  308.5 3.0 convert_add_fusion.1
  311.5 2.5 convolution_convert_fusion.6
  314.0 2.6 convolution_convert_fusion.2.do_ref
  316.6 67.9 %shard_map.230 = (bf16[1024,768]{1,0:T(8,128)(2,1)}, bf16[1024,768]{1,0:T(8,128)(2,1)}, bf16[1024,768]{1,0:T(8,128)(2,1)}, f32[60,256]{1,0:T(8,128)}) custom-call(s32[8]{0:T(128)} %get-tuple-element.80.lo_ref, s32[8]{0:T(128)} %get-tuple-element.79.hi_ref, bf16[1024,768]{1,0:T(8,128)(2,1)} %fusion.56.q_ref, ...), custom_call_target="tpu_custom_call" | custom-call | flops 8053063680 | bytes 15728640 | tf_op jit(solution)/shard_map/pallas_call | solution.py:259
  384.6 3.1 convolution_convert_fusion.9
  387.7 1.7 convolution_convert_fusion.8
  391.1 2.5 pad_maximum_fusion
  393.7 10.8 %convolution_convert_fusion.1 = bf16[768,3072]{1,0:T(8,128)(2,1)} fusion(bf16[1280,768]{1,0:T(8,128)(2,1)} %bitcast.4, bf16[1280,3072]{1,0:T(8,128)(2,1)} %add_convert_fusion), kind=kOutput, calls=%fused_computation.28 | convolution fusion | flops 6042157056 | bytes 14548992 | tf_op jit(solution)/shard_map/dot_general | solution.py:297
  404.7 10.8 %convolution_convert_fusion = bf16[3072,768]{1,0:T(8,128)(2,1)} fusion(bf16[1280,3072]{1,0:T(8,128)(2,1)} %get-tuple-element.58, bf16[1280,768]{1,0:T(8,128)(2,1)} %bitcast.10), kind=kOutput, calls=%fused_computation.27 | convolution fusion | flops 6042157056 | bytes 14548992 | tf_op jit(solution)/shard_map/dot_general | solution.py:297
  415.8 2.6 copy.46
  418.4 3.4 fusion.99
  423.3 2.1 fusion.39
  425.4 2.1 fusion.33
  427.4 2.6 copy.47
  430.5 5.8 fusion.44
  436.3 56.9 %all-reduce = (f32[768]{0:T(1024)}, f32[768]{0:T(1024)}, f32[32,12]{0,1:T(8,128)}, f32[768,8]{0,1:T(8,128)}) all-reduce(f32[768]{0:T(1024)S(1)} %get-tuple-element.50, f32[768]{0:T(1024)S(1)} %get-tuple-element.48, f32[32,12]{0,1:T(8,128)S(1)} %fusion.61, f32[768,8]{0,1:T(8,128)S(1)} %fusion.44), channel_id=1, replica_groups=mesh['dp'=4,'expert'=8] {'dp','expert'}, use_global_device_ids=true, to_apply=%region_12.13 | all-reduce | flops 8064 | bytes 64512 | tf_op jit(solution)/shard_map/psum | solution.py:448
  493.2 89.6 %all-reduce.3.cloned.1.call-done = bf16[768,3072]{0,1:T(8,128)(2,1)} async-done(((bf16[768,3072]{0,1:T(8,128)(2,1)}), bf16[768,3072]{0,1:T(8,128)(2,1)}) %all-reduce.3.cloned.1.call-update) | async-done | bytes 4718608 | tf_op jit(solution)/shard_map/psum | solution.py:446
  582.8 5.5 fusion.95
  588.3 3.0 copy.51
  591.3 3.0 copy.50
  594.4 3.0 copy.49
  597.4 1.9 copy.48
  599.3 2.8 bitcast_convert_fusion.1
  602.2 2.8 bitcast_convert_fusion
  (138 shorter events, 14.5 us)
Async XLA Ops:
  8.0 13.0 %copy-start = (bf16[768,768]{1,0:T(8,128)(2,1)S(1)}, bf16[768,768]{1,0:T(8,128)(2,1)}, u32[]{:S(2)}) copy-start(bf16[768,768]{1,0:T(8,128)(2,1)} %param.22) | copy-start | bytes 3538948
  9.7 7.2 %copy-start.33 = (f32[768]{0:T(1024)S(1)}, f32[768]{0:T(1024)}, u32[]{:S(2)}) copy-start(f32[768]{0:T(1024)} %param.18) | copy-start | bytes 9220
  13.2 68.7 %copy-start.38 = (s32[1024]{0:T(1024)}, s32[1024]{0:T(1024)S(1)}, u32[]{:S(2)}) copy-start(s32[1024]{0:T(1024)S(1)} %add_select_fusion) | copy-start | bytes 12292
  16.5 41.7 %copy-start.3 = (bf16[1024,768]{0,1:T(8,128)(2,1)}, bf16[1024,768]{0,1:T(8,128)(2,1)S(1)}, u32[]{:S(2)}) copy-start(bf16[1024,768]{0,1:T(8,128)(2,1)S(1)} %copy.39) | copy-start | bytes 4718596
  16.9 6.8 %copy-start.16 = (f32[1024]{0:T(1024)}, f32[1024]{0:T(1024)S(1)}, u32[]{:S(2)}) copy-start(f32[1024]{0:T(1024)S(1)} %add_rsqrt_fusion.1) | copy-start | bytes 12292
  21.0 2.7 copy-start.41
  23.7 2.7 copy-start.35
  58.2 3.4 copy-start.26
  61.5 3.9 copy-start.1
  61.5 15.3 %copy-start.20 = (f32[1024]{0:T(1024)}, f32[1024]{0:T(1024)S(1)}, u32[]{:S(2)}) copy-start(f32[1024]{0:T(1024)S(1)} %add_rsqrt_fusion) | copy-start | bytes 12292
  65.4 11.5 %copy-start.24 = (f32[768,8]{0,1:T(8,128)S(1)}, f32[768,8]{0,1:T(8,128)}, u32[]{:S(2)}) copy-start(f32[768,8]{0,1:T(8,128)} %param.25) | copy-start | bytes 73732
  65.4 52.8 %all-to-all-start = ((bf16[8,160,768]{2,1,0:T(8,128)(2,1)}), bf16[8,160,768]{2,1,0:T(8,128)(2,1)}, u32[]{:S(2)}, u32[]{:S(2)}) async-start(bf16[8,160,768]{2,1,0:T(8,128)(2,1)} %bitcast.3), calls=%async_computation | async-start | bytes 3932160 | tf_op jit(solution)/shard_map/all_to_all | solution.py:388
  75.1 6.8 %copy-start.28 = (s32[1024,1]{0,1:T(1,128)S(1)}, s32[1024,1]{0,1:T(1,128)}, u32[]{:S(2)}) copy-start(s32[1024,1]{0,1:T(1,128)} %param.16) | copy-start | bytes 12292
  76.8 8.9 %copy-start.7 = (bf16[1024,768]{0,1:T(8,128)(2,1)}, bf16[1024,768]{0,1:T(8,128)(2,1)S(1)}, u32[]{:S(2)}) copy-start(bf16[1024,768]{0,1:T(8,128)(2,1)S(1)} %copy.40) | copy-start | bytes 4718596
  81.9 3.9 copy-start.30
  81.9 3.8 copy-start.36
  118.2 51.1 %all-to-all-start.2 = ((bf16[8,160,768]{2,1,0:T(8,128)(2,1)}), bf16[8,160,768]{2,1,0:T(8,128)(2,1)}, u32[]{:S(2)}, u32[]{:S(2)}) async-start(bf16[8,160,768]{2,1,0:T(8,128)(2,1)} %bitcast.66), calls=%async_computation.2 | async-start | bytes 3932160 | tf_op jit(solution)/shard_map/all_to_all | solution.py:388
  201.6 48.9 %all-to-all-start.3 = ((bf16[8,160,768]{2,1,0:T(8,128)(2,1)}), bf16[8,160,768]{2,1,0:T(8,128)(2,1)S(1)}, u32[]{:S(2)}, u32[]{:S(2)}) async-start(bf16[8,160,768]{2,1,0:T(8,128)(2,1)} %bitcast.67), calls=%async_computation.3 | async-start | bytes 3932160 | tf_op jit(solution)/shard_map/all_to_all | solution.py:388
  218.0 38.6 %copy-start.18 = (f32[12,512]{1,0:T(8,128)S(1)}, f32[12,512]{1,0:T(8,128)}, u32[]{:S(2)}) copy-start(f32[12,512]{1,0:T(8,128)} %get-tuple-element.66) | copy-start | bytes 73732
  218.0 38.6 %copy-start.19 = (f32[12,512]{1,0:T(8,128)S(1)}, f32[12,512]{1,0:T(8,128)}, u32[]{:S(2)}) copy-start(f32[12,512]{1,0:T(8,128)} %get-tuple-element.67.diag_ref) | copy-start | bytes 73732
  218.0 39.2 %copy-start.39 = (s32[1024]{0:T(1024)S(1)}, s32[1024]{0:T(1024)}, u32[]{:S(2)}) copy-start(s32[1024]{0:T(1024)} %copy-done.38) | copy-start | bytes 12292
  250.5 6.7 %copy-start.12 = (bf16[8,160,768]{2,1,0:T(8,128)(2,1)}, bf16[8,160,768]{2,1,0:T(8,128)(2,1)S(1)}, u32[]{:S(2)}) copy-start(bf16[8,160,768]{2,1,0:T(8,128)(2,1)S(1)} %all-to-all-done.3) | copy-start | bytes 5898244
  250.5 50.1 %all-to-all-start.1 = ((bf16[8,160,768]{2,1,0:T(8,128)(2,1)}), bf16[8,160,768]{2,1,0:T(8,128)(2,1)}, u32[]{:S(2)}, u32[]{:S(2)}) async-start(bf16[8,160,768]{2,1,0:T(8,128)(2,1)} %bitcast.65), calls=%async_computation.1 | async-start | bytes 3932160 | tf_op jit(solution)/shard_map/all_to_all | solution.py:388
  256.3 326.5 %all-reduce.3.cloned.1.call-start = ((), (), s32[]{:S(2)}) async-start(), calls=%async_computation.6 | async-start | bytes 9437184 | tf_op jit(solution)/shard_map/psum | solution.py:446
  257.2 43.4 %copy-start.8 = (bf16[1024,768]{0,1:T(8,128)(2,1)S(1)}, bf16[1024,768]{0,1:T(8,128)(2,1)}, u32[]{:S(2)}) copy-start(bf16[1024,768]{0,1:T(8,128)(2,1)} %copy-done.7) | copy-start | bytes 4718596
  300.6 4.2 copy-start.37
  300.6 4.2 copy-start.2
  300.6 4.2 copy-start.11
  300.6 4.2 copy-start.15
  300.6 4.2 copy-start.21
  300.6 4.2 copy-start.23
  300.6 4.2 copy-start.25
  300.6 4.2 copy-start.27
  300.7 4.2 copy-start.29
  300.7 4.2 copy-start.31
  308.5 3.0 copy-start.45
  311.5 2.5 copy-start.5
  311.5 2.5 copy-start.40
  316.6 67.9 %copy-start.4 = (bf16[1024,768]{0,1:T(8,128)(2,1)S(1)}, bf16[1024,768]{0,1:T(8,128)(2,1)}, u32[]{:S(2)}) copy-start(bf16[1024,768]{0,1:T(8,128)(2,1)} %copy-done.3) | copy-start | bytes 4718596
  316.6 68.0 %copy-start.17 = (f32[1024]{0:T(1024)S(1)}, f32[1024]{0:T(1024)}, u32[]{:S(2)}) copy-start(f32[1024]{0:T(1024)} %copy-done.16) | copy-start | bytes 12292
  316.6 68.0 %copy-start.34 = (f32[768]{0:T(1024)S(1)}, f32[768]{0:T(1024)}, u32[]{:S(2)}) copy-start(f32[768]{0:T(1024)} %param.18) | copy-start | bytes 9220
  384.6 3.2 copy-start.44
  393.6 205.7 %reduce-scatter.3.cloned.1.call-start = ((), (), s32[]{:S(2)}) async-start(), calls=%async_computation.7 | async-start | bytes 5898240 | tf_op jit(solution)/shard_map/reduce_scatter | solution.py:409
  404.5 197.7 %reduce-scatter.5.cloned.1.call-start = ((), (), s32[]{:S(2)}) async-start(), calls=%async_computation.8 | async-start | bytes 5898240 | tf_op jit(solution)/shard_map/reduce_scatter | solution.py:412
  415.5 2.9 copy-start.32
  418.4 3.4 copy-start.42
  418.4 3.4 copy-start.43
  423.3 2.1 copy-start.6
  (5 other events, 6.0 us)
Sparse Core Ops, SparseCore 0:
  393.7 189.0 all-reduce.2
Sparse Core Ops, SparseCore 1:
  404.6 66.9 reduce-scatter.2
  474.0 48.1 reduce-scatter.4

commit v2 on v1

--- a/solution.py
+++ b/solution.py
@@ -275,6 +275,255 @@
     )(lo, hi, q, k, v, qx, do, o, km, diag)
 
 
+def gelu_parts(v):
+    mag = jnp.abs(v)
+    t = 1.0 / (1.0 + (0.3275911 * 0.7071067811865476) * mag)
+    poly = t * (0.127414796 + t * (-0.142248368 + t * (0.7107068705 + t * (-0.7265760135 + t * 0.5307027145))))
+    gauss = jnp.exp(-0.5 * v * v)
+    tail = poly * gauss
+    phi = jnp.where(v < 0, tail, 1.0 - tail)
+    return v * phi, phi + v * gauss * 0.3989422804014327
+
+
+def flip_bits(index, mask, count):
+    out = 0
+    bit = 1
+    while bit < count:
+        a, b = (index // bit) % 2, (mask // bit) % 2
+        out = out + bit * (a + b - 2 * a * b)
+        bit *= 2
+    return out
+
+
+def ffn_kernel(
+    xs, gs, g, win_hbm, wout_hbm,
+    home, home_gate, produced, keep, give,
+    win, wout, xr, gr, act, pg, gated, igs, ggs, dws, dwr, stage,
+    wsem, own_sem, psem, ksem, xsend, xrecv, gsend, grecv, isend, irecv, qsend, qrecv, dsend, drecv,
+    *, groups, dp_size, tiles,
+):
+    f32, bf16 = jnp.float32, jnp.bfloat16
+    me = lax.axis_index("expert")
+    dp = lax.axis_index("dp")
+    core = dp % 2
+    sibling = dp + 1 - 2 * core
+    rows = xs.shape[1]
+    width = xs.shape[2]
+    hidden = win.shape[1]
+    tile = hidden // tiles
+    lanes = gs.shape[2]
+
+    def there(peer):
+        return (dp, peer)
+
+    load_in = pltpu.make_async_copy(win_hbm, win, wsem.at[0])
+    load_out = pltpu.make_async_copy(wout_hbm, wout, wsem.at[1])
+    load_in.start()
+    load_out.start()
+    load_g = pltpu.make_async_copy(g, gated, wsem.at[2])
+    load_g.start()
+
+    barrier = pltpu.get_barrier_semaphore()
+
+    def greet(s, _):
+        pl.semaphore_signal(
+            barrier, inc=1, device_id=there(flip_bits(me, s, groups)), device_id_type=pl.DeviceIdType.MESH
+        )
+        return 0
+    lax.fori_loop(1, groups, greet, 0)
+    pl.semaphore_signal(barrier, inc=1, device_id=(sibling, me), device_id_type=pl.DeviceIdType.MESH)
+    pl.semaphore_wait(barrier, groups)
+
+    def x_copy(peer, slot):
+        return pltpu.make_async_remote_copy(
+            src_ref=xs.at[peer], dst_ref=xr.at[slot], send_sem=xsend.at[peer], recv_sem=xrecv.at[slot],
+            device_id=there(peer), device_id_type=pl.DeviceIdType.MESH)
+
+    def g_copy(peer, slot):
+        return pltpu.make_async_remote_copy(
+            src_ref=gs.at[peer], dst_ref=gr.at[slot], send_sem=gsend.at[peer], recv_sem=grecv.at[slot],
+            device_id=there(peer), device_id_type=pl.DeviceIdType.MESH)
+
+    def i_copy(peer, slot):
+        return pltpu.make_async_remote_copy(
+            src_ref=igs.at[peer], dst_ref=home.at[slot], send_sem=isend.at[peer], recv_sem=irecv.at[slot],
+            device_id=there(peer), device_id_type=pl.DeviceIdType.MESH)
+
+    def q_copy(peer, slot):
+        return pltpu.make_async_remote_copy(
+            src_ref=ggs.at[peer], dst_ref=home_gate.at[slot], send_sem=qsend.at[peer], recv_sem=qrecv.at[slot],
+            device_id=there(peer), device_id_type=pl.DeviceIdType.MESH)
+
+    def send(s, _):
+        peer = flip_bits(me, s, groups)
+        x_copy(peer, me).start()
+        g_copy(peer, me).start()
+        return 0
+    lax.fori_loop(1, groups, send, 0)
+    own_x = pltpu.make_async_copy(xs.at[me], xr.at[me], own_sem.at[0])
+    own_g = pltpu.make_async_copy(gs.at[me], gr.at[me], own_sem.at[1])
+    own_x.start()
+    own_g.start()
+    load_in.wait()
+    load_out.wait()
+    load_g.wait()
+
+    spot = (
+        lax.broadcasted_iota(jnp.int32, (rows, lanes), 0)
+        == lax.broadcasted_iota(jnp.int32, (rows, lanes), 1)
+    )
+
+    def work(p):
+        x = xr[p]
+        place = pl.ds(pl.multiple_of(p * rows, rows), rows)
+        gg = gated[place, :]
+        gate = jnp.sum(jnp.where(spot, gr[p, 0:1, :], 0.0), 1, keepdims=True)
+        gated[place, :] = (gate * gg.astype(f32)).astype(bf16)
+        total = jnp.zeros((rows, width), f32)
+        gate_grad = jnp.zeros((rows, 1), f32)
+        for t in range(tiles):
+            cols = slice(t * tile, (t + 1) * tile)
+            pre = matmul(x, win[:, cols])
+            out_grad = matmul_nt(gg, wout[cols, :])
+            value, slope = gelu_parts(pre)
+            act[place, cols] = value.astype(bf16)
+            gate_grad = gate_grad + jnp.sum(value * out_grad, 1, keepdims=True)
+            low = (gate * out_grad * slope).astype(bf16)
+            pg[place, cols] = low
+            total = total + matmul_nt(low, win[:, cols])
+        igs[p] = total.astype(bf16)
+        row = jnp.sum(jnp.where(spot, gate_grad, 0.0), 0, keepdims=True)
+        ggs[p] = jnp.broadcast_to(row, ggs.shape[1:])
+
+    own_x.wait()
+    own_g.wait()
+    work(me)
+    own_i = pltpu.make_async_copy(igs.at[me], home.at[me], own_sem.at[0])
+    own_q = pltpu.make_async_copy(ggs.at[me], home_gate.at[me], own_sem.at[1])
+    own_i.start()
+    own_q.start()
+
+    def chunk(s, _):
+        peer = flip_bits(me, s, groups)
+        x_copy(peer, peer).wait_recv()
+        g_copy(peer, peer).wait_recv()
+        work(peer)
+        i_copy(peer, me).start()
+        q_copy(peer, me).start()
+        return 0
+    lax.fori_loop(1, groups, chunk, 0)
+
+    def d_copy(k):
+        return pltpu.make_async_remote_copy(
+            src_ref=dws.at[k % 2], dst_ref=dwr.at[k], send_sem=dsend.at[k], recv_sem=drecv.at[k],
+            device_id=(sibling, me), device_id_type=pl.DeviceIdType.MESH)
+
+    part = hidden // dp_size
+    flat = groups * rows
+    items = [(which, half) for half in range(dp_size // 2) for which in range(2)]
+
+    def grad(which, quarter):
+        span = pl.ds(pl.multiple_of(quarter * part, part), part)
+        if which == 0:
+            return matmul_tn(xr[...].reshape(flat, width), pg[:, span])
+        return matmul_tn(act[:, span], gated[...])
+
+    half_of = dp // 2
+    for k, (which, half) in enumerate(items):
+        if k >= 2:
+            d_copy(k - 2).wait_send()
+        dws[k % 2] = grad(which, 2 * half + 1 - core).astype(bf16)
+        d_copy(k).start()
+
+    span = stage.shape[1]
+    copies = []
+    for b in range(flat // span):
+        if b >= 2:
+            copies[b - 2].wait()
+        stage[b % 2] = matmul(act[b * span : (b + 1) * span, :], wout[...]).astype(bf16)
+        copy = pltpu.make_async_copy(stage.at[b % 2], produced.at[pl.ds(b * span, span)], psem.at[b % 2])
+        copy.start()
+        copies.append(copy)
+    for copy in copies[-2:]:
+        copy.wait()
+    for k, (which, half) in enumerate(items):
+        local = grad(which, 2 * half + core)
+        d_copy(k).wait_recv()
+        both = (local + dwr[k].astype(f32)).astype(bf16)
+        dwr[k] = both
+    outs = []
+    for which in range(2):
+        outs.append(pltpu.make_async_copy(dwr.at[half_of * 2 + which], keep.at[which], ksem.at[which]))
+        outs.append(pltpu.make_async_copy(dwr.at[(1 - half_of) * 2 + which], give.at[which], ksem.at[2 + which]))
+    for copy in outs:
+        copy.start()
+    for copy in outs:
+        copy.wait()
+    own_i.wait()
+    own_q.wait()
+    for k in (2, 3):
+        d_copy(k).wait_send()
+
+    def finish(s, _):
+        peer = flip_bits(me, s, groups)
+        x_copy(peer, me).wait_send()
+        g_copy(peer, me).wait_send()
+        i_copy(peer, me).wait_send()
+        q_copy(peer, me).wait_send()
+        i_copy(peer, peer).wait_recv()
+        q_copy(peer, peer).wait_recv()
+        return 0
+    lax.fori_loop(1, groups, finish, 0)
+
+
+def ffn(xs, gs, g, weight_in, weight_out, groups, dp_size, tiles=6):
+    f32, bf16 = jnp.float32, jnp.bfloat16
+    _, rows, width = xs.shape
+    hidden = weight_in.shape[1]
+    lanes = gs.shape[2]
+    part = hidden // dp_size
+    anywhere = pl.BlockSpec(memory_space=pl.ANY)
+    sem = pltpu.SemaphoreType.DMA
+    flat = groups * rows
+    shape = jax.ShapeDtypeStruct
+    return pl.pallas_call(
+        functools.partial(ffn_kernel, groups=groups, dp_size=dp_size, tiles=tiles),
+        out_shape=(
+            shape((groups, rows, width), bf16),
+            shape((groups, 8, lanes), f32),
+            shape((flat, width), bf16),
+            shape((2, width, part), bf16),
+            shape((2, width, part), bf16),
+        ),
+        in_specs=[anywhere] * 5,
+        out_specs=(anywhere,) * 5,
+        scratch_shapes=[
+            pltpu.VMEM((width, hidden), bf16),
+            pltpu.VMEM((hidden, width), bf16),
+            pltpu.VMEM((groups, rows, width), bf16),
+            pltpu.VMEM((groups, 8, lanes), f32),
+            pltpu.VMEM((flat, hidden), bf16),
+            pltpu.VMEM((flat, hidden), bf16),
+            pltpu.VMEM((flat, width), bf16),
+            pltpu.VMEM((groups, rows, width), bf16),
+            pltpu.VMEM((groups, 8, lanes), f32),
+            pltpu.VMEM((2, width, part), bf16),
+            pltpu.VMEM((4, width, part), bf16),
+            pltpu.VMEM((2, flat // 8, width), bf16),
+            sem((3,)), sem((2,)), sem((2,)), sem((4,)),
+            sem((groups,)), sem((groups,)), sem((groups,)), sem((groups,)),
+            sem((groups,)), sem((groups,)), sem((groups,)), sem((groups,)),
+            sem((4,)), sem((4,)),
+        ],
+        compiler_params=pltpu.CompilerParams(
+            collective_id=1, has_side_effects=True, vmem_limit_bytes=62 << 20
+        ),
+        cost_estimate=pl.CostEstimate(
+            flops=12 * flat * width * hidden, bytes_accessed=40 << 20, transcendentals=flat * hidden
+        ),
+    )(xs, gs, g, weight_in, weight_out)
+
+
 def rms_forward(values, norm_gain):
     inverse = lax.rsqrt(jnp.mean(values * values, -1, keepdims=True) + epsilon)
     return (values * inverse * norm_gain, inverse)
@@ -299,6 +548,10 @@
 
 def matmul_nt(left, right):
     return lax.dot_general(left, right, (((1,), (1,)), ((), ())), preferred_element_type=jnp.float32)
+
+
+def pieces(column):
+    return jnp.stack(split3(column), 1)
 
 
 def attention_operands(segment_row, bias_grid):
@@ -353,7 +606,10 @@
     score_scale = head_width ** (-0.5)
     experts_all = router_weight.shape[1]
     capacity = (5 * token_count + 4 * experts_all - 1) // (4 * experts_all)
-    slots = experts_all * capacity
+    slot_rows = (capacity + 15) // 16 * 16
+    slots = experts_all * slot_rows
+    groups = lax.axis_size("expert")
+    dp_size = lax.axis_size("dp")
 
     chosen = routes[:, 0]
     expert_hot = chosen[:, None] == lax.iota(jnp.int32, experts_all)[None, :]
@@ -361,7 +617,7 @@
     before = lax.iota(jnp.int32, token_count)[:, None] > lax.iota(jnp.int32, token_count)[None, :]
     ranks = matmul(before.astype(bf16), expert_hot.astype(bf16))
     slot_rank = jnp.sum(ranks * expert_float, 1).astype(jnp.int32)
-    token_slot = jnp.where(slot_rank < capacity, chosen * capacity + slot_rank, slots)
+    token_slot = jnp.where(slot_rank < capacity, chosen * slot_rows + slot_rank, slots)
     to_slots = (lax.iota(jnp.int32, slots)[:, None] == token_slot[None, :]).astype(bf16)
 
     inputs = tokens.astype(f32)
@@ -384,35 +640,30 @@
     upstream = cotangent.astype(f32)
 
     def exchange(rows):
-        rows = rows.reshape(experts_all, capacity, model_width)
-        rows = lax.all_to_all(rows, "expert", split_axis=0, concat_axis=0, tiled=True)
-        return rows.reshape(slots, model_width)
-
-    arrived = exchange(matmul(to_slots, hidden_two.astype(bf16)).astype(bf16))
-    out_grad_rows = (gate_values[:, None] * upstream).astype(bf16)
-    grad_arrived = exchange(matmul(to_slots, out_grad_rows).astype(bf16))
-    weight_in, weight_out = expert_in[0], expert_out[0]
-    pre_act = matmul(arrived, weight_in)
-    activated = jax.nn.gelu(pre_act, approximate=False).astype(bf16)
-    produced = matmul(activated, weight_out).astype(bf16)
-    returned = exchange(produced)
+        rows = rows.reshape(experts_all, slot_rows, model_width)
+        return lax.all_to_all(rows, "expert", split_axis=0, concat_axis=0, tiled=True)
+
+    grad_arrived = exchange(matmul(to_slots, cotangent).astype(bf16))
+    sent = matmul(to_slots, hidden_two.astype(bf16)).astype(bf16)
+    gate_slots = jnp.sum(matmul(to_slots, pieces(gate_values)), 1)
+    lanes = (slot_rows + LANES - 1) // LANES * LANES
+    gate_slots = jnp.pad(gate_slots.reshape(experts_all, slot_rows), ((0, 0), (0, lanes - slot_rows)))
+    gate_slots = jnp.broadcast_to(gate_slots[:, None, :], (experts_all, 8, lanes))
+    home_grad, home_gate, produced, keep, give = ffn(
+        sent.reshape(experts_all, slot_rows, model_width), gate_slots,
+        grad_arrived.reshape(slots, model_width),
+        expert_in[0], expert_out[0], groups, dp_size,
+    )
+    passed = lax.ppermute(give, "dp", [(i, (i + dp_size // 2) % dp_size) for i in range(dp_size)])
+    weight_grads = keep.astype(f32) + passed.astype(f32)
+    in_weight_grad, out_weight_grad = weight_grads[0], weight_grads[1]
+    returned = exchange(produced).reshape(slots, model_width)
     expert_rows = matmul_tn(to_slots, returned)
     mixed = (middle + gate_values[:, None] * expert_rows).astype(bf16)
-    gate_grad = jnp.sum(upstream * expert_rows, 1)
-
-    act_grad = matmul_nt(grad_arrived, weight_out)
-    _, gelu_pull = jax.vjp(functools.partial(jax.nn.gelu, approximate=False), pre_act)
-    pre_grad = gelu_pull(act_grad)[0].astype(bf16)
-    out_weight_grad = matmul_tn(activated, grad_arrived)
-    in_weight_grad = matmul_tn(arrived, pre_grad)
-    home_grad = exchange(matmul_nt(pre_grad, weight_in).astype(bf16))
-    in_weight_grad = lax.psum_scatter(
-        in_weight_grad.astype(bf16), "dp", scatter_dimension=1, tiled=True
-    ).astype(f32)
-    out_weight_grad = lax.psum_scatter(
-        out_weight_grad.astype(bf16), "dp", scatter_dimension=0, tiled=True
-    ).astype(f32)
-    expert_input_grad = matmul_tn(to_slots, home_grad)
+
+    gate_grad_slots = home_gate[:, 0, :slot_rows].reshape(slots)
+    gate_grad = jnp.sum(matmul_tn(to_slots, pieces(gate_grad_slots)), 1)
+    expert_input_grad = matmul_tn(to_slots, home_grad.reshape(slots, model_width))
     logit_grad = router_probs * (
         expert_float * gate_grad[:, None] - (gate_values * gate_grad)[:, None]
     )

time: 620 us -> 524 us (0.85)
  waiting for transfers between devices: 192 us -> 75.5 us
  matrix products: 174 us -> 73.2 us
  Pallas kernels: 98.1 us -> 197 us
  blocking collectives: 56.9 us -> 78 us
  starting transfers between devices: 28.1 us -> 34.8 us
    all_to_all x4 -> x2, waiting for transfers between devices: 103 us -> 0.01 us  [exchange(): lax.all_to_all(rows, 'expert', split_axis=0, concat_axis=0, tiled=True)]
    pallas_call x0 -> x1, Pallas kernels: none -> 84.2 us  [ffn(): pl.pallas_call(functools.partial(ffn_kernel, groups=groups, dp_size=dp_si...]
    dot_general x9 -> x8, matrix products: 77 us -> 26 us  [matmul(): return jnp.dot(left, right, preferred_element_type=jnp.float32)]
    dot_general x6 -> x4, matrix products: 41.8 us -> 17.6 us  [matmul_nt(): lax.dot_general(left, right, (((1,), (1,)), ((), ())), preferred_element_...]
    dot_general x8 -> x7, matrix products: 40.2 us -> 18.6 us  [matmul_tn(): lax.dot_general(left, right, (((0,), (0,)), ((), ())), preferred_element_...]
    psum x1, blocking collectives: 56.9 us -> 78 us  [per_device(): lax.psum((table_grad, router_grad, attn_gain_grad, ffn_gain_grad), ('dp',...]
    psum x1, waiting for transfers between devices: 89.6 us -> 75.5 us  [per_device(): weights = lax.psum(weights, ('dp', 'expert')).astype(f32)]
    pallas_call x1, Pallas kernels: 67.9 us -> 78.9 us  [attn_bwd(): pl.pallas_call(functools.partial(attn_bwd_kernel, heads=heads, scale=scal...]
  transfers between devices with their start and end apart: 7 -> 4, of which waited for: 4 -> 1; matrix products, arithmetic and copies ran while one was open for 22% -> 15% of each run, Pallas kernels for 0% -> 7%
where the time goes in v2:
time: 524 us; the launch traced here: 518 us
  Pallas kernels  197 us (38%)
  blocking collectives  78 us (15%)
  waiting for transfers between devices  75.5 us (14%)
  matrix products  73.2 us (14%)
  starting transfers between devices  34.8 us (7%)
  local copies, waits for them, and re-layouts  31.4 us (6%)
  between operations  14.7 us (3%)
  other arithmetic  12.8 us (2%)
    pallas_call x1, Pallas kernels, ffn(): pl.pallas_call(functools.partial(ffn_kernel, groups=groups, dp_size=dp_si...  84.2 us
    pallas_call x1, Pallas kernels, attn_bwd(): pl.pallas_call(functools.partial(attn_bwd_kernel, heads=heads, scale=scal...  78.9 us
    psum x1, blocking collectives, per_device(): lax.psum((table_grad, router_grad, attn_gain_grad, ffn_gain_grad), ('dp',...  78 us
    psum x1, waiting for transfers between devices, per_device(): weights = lax.psum(weights, ('dp', 'expert')).astype(f32)  75.5 us
    pallas_call x1, Pallas kernels, attn_fwd(): pl.pallas_call(functools.partial(attn_fwd_kernel, heads=heads), out_shape...  34.3 us
    all_to_all x2, starting transfers between devices, exchange(): lax.all_to_all(rows, 'expert', split_axis=0, concat_axis=0, tiled=True)  33.5 us
    dot_general x8, matrix products, matmul(): return jnp.dot(left, right, preferred_element_type=jnp.float32)  26 us
    unnamed x54, local copies, waits for them, and re-layouts  20.8 us
  transfers between devices with their start and end apart: 4, of which 1 were waited for; matrix products, arithmetic and copies ran while one was open for 15% of the time, Pallas kernels for 7%

profile of v2, /device:TPU:1, one launch (start us, length us, event | category | flops | bytes accessed | tf_op | source)
XLA Modules:
  0.0 517.9 jit_solution(17612648408934502665)
XLA Ops:
  7.2 1.3 fusion.39
  9.2 5.1 fusion.10
  14.3 6.5 %all-to-all-start = ((bf16[8,160,768]{2,1,0:T(8,128)(2,1)}), bf16[8,160,768]{2,1,0:T(8,128)(2,1)}, u32[]{:S(2)}, u32[]{:S(2)}) async-start(bf16[8,160,768]{2,1,0:T(8,128)(2,1)} %bitcast.5), calls=%async_computation | async-start | bytes 3932160 | tf_op jit(solution)/shard_map/all_to_all | solution.py:644
  21.1 0.9 select_convert_fusion.1.qm_ref
  22.0 1.6 copy.56
  24.7 1.7 copy.54
  26.8 4.1 convolution_convert_fusion.2.k_ref
  30.9 2.7 convolution_convert_fusion.1.v_ref
  34.3 0.9 select_convert_fusion.km_ref
  35.2 2.7 fusion.37.q_ref
  38.0 34.3 %shard_map.229 = (bf16[1024,768]{1,0:T(8,128)(2,1)}, bf16[1024,768]{1,0:T(8,128)(2,1)}) custom-call(s32[8]{0:T(128)} %get-tuple-element.102.lo_ref, s32[8]{0:T(128)} %get-tuple-element.101.hi_ref, bf16[1024,768]{1,0:T(8,128)(2,1)} %fusion.37.q_ref, bf16[1024,768]{1,0:T(8,128)(2,1)} %convolution_convert_fusion.2.k_ref, ...), custom_call_target="tpu_custom_call" | custom-call | flops 3221225472 | bytes 7864320 | tf_op jit(solution)/shard_map/pallas_call | solution.py:133
  72.3 3.4 multiply_reduce_fusion.2
  75.7 1.6 copy-done.1
  77.3 2.0 fusion.95
  79.4 1.0 fusion.40
  81.1 5.7 %fusion.9 = bf16[1280,768]{1,0:T(8,128)(2,1)} fusion(s32[1024]{0:T(1024)S(1)} %add_select_fusion, f32[1024,768]{0,1:T(8,128)} %copy-done.1, f32[768]{0:T(1024)S(1)} %copy-done.13, f32[1024]{0:T(1024)S(1)} %add_rsqrt_fusion), kind=kOutput, calls=%fused_computation.18 | convolution fusion | flops 2017918976 | bytes 5123072 | tf_op jit(solution)/shard_map/dot_general | solution.py:542
  87.5 84.2 %shard_map.230 = (bf16[8,160,768]{2,1,0:T(8,128)(2,1)}, f32[8,8,256]{2,1,0:T(8,128)}, bf16[1280,768]{1,0:T(8,128)(2,1)}, bf16[2,768,768]{2,1,0:T(8,128)(2,1)}, bf16[2,768,768]{2,1,0:T(8,128)(2,1)}) custom-call(bf16[8,160,768]{2,1,0:T(8,128)(2,1)} %bitcast.52, f32[8,8,256]{2,1,0:T(8,128)} %broadcast_in_dim.41.gs, bf16[1280,768]{1,0:T(8,128)(2,1)} %bitcast.6.g, ...), custom_call_target="tpu_custom_call" | custom-call | flops 36238786560 | bytes 41943040 | tf_op jit(solution)/shard_map/pallas_call | solution.py:489
  171.7 0.9 slice_reduce_fusion
  172.7 0.9 fusion.41
  173.7 4.0 fusion.1
  177.7 3.5 multiply_reduce_fusion
  181.3 0.9 multiply_add_fusion
  182.7 2.4 convolution_convert_fusion.4
  185.1 2.6 convolution_convert_fusion.do_ref
  187.7 78.9 %shard_map.231 = (bf16[1024,768]{1,0:T(8,128)(2,1)}, bf16[1024,768]{1,0:T(8,128)(2,1)}, bf16[1024,768]{1,0:T(8,128)(2,1)}, f32[60,256]{1,0:T(8,128)}) custom-call(s32[8]{0:T(128)} %get-tuple-element.102.lo_ref, s32[8]{0:T(128)} %get-tuple-element.101.hi_ref, bf16[1024,768]{1,0:T(8,128)(2,1)} %fusion.37.q_ref, ...), custom_call_target="tpu_custom_call" | custom-call | flops 8053063680 | bytes 15728640 | tf_op jit(solution)/shard_map/pallas_call | solution.py:259
  266.7 3.1 convolution_convert_fusion.7
  269.9 1.7 convolution_convert_fusion.6
  271.5 1.7 convolution_convert_fusion.5
  273.2 2.5 pad_maximum_fusion
  275.8 4.8 fusion.97
  280.6 27.0 %all-to-all-start.1 = ((bf16[8,160,768]{2,1,0:T(8,128)(2,1)}), bf16[8,160,768]{2,1,0:T(8,128)(2,1)}, u32[]{:S(2)}, u32[]{:S(2)}) async-start(bf16[8,160,768]{2,1,0:T(8,128)(2,1)} %bitcast.36), calls=%async_computation.1 | async-start | bytes 3932160 | tf_op jit(solution)/shard_map/all_to_all | solution.py:644
  307.6 4.9 fusion.96
  312.5 1.2 collective-permute-start
  313.7 5.3 %fusion.20 = (f32[768]{0:T(1024)S(1)}, f32[1024]{0:T(1024)S(1)}, f32[1024,768]{0,1:T(8,128)S(1)}) fusion(bf16[1024,768]{0,1:T(8,128)(2,1)S(1)} %copy-done.4, f32[1024]{0:T(1024)S(1)} %add_rsqrt_fusion.1, f32[768]{0:T(1024)S(1)} %copy-done.16, bf16[1024,768]{1,0:T(8,128)(2,1)} %get-tuple-element.30, bf16[768,768]{1,0:T(8,128)(2,1)S(1)} %copy-done, ...), kind=kOutput, calls=%fused_computation.29 | convolution fusion | flops 1215035648 | bytes 13776896 | tf_op jit(solution)/shard_map/dot_general | solution.py:550
  319.1 2.1 fusion.16
  321.2 2.6 copy.63
  324.2 4.8 fusion.27
  329.0 78.0 %all-reduce.1 = (f32[768]{0:T(1024)}, f32[768]{0:T(1024)}, f32[32,12]{0,1:T(8,128)}, f32[768,8]{0,1:T(8,128)}) all-reduce(f32[768]{0:T(1024)S(1)} %get-tuple-element.72, f32[768]{0:T(1024)S(1)} %get-tuple-element.70, f32[32,12]{0,1:T(8,128)S(1)} %fusion.44, f32[768,8]{0,1:T(8,128)S(1)} %fusion.27), channel_id=1, replica_groups=mesh['dp'=4,'expert'=8] {'dp','expert'}, use_global_device_ids=true, to_apply=%region_13.14 | all-reduce | flops 8064 | bytes 64512 | tf_op jit(solution)/shard_map/psum | solution.py:699
  407.0 75.5 %all-reduce.4.cloned.1.call-done = bf16[768,3072]{0,1:T(8,128)(2,1)} async-done(((bf16[768,3072]{0,1:T(8,128)(2,1)}), bf16[768,3072]{0,1:T(8,128)(2,1)}) %all-reduce.4.cloned.1.call-update) | async-done | bytes 4718608 | tf_op jit(solution)/shard_map/psum | solution.py:697
  482.5 5.5 %fusion.92 = (f32[768,768]{0,1:T(8,128)}, f32[768,768]{0,1:T(8,128)}, f32[768,768]{0,1:T(8,128)}, f32[768,768]{0,1:T(8,128)S(1)}) fusion(bf16[768,3072]{0,1:T(8,128)(2,1)} %all-reduce.4.cloned.1.call-done), kind=kLoop, calls=%fused_computation.158 | loop fusion | bytes 18874368 | tf_op jit(solution)/shard_map/slice | solution.py:698
  488.0 3.0 copy.67
  491.0 3.0 copy.66
  494.1 3.0 copy.65
  497.1 1.9 copy.64
  499.1 2.9 convert_add_fusion.1
  501.9 2.5 fusion.91
  504.4 4.8 add_convert_fusion
  509.2 1.6 copy.62
  (89 shorter events, 5.7 us)
Async XLA Ops:
  7.2 23.7 %copy-start = (bf16[768,768]{1,0:T(8,128)(2,1)S(1)}, bf16[768,768]{1,0:T(8,128)(2,1)}, u32[]{:S(2)}) copy-start(bf16[768,768]{1,0:T(8,128)(2,1)} %param.22) | copy-start | bytes 3538948
  14.3 6.6 %copy-start.17 = (s32[1,1024]{1,0:T(1,128)S(1)}, s32[1,1024]{1,0:T(1,128)}, u32[]{:S(2)}) copy-start(s32[1,1024]{1,0:T(1,128)} %param.15) | copy-start | bytes 12292
  14.3 7.7 %copy-start.9 = (bf16[1024,768]{1,0:T(8,128)(2,1)S(1)}, bf16[1024,768]{1,0:T(8,128)(2,1)}, u32[]{:S(2)}) copy-start(bf16[1024,768]{1,0:T(8,128)(2,1)} %param.17) | copy-start | bytes 4718596
  14.3 72.6 %all-to-all-start = ((bf16[8,160,768]{2,1,0:T(8,128)(2,1)}), bf16[8,160,768]{2,1,0:T(8,128)(2,1)}, u32[]{:S(2)}, u32[]{:S(2)}) async-start(bf16[8,160,768]{2,1,0:T(8,128)(2,1)} %bitcast.5), calls=%async_computation | async-start | bytes 3932160 | tf_op jit(solution)/shard_map/all_to_all | solution.py:644
  20.8 3.1 copy-start.18
  20.8 461.7 %all-reduce.4.cloned.1.call-start = ((), (), s32[]{:S(2)}) async-start(), calls=%async_computation.2 | async-start | bytes 9437184 | tf_op jit(solution)/shard_map/psum | solution.py:697
  24.7 2.1 copy-start.16
  26.4 45.9 %copy-start.3 = (bf16[1024,768]{0,1:T(8,128)(2,1)}, bf16[1024,768]{0,1:T(8,128)(2,1)S(1)}, u32[]{:S(2)}) copy-start(bf16[1024,768]{0,1:T(8,128)(2,1)S(1)} %copy.54) | copy-start | bytes 4718596
  30.9 4.3 copy-start.20
  72.3 5.0 copy-start.12
  72.3 5.0 copy-start.13
  75.7 1.6 copy-start.1
  75.7 3.6 copy-start.14
  77.3 3.2 copy-start.11
  173.7 4.0 copy-start.2
  177.7 3.6 copy-start.7
  181.3 1.4 copy-start.22
  182.7 2.4 copy-start.5
  182.7 2.4 copy-start.19
  187.7 78.9 %copy-start.4 = (bf16[1024,768]{0,1:T(8,128)(2,1)S(1)}, bf16[1024,768]{0,1:T(8,128)(2,1)}, u32[]{:S(2)}) copy-start(bf16[1024,768]{0,1:T(8,128)(2,1)} %copy-done.3) | copy-start | bytes 4718596
  266.7 3.2 copy-start.21
  269.8 1.7 copy-start.8
  271.5 1.7 copy-start.10
  280.6 223.8 %all-to-all-start.1 = ((bf16[8,160,768]{2,1,0:T(8,128)(2,1)}), bf16[8,160,768]{2,1,0:T(8,128)(2,1)}, u32[]{:S(2)}, u32[]{:S(2)}) async-start(bf16[8,160,768]{2,1,0:T(8,128)(2,1)} %bitcast.36), calls=%async_computation.1 | async-start | bytes 3932160 | tf_op jit(solution)/shard_map/all_to_all | solution.py:644
  307.6 4.9 copy-start.15
  312.5 6.6 %copy-start.6 = (f32[1024,768]{0,1:T(8,128)S(1)}, f32[1024,768]{0,1:T(8,128)}, u32[]{:S(2)}) copy-start(f32[1024,768]{0,1:T(8,128)} %copy-done.5) | copy-start | bytes 9437188
  312.5 186.6 %collective-permute-start = (bf16[2,768,768]{2,1,0:T(8,128)(2,1)}, bf16[2,768,768]{2,1,0:T(8,128)(2,1)}, u32[]{:S(2)}, u32[]{:S(2)}) collective-permute-start(bf16[2,768,768]{2,1,0:T(8,128)(2,1)} %get-tuple-element.33), channel_id=1, source_target_pairs={{0,16},{8,24},{16,0},{24,8},{1,17},{9,25},{17,1},{25,9},{2,18},{10... | collective-permute-start | bytes 7077896 | tf_op jit(solution)/shard_map/ppermute | solution.py:657
Sparse Core Ops, SparseCore 0:
  275.9 206.5 all-reduce.3

commit v3 on v2

--- a/solution.py
+++ b/solution.py
@@ -524,6 +524,225 @@
     )(xs, gs, g, weight_in, weight_out)
 
 
+def fold_steps(rows, cols, bits):
+    steps = []
+    for bit in bits:
+        if rows % 32 == 0:
+            rows = rows // 2
+            steps.append((bit, "rows", rows, cols))
+        elif cols % 256 == 0:
+            cols = cols // 2
+            steps.append((bit, "cols", rows, cols))
+        else:
+            steps.append((bit, "whole", rows, cols))
+    return steps
+
+
+def reduce_kernel(
+    normed, attended, branch, dq, dk, dv, wq, wk, wv, tokens, middle_grad, inverse, gain, small_in,
+    sums, token_grad, small_out,
+    acc, outbox, inbox, small_box, small_sent,
+    ssend, srecv, tsend, trecv,
+    *, dp_bits, expert_bits,
+):
+    f32, bf16 = jnp.float32, jnp.bfloat16
+    dp = lax.axis_index("dp")
+    ex = lax.axis_index("expert")
+    MESH = pl.DeviceIdType.MESH
+    length, width = normed.shape
+
+    def own_bit(bit):
+        axis, place = bit
+        return (dp // 2 ** place) % 2 if axis == "dp" else (ex // 2 ** place) % 2
+
+    def partner(bit):
+        axis, place = bit
+        flip = (1 - 2 * own_bit(bit)) * 2 ** place
+        return (dp + flip, ex) if axis == "dp" else (dp, ex + flip)
+
+    dpb = [("dp", i) for i in range(dp_bits)]
+    exb = [("expert", i) for i in range(expert_bits)]
+    orders = [
+        [dpb[0], dpb[1], exb[0]] + dpb[2:] + exb[1:],
+        [dpb[0], exb[0], dpb[1]] + dpb[2:] + exb[1:],
+    ]
+    every = dpb + exb
+    count = len(every)
+
+    barrier = pltpu.get_barrier_semaphore()
+    for bit in every:
+        pl.semaphore_signal(barrier, inc=1, device_id=partner(bit), device_id_type=MESH)
+    pl.semaphore_wait(barrier, count)
+
+    lefts = (attended, normed, normed, normed)
+    rights = (branch, dv, dk, dq)
+    streams = []
+    for s in range(4):
+        steps = fold_steps(width, width, orders[s % 2])
+        row, col = 0, 0
+        at = 0
+        plan = []
+        for bit, kind, r, c in steps:
+            mine = own_bit(bit)
+            if kind == "rows":
+                keep_at, send_at = (row + mine * r, col), (row + (1 - mine) * r, col)
+            elif kind == "cols":
+                keep_at, send_at = (row, col + mine * c), (row, col + (1 - mine) * c)
+            else:
+                keep_at, send_at = (row, col), (row, col)
+            plan.append((bit, kind, r, c, at, keep_at, send_at))
+            row, col = keep_at
+            at += r
+        streams.append(plan)
+
+    def rs_copy(s, k):
+        bit, kind, r, c, at, _, _ = streams[s][k]
+        return pltpu.make_async_remote_copy(
+            src_ref=outbox.at[s, pl.ds(at, r), pl.ds(0, c)],
+            dst_ref=inbox.at[s, pl.ds(at, r), pl.ds(0, c)],
+            send_sem=ssend.at[s, k], recv_sem=srecv.at[s, k],
+            device_id=partner(bit), device_id_type=MESH)
+
+    def block(s, at, r, c):
+        row, col = at
+        row = pl.multiple_of(row, 16) if not isinstance(row, int) else row
+        col = pl.multiple_of(col, 128) if not isinstance(col, int) else col
+        return sums.at[s, pl.ds(row, r), pl.ds(col, c)]
+
+    def ag_copy(s, k, incoming):
+        bit, kind, r, c, _, keep_at, send_at = streams[s][k]
+        ref = block(s, send_at if incoming else keep_at, r, c)
+        return pltpu.make_async_remote_copy(
+            src_ref=ref, dst_ref=ref,
+            send_sem=ssend.at[s, count + k], recv_sem=srecv.at[s, count + k],
+            device_id=partner(bit), device_id_type=MESH)
+
+    half = width // 2
+    core = own_bit(dpb[0])
+
+    def grad(s, which):
+        span = pl.ds(pl.multiple_of(which * half, half), half)
+        return matmul_tn(lefts[s][:, span], rights[s][...])
+
+    def local(s, k, at):
+        base = streams[s][0][5][0]
+        row, col = at
+        row = row - base
+        row = pl.multiple_of(row, 16) if not isinstance(row, int) else row
+        col = pl.multiple_of(col, 128) if not isinstance(col, int) else col
+        return row, col
+
+    def phase(s, k):
+        plan = streams[s]
+        if k == 0:
+            outbox[s, 0:half, :] = grad(s, 1 - core).astype(bf16)
+            rs_copy(s, 0).start()
+            acc[s] = grad(s, core)
+            return
+        if k <= count:
+            bit, kind, r, c, at, keep_at, _ = plan[k - 1]
+            rs_copy(s, k - 1).wait_recv()
+            row, col = local(s, k - 1, keep_at)
+            view = acc.at[s, pl.ds(row, r), pl.ds(col, c)]
+            own = outbox[s, at : at + r, 0:c].astype(f32) if kind == "whole" else view[...]
+            view[...] = own + inbox[s, at : at + r, 0:c].astype(f32)
+            if k < count:
+                bit, kind, r, c, at, keep_at, send_at = plan[k]
+                row, col = local(s, k, send_at)
+                outbox[s, at : at + r, 0:c] = acc[s, pl.ds(row, r), pl.ds(col, c)].astype(bf16)
+                rs_copy(s, k).start()
+                return
+            block(s, keep_at, r, c)[...] = view[...].astype(bf16)
+        g = 2 * count - 1 - k
+        if k > count:
+            prev = g + 1
+            if plan[prev][1] != "whole":
+                ag_copy(s, prev, True).wait_recv()
+        if g >= 0 and plan[g][1] != "whole":
+            ag_copy(s, g, False).start()
+
+    gain_row = gain[...]
+    rows = 256
+
+    def norm_block(i, gain_grad):
+        span = pl.ds(pl.multiple_of(i * rows, rows), rows)
+        grads = (
+            matmul_nt(dq[span, :], wq[...]) + matmul_nt(dk[span, :], wk[...]) + matmul_nt(dv[span, :], wv[...])
+        )
+        x = tokens[span, :].astype(f32)
+        inv = inverse[span, :]
+        scaled = grads * gain_row
+        mean = jnp.sum(scaled * x, 1, keepdims=True) * (1.0 / width)
+        part = inv * (scaled - x * (inv * inv * mean))
+        token_grad[span, :] = (middle_grad[span, :] + part).astype(bf16)
+        return gain_grad + jnp.sum(grads * (x * inv), 0, keepdims=True)
+
+    def small_copy(k):
+        return pltpu.make_async_remote_copy(
+            src_ref=small_sent.at[k], dst_ref=small_box.at[k],
+            send_sem=tsend.at[k], recv_sem=trecv.at[k],
+            device_id=partner(every[k]), device_id_type=MESH)
+
+    def small_phase(k):
+        if k == 0:
+            gain_grad = lax.fori_loop(0, length // rows, norm_block, jnp.zeros((1, width), f32))
+            small_out[...] = small_in[...]
+            for i in range(width // LANES):
+                small_out[i : i + 1, :] = gain_grad[:, i * LANES : (i + 1) * LANES]
+        else:
+            small_copy(k - 1).wait_recv()
+            small_out[...] = small_out[...] + small_box[k - 1]
+        if k < count:
+            small_sent[k] = small_out[...]
+            small_copy(k).start()
+
+    last = 2 * count
+    for t in range(last + 4):
+        for s in range(4):
+            if 0 <= t - s <= last:
+                phase(s, t - s)
+        if 4 <= t and t - 4 <= count:
+            small_phase(t - 4)
+    for s in range(4):
+        for k in range(count):
+            rs_copy(s, k).wait_send()
+            if streams[s][k][1] != "whole":
+                ag_copy(s, k, False).wait_send()
+    for k in range(count):
+        small_copy(k).wait_send()
+
+
+def reduce_grads(normed, attended, branch, dq, dk, dv, wq, wk, wv, tokens, middle_grad, inverse, gain, small, dp_size, groups):
+    f32, bf16 = jnp.float32, jnp.bfloat16
+    length, width = normed.shape
+    dp_bits, expert_bits = dp_size.bit_length() - 1, groups.bit_length() - 1
+    count = dp_bits + expert_bits
+    box = sum(step[2] for step in fold_steps(width, width, range(count)))
+    vmem = pl.BlockSpec(memory_space=pltpu.VMEM)
+    sem = pltpu.SemaphoreType.DMA
+    shape = jax.ShapeDtypeStruct
+    return pl.pallas_call(
+        functools.partial(reduce_kernel, dp_bits=dp_bits, expert_bits=expert_bits),
+        out_shape=(shape((4, width, width), bf16), shape((length, width), bf16), shape(small.shape, f32)),
+        in_specs=[vmem] * 14,
+        out_specs=(vmem,) * 3,
+        scratch_shapes=[
+            pltpu.VMEM((4, width // 2, width), f32),
+            pltpu.VMEM((4, box, width), bf16),
+            pltpu.VMEM((4, box, width), bf16),
+            pltpu.VMEM((count,) + small.shape, f32),
+            pltpu.VMEM((count,) + small.shape, f32),
+            sem((4, 2 * count)), sem((4, 2 * count)), sem((count,)), sem((count,)),
+        ],
+        compiler_params=pltpu.CompilerParams(
+            collective_id=2, has_side_effects=True, vmem_limit_bytes=62 << 20
+        ),
+        cost_estimate=pl.CostEstimate(
+            flops=14 * length * width * width, bytes_accessed=30 << 20, transcendentals=0
+        ),
+    )(normed, attended, branch, dq, dk, dv, wq, wk, wv, tokens, middle_grad, inverse, gain, small)
+
+
 def rms_forward(values, norm_gain):
     inverse = lax.rsqrt(jnp.mean(values * values, -1, keepdims=True) + epsilon)
     return (values * inverse * norm_gain, inverse)
@@ -674,37 +893,38 @@
     middle_part, ffn_gain_grad = rms_backward(middle, inverse_two, ffn_gain, hidden_grad)
     middle_grad = upstream + middle_part
     branch_grad = middle_grad.astype(bf16)
-    output_weight_grad = matmul_tn(attended, branch_grad)
     attended_grad = matmul_nt(branch_grad, output_weight).astype(bf16)
     query_grad, key_grad, value_grad, diag_sums = attn_bwd(
         lo, hi, queries, key_rows, value_rows, query_extra, attended_grad, attended, key_mask,
         diag, score_scale,
     )
     table_grad = bias_grad(diag_sums, head_count, bucket_count)
-    query_weight_grad = matmul_tn(normed_low, query_grad)
-    key_weight_grad = matmul_tn(normed_low, key_grad)
-    value_weight_grad = matmul_tn(normed_low, value_grad)
-    normed_grad = (
-        matmul_nt(query_grad, query_weight)
-        + matmul_nt(key_grad, key_weight)
-        + matmul_nt(value_grad, value_weight)
-    )
-    input_part, attn_gain_grad = rms_backward(inputs, inverse_one, attn_gain, normed_grad)
-    token_grad = (middle_grad + input_part).astype(bf16)
-    weights = jnp.concatenate(
-        [query_weight_grad, key_weight_grad, value_weight_grad, output_weight_grad], 1
-    ).astype(bf16)
-    weights = lax.psum(weights, ("dp", "expert")).astype(f32)
-    weights = [weights[:, i * model_width : (i + 1) * model_width] for i in range(4)]
-    small = lax.psum((table_grad, router_grad, attn_gain_grad, ffn_gain_grad), ("dp", "expert"))
+    flat = jnp.concatenate(
+        [jnp.zeros((model_width,), f32), ffn_gain_grad, table_grad.reshape(-1), router_grad.reshape(-1)]
+    )
+    small_rows = -(-flat.shape[0] // (8 * LANES)) * 8
+    small = jnp.pad(flat, (0, small_rows * LANES - flat.shape[0])).reshape(small_rows, LANES)
+    weights, token_grad, small = reduce_grads(
+        normed_low, attended, branch_grad, query_grad, key_grad, value_grad,
+        query_weight, key_weight, value_weight, tokens, middle_grad, inverse_one,
+        attn_gain[None, :], small, dp_size, groups,
+    )
+    weights = weights.astype(f32)
+    flat = small.reshape(-1)
+    ends = [model_width, 2 * model_width]
+    ends.append(ends[-1] + table_grad.size)
+    ends.append(ends[-1] + router_grad.size)
     return (
         mixed,
         token_grad,
-        small[2],
-        small[3],
-        *weights,
-        small[0],
-        small[1],
+        flat[: ends[0]],
+        flat[ends[0] : ends[1]],
+        weights[3],
+        weights[2],
+        weights[1],
+        weights[0],
+        flat[ends[1] : ends[2]].reshape(table_grad.shape),
+        flat[ends[2] : ends[3]].reshape(router_grad.shape),
         in_weight_grad[None],
         out_weight_grad[None],
     )

time: 524 us -> 436 us (0.83)
  Pallas kernels: 197 us -> 303 us
  blocking collectives: 78 us -> 0 us
  waiting for transfers between devices: 75.5 us -> 0.01 us
  matrix products: 73.2 us -> 54.2 us
  between operations: 14.7 us -> 1.16 us
  local copies, waits for them, and re-layouts: 31.4 us -> 19.1 us
    pallas_call x0 -> x1, Pallas kernels: none -> 106 us  [reduce_grads(): pl.pallas_call(functools.partial(reduce_kernel, dp_bits=dp_bits, expert_b...]
    psum x1 -> x0, blocking collectives: 78 us -> none  [per_device(): lax.psum((table_grad, router_grad, attn_gain_grad, ffn_gain_grad), ('dp',...]
    psum x1 -> x0, waiting for transfers between devices: 75.5 us -> none  [per_device(): weights = lax.psum(weights, ('dp', 'expert')).astype(f32)]
    unnamed x54 -> x39, local copies, waits for them, and re-layouts: 20.8 us -> 4.28 us
    dot_general x4 -> x1, matrix products: 17.6 us -> 2.57 us  [matmul_nt(): lax.dot_general(left, right, (((1,), (1,)), ((), ())), preferred_element_...]
    ppermute x1, starting transfers between devices: 1.25 us -> 11.1 us  [per_device(): lax.ppermute(give, 'dp', [(i, (i + dp_size // 2) % dp_size) for i in rang...]
    all_to_all x2, starting transfers between devices: 33.5 us -> 23.9 us  [exchange(): lax.all_to_all(rows, 'expert', split_axis=0, concat_axis=0, tiled=True)]
    dot_general x7 -> x3, matrix products: 18.6 us -> 11.4 us  [matmul_tn(): lax.dot_general(left, right, (((0,), (0,)), ((), ())), preferred_element_...]
  transfers between devices with their start and end apart: 4 -> 3, of which waited for: 1 -> 0; matrix products, arithmetic and copies ran while one was open for 15% -> 17% of each run, Pallas kernels for 7% -> 51%
where the time goes in v3:
time: 436 us; the launch traced here: 428 us
  Pallas kernels  303 us (69%)
  matrix products  54.2 us (12%)
  starting transfers between devices  35 us (8%)
  local copies, waits for them, and re-layouts  19.1 us (4%)
  other arithmetic  15.2 us (3%)
    pallas_call x1, Pallas kernels, reduce_grads(): pl.pallas_call(functools.partial(reduce_kernel, dp_bits=dp_bits, expert_b...  106 us
    pallas_call x1, Pallas kernels, ffn(): pl.pallas_call(functools.partial(ffn_kernel, groups=groups, dp_size=dp_si...  84 us
    pallas_call x1, Pallas kernels, attn_bwd(): pl.pallas_call(functools.partial(attn_bwd_kernel, heads=heads, scale=scal...  78.8 us
    pallas_call x1, Pallas kernels, attn_fwd(): pl.pallas_call(functools.partial(attn_fwd_kernel, heads=heads), out_shape...  34.3 us
    dot_general x8, matrix products, matmul(): return jnp.dot(left, right, preferred_element_type=jnp.float32)  25.6 us
    all_to_all x2, starting transfers between devices, exchange(): lax.all_to_all(rows, 'expert', split_axis=0, concat_axis=0, tiled=True)  23.9 us
    dot_general x3, matrix products, matmul_tn(): lax.dot_general(left, right, (((0,), (0,)), ((), ())), preferred_element_...  11.4 us
    ppermute x1, starting transfers between devices, per_device(): lax.ppermute(give, 'dp', [(i, (i + dp_size // 2) % dp_size) for i in rang...  11.1 us
  transfers between devices with their start and end apart: 3, of which 0 were waited for; matrix products, arithmetic and copies ran while one was open for 17% of the time, Pallas kernels for 51%

profile of v3, /device:TPU:1, one launch (start us, length us, event | category | flops | bytes accessed | tf_op | source)
XLA Modules:
  0.0 427.6 jit_solution(5650611032501142292)
XLA Ops:
  0.7 1.3 fusion.30
  1.9 0.7 add_select_fusion
  2.6 5.1 %fusion.8 = bf16[1280,768]{1,0:T(8,128)(2,1)} fusion(bf16[1024,768]{1,0:T(8,128)(2,1)} %param.17, s32[1024]{0:T(1024)S(1)} %add_select_fusion), kind=kOutput, calls=%fused_computation.14 | convolution fusion | flops 2015559680 | bytes 3543040 | tf_op jit(solution)/shard_map/dot_general | solution.py:761
  7.7 6.5 %all-to-all-start = ((bf16[8,160,768]{2,1,0:T(8,128)(2,1)}), bf16[8,160,768]{2,1,0:T(8,128)(2,1)}, u32[]{:S(2)}, u32[]{:S(2)}) async-start(bf16[8,160,768]{2,1,0:T(8,128)(2,1)} %bitcast.46), calls=%async_computation | async-start | bytes 3932160 | tf_op jit(solution)/shard_map/all_to_all | solution.py:863
  14.5 0.9 select_convert_fusion.1.qm_ref
  15.6 0.6 broadcast_in_dim.47.gain
  16.9 0.6 fusion.79
  17.5 1.6 fusion.11.normed
  19.0 1.0 copy.38.inverse
  20.3 0.5 and_select_fusion.1
  20.8 0.9 select_convert_fusion.km_ref
  21.7 4.4 %convolution_convert_fusion.1.v_ref = bf16[1024,768]{1,0:T(8,128)(2,1)} fusion(bf16[1024,768]{1,0:T(8,128)(2,1)} %fusion.11.normed, bf16[768,768]{1,0:T(8,128)(2,1)} %wv.1), kind=kOutput, calls=%fused_computation.39 | convolution fusion | flops 1208745984 | bytes 4325376 | tf_op jit(solution)/shard_map/dot_general | solution.py:761
  26.2 2.5 convolution_convert_fusion.2.k_ref
  28.7 2.5 fusion.28.q_ref
  31.2 34.3 %shard_map.229 = (bf16[1024,768]{1,0:T(8,128)(2,1)}, bf16[1024,768]{1,0:T(8,128)(2,1)}) custom-call(s32[8]{0:T(128)} %get-tuple-element.105.lo_ref, s32[8]{0:T(128)} %get-tuple-element.104.hi_ref, bf16[1024,768]{1,0:T(8,128)(2,1)} %fusion.28.q_ref, bf16[1024,768]{1,0:T(8,128)(2,1)} %convolution_convert_fusion.2.k_ref, ...), custom_call_target="tpu_custom_call" | custom-call | flops 3221225472 | bytes 7864320 | tf_op jit(solution)/shard_map/pallas_call | solution.py:133
  65.5 2.9 multiply_reduce_fusion.2
  68.5 1.6 copy-done.1
  70.2 3.0 fusion.81
  73.3 1.0 fusion.31
  74.4 0.6 pad_maximum_fusion.diag_ref
  75.0 5.8 %fusion.7 = bf16[1280,768]{1,0:T(8,128)(2,1)} fusion(s32[1024]{0:T(1024)S(1)} %add_select_fusion, f32[1024,768]{1,0:T(8,128)} %copy-done.1, f32[768]{0:T(1024)S(1)} %copy-done.11, f32[1024]{0:T(1024)S(1)} %add_rsqrt_fusion), kind=kOutput, calls=%fused_computation.13 | convolution fusion | flops 2017918976 | bytes 5123072 | tf_op jit(solution)/shard_map/dot_general | solution.py:761
  80.8 0.6 broadcast_in_dim.46.gs
  81.4 84.0 %shard_map.230 = (bf16[8,160,768]{2,1,0:T(8,128)(2,1)}, f32[8,8,256]{2,1,0:T(8,128)}, bf16[1280,768]{1,0:T(8,128)(2,1)}, bf16[2,768,768]{2,1,0:T(8,128)(2,1)}, bf16[2,768,768]{2,1,0:T(8,128)(2,1)}) custom-call(bf16[8,160,768]{2,1,0:T(8,128)(2,1)} %bitcast.63, f32[8,8,256]{2,1,0:T(8,128)} %broadcast_in_dim.46.gs, bf16[1280,768]{1,0:T(8,128)(2,1)} %bitcast.6.g, ...), custom_call_target="tpu_custom_call" | custom-call | flops 36238786560 | bytes 41943040 | tf_op jit(solution)/shard_map/pallas_call | solution.py:489
  165.4 0.9 slice_reduce_fusion
  166.4 17.4 %all-to-all-start.1 = ((bf16[8,160,768]{2,1,0:T(8,128)(2,1)}), bf16[8,160,768]{2,1,0:T(8,128)(2,1)}, u32[]{:S(2)}, u32[]{:S(2)}) async-start(bf16[8,160,768]{2,1,0:T(8,128)(2,1)} %bitcast.45), calls=%async_computation.1 | async-start | bytes 3932160 | tf_op jit(solution)/shard_map/all_to_all | solution.py:863
  183.7 0.9 fusion.32
  184.7 7.1 %fusion.18 = f32[768,8]{1,0:T(8,128)S(1)} fusion(f32[1024,768]{1,0:T(8,128)} %copy-done.1, f32[768]{0:T(1024)S(1)} %copy-done.11, f32[1024]{0:T(1024)S(1)} %add_rsqrt_fusion, f32[1024]{0:T(1024)S(1)} %mul.157, f32[1024]{0:T(1024)S(1)} %fusion.32, s32[1024]{0:T(1024)S(1)} %bitcast.50, f32[1024,8]{0,1:T(8,128)S(1)} %get-tuple-element.102, ...), kind=kOutput, calls=%fused_computation.30 | convolution fusion | flops 77119488 | bytes 3230720 | tf_op jit(solution)/shard_map/dot_general | solution.py:889
  192.0 4.3 fusion.1
  196.3 3.7 multiply_reduce_fusion
  200.0 3.1 fusion.77
  203.1 2.6 convolution_convert_fusion.do_ref
  205.7 11.1 %collective-permute-start = (bf16[2,768,768]{2,1,0:T(8,128)(2,1)}, bf16[2,768,768]{2,1,0:T(8,128)(2,1)}, u32[]{:S(2)}, u32[]{:S(2)}) collective-permute-start(bf16[2,768,768]{2,1,0:T(8,128)(2,1)} %get-tuple-element.39), channel_id=1, source_target_pairs={{0,16},{8,24},{16,0},{24,8},{1,17},{9,25},{17,1},{25,9},{2,18},{10... | collective-permute-start | bytes 7077896 | tf_op jit(solution)/shard_map/ppermute | solution.py:876
  216.8 78.8 %shard_map.231 = (bf16[1024,768]{1,0:T(8,128)(2,1)}, bf16[1024,768]{1,0:T(8,128)(2,1)}, bf16[1024,768]{1,0:T(8,128)(2,1)}, f32[60,256]{1,0:T(8,128)}) custom-call(s32[8]{0:T(128)} %get-tuple-element.105.lo_ref, s32[8]{0:T(128)} %get-tuple-element.104.hi_ref, bf16[1024,768]{1,0:T(8,128)(2,1)} %fusion.28.q_ref, ...), custom_call_target="tpu_custom_call" | custom-call | flops 8053063680 | bytes 15728640 | tf_op jit(solution)/shard_map/pallas_call | solution.py:259
  295.6 0.9 reshape.353
  296.5 0.7 fusion.34
  297.3 0.6 fusion.38.small_in
  298.0 105.8 %shard_map.232 = (bf16[4,768,768]{2,1,0:T(8,128)(2,1)}, bf16[1024,768]{1,0:T(8,128)(2,1)}, f32[64,128]{1,0:T(8,128)}) custom-call(bf16[1024,768]{1,0:T(8,128)(2,1)} %fusion.11.normed, bf16[1024,768]{1,0:T(8,128)(2,1)} %get-tuple-element.26.o_ref.attended, bf16[1024,768]{1,0:T(8,128)(2,1)} %copy-done.6, bf16[1024,768]{1,0:T(8,128)(2,1)} %get-tuple-element.31.dq, ...), custom_call_target="tpu_custom_call" | custom-call | flops 8455716864 | bytes 31457280 | tf_op jit(solution)/shard_map/pallas_call | solution.py:724
  403.8 0.7 slice.66
  404.4 0.8 slice.67
  405.3 0.7 copy.39
  406.2 0.7 copy.40
  407.0 3.2 convert_element_type.360
  410.1 1.4 slice_bitcast_fusion.4
  411.5 3.8 slice_bitcast_fusion
  415.3 2.3 convert_add_fusion.1
  417.6 2.5 fusion.78
  420.1 6.2 %add_convert_fusion = bf16[1024,768]{1,0:T(8,128)(2,1)} fusion(f32[1024,768]{1,0:T(8,128)} %copy-done.1, f32[1024]{0:T(1024)S(1)} %select_reduce_fusion, bf16[1280,768]{1,0:T(8,128)(2,1)} %bitcast.10, s32[1024]{0:T(1024)S(1)} %add_select_fusion), kind=kOutput, calls=%fused_computation.21 | convolution fusion | flops 2016935936 | bytes 6692864 | tf_op jit(solution)/shard_map/dot_general | solution.py:765
  426.3 1.1 copy.45
  (74 shorter events, 2.2 us)
Async XLA Ops:
  0.6 64.9 %copy-start = (bf16[768,768]{1,0:T(8,128)(2,1)S(1)}, bf16[768,768]{1,0:T(8,128)(2,1)}, u32[]{:S(2)}) copy-start(bf16[768,768]{1,0:T(8,128)(2,1)} %param.23) | copy-start | bytes 3538948
  7.7 6.5 %copy-start.13 = (s32[1,1024]{1,0:T(1,128)S(1)}, s32[1,1024]{1,0:T(1,128)}, u32[]{:S(2)}) copy-start(s32[1,1024]{1,0:T(1,128)} %param.15) | copy-start | bytes 12292
  7.7 7.9 %copy-start.14 = (f32[768]{0:T(1024)S(1)}, f32[768]{0:T(1024)}, u32[]{:S(2)}) copy-start(f32[768]{0:T(1024)} %param.18) | copy-start | bytes 9220
  7.7 8.4 %copy-start.3 = (bf16[1024,768]{1,0:T(8,128)(2,1)S(1)}, bf16[1024,768]{1,0:T(8,128)(2,1)}, u32[]{:S(2)}) copy-start(bf16[1024,768]{1,0:T(8,128)(2,1)} %tokens.1) | copy-start | bytes 4718596
  7.7 8.9 %copy-start.15 = (f32[32,12]{0,1:T(8,128)S(1)}, f32[32,12]{0,1:T(8,128)}, u32[]{:S(2)}) copy-start(f32[32,12]{0,1:T(8,128)} %param.24) | copy-start | bytes 4612
  7.7 73.1 %all-to-all-start = ((bf16[8,160,768]{2,1,0:T(8,128)(2,1)}), bf16[8,160,768]{2,1,0:T(8,128)(2,1)}, u32[]{:S(2)}, u32[]{:S(2)}) async-start(bf16[8,160,768]{2,1,0:T(8,128)(2,1)} %bitcast.46), calls=%async_computation | async-start | bytes 3932160 | tf_op jit(solution)/shard_map/all_to_all | solution.py:863
  21.7 4.4 %copy-start.7 = (bf16[1024,768]{1,0:T(8,128)(2,1)S(1)}, bf16[1024,768]{1,0:T(8,128)(2,1)}, u32[]{:S(2)}) copy-start(bf16[1024,768]{1,0:T(8,128)(2,1)} %fusion.11.normed) | copy-start | bytes 4718596
  21.7 4.4 %copy-start.17 = (bf16[768,768]{1,0:T(8,128)(2,1)S(1)}, bf16[768,768]{1,0:T(8,128)(2,1)}, u32[]{:S(2)}) copy-start(bf16[768,768]{1,0:T(8,128)(2,1)} %wk.1) | copy-start | bytes 3538948
  26.1 2.5 copy-start.16
  65.5 4.6 %copy-start.10 = (f32[768,8]{0,1:T(8,128)S(1)}, f32[768,8]{0,1:T(8,128)}, u32[]{:S(2)}) copy-start(f32[768,8]{0,1:T(8,128)} %param.25) | copy-start | bytes 73732
  65.5 4.6 %copy-start.11 = (f32[768]{0:T(1024)S(1)}, f32[768]{0:T(1024)}, u32[]{:S(2)}) copy-start(f32[768]{0:T(1024)} %param.19) | copy-start | bytes 9220
  68.5 1.7 copy-start.1
  68.5 4.7 %copy-start.12 = (s32[1024,1]{0,1:T(1,128)S(1)}, s32[1024,1]{0,1:T(1,128)}, u32[]{:S(2)}) copy-start(s32[1024,1]{0,1:T(1,128)} %param.16) | copy-start | bytes 12292
  70.2 4.2 copy-start.9
  166.4 253.7 %all-to-all-start.1 = ((bf16[8,160,768]{2,1,0:T(8,128)(2,1)}), bf16[8,160,768]{2,1,0:T(8,128)(2,1)}, u32[]{:S(2)}, u32[]{:S(2)}) async-start(bf16[8,160,768]{2,1,0:T(8,128)(2,1)} %bitcast.45), calls=%async_computation.1 | async-start | bytes 3932160 | tf_op jit(solution)/shard_map/all_to_all | solution.py:863
  192.0 4.3 %copy-start.2 = (f32[1024,768]{1,0:T(8,128)S(1)}, f32[1024,768]{1,0:T(8,128)}, u32[]{:S(2)}) copy-start(f32[1024,768]{1,0:T(8,128)} %copy-done.1) | copy-start | bytes 9437188
  196.3 3.7 copy-start.5
  203.1 2.6 copy-start.6
  205.7 209.6 %collective-permute-start = (bf16[2,768,768]{2,1,0:T(8,128)(2,1)}, bf16[2,768,768]{2,1,0:T(8,128)(2,1)}, u32[]{:S(2)}, u32[]{:S(2)}) collective-permute-start(bf16[2,768,768]{2,1,0:T(8,128)(2,1)} %get-tuple-element.39), channel_id=1, source_target_pairs={{0,16},{8,24},{16,0},{24,8},{1,17},{9,25},{17,1},{25,9},{2,18},{10... | collective-permute-start | bytes 7077896 | tf_op jit(solution)/shard_map/ppermute | solution.py:876
  411.5 3.8 copy-start.4
  420.1 6.2 %copy-start.8 = (bf16[1024,768]{1,0:T(8,128)(2,1)S(1)}, bf16[1024,768]{1,0:T(8,128)(2,1)}, u32[]{:S(2)}) copy-start(bf16[1024,768]{1,0:T(8,128)(2,1)} %get-tuple-element.123) | copy-start | bytes 4718596

commit v4 on v3

v4 whole, which is shorter than its diff:
```python
import functools

import jax
import jax.numpy as jnp
from jax import lax
from jax.experimental import pallas as pl
from jax.experimental.pallas import tpu as pltpu
from jax.sharding import PartitionSpec as P

epsilon = 1e-06
precise_setting = lax.Precision.HIGHEST
def matmul(left, right):
    return jnp.dot(left, right, preferred_element_type=jnp.float32)


def matmul_tn(left, right):
    return lax.dot_general(left, right, (((0,), (0,)), ((), ())), preferred_element_type=jnp.float32)


def matmul_nt(left, right):
    return lax.dot_general(left, right, (((1,), (1,)), ((), ())), preferred_element_type=jnp.float32)


bucket_bounds = (12, 16, 23, 32, 46, 64, 91)
masked_score = -1e30
LANES = 128
BLOCK = 128
NEAR = 5
UF = 6
UB = 6


def bucket_of(relative):
    distance = jnp.abs(relative)
    beyond = jnp.zeros_like(distance)
    for threshold in bucket_bounds:
        beyond = beyond + (distance >= threshold).astype(jnp.int32)
    inside = jnp.where(distance < 8, distance, 8 + beyond)
    return inside + 16 * (relative > 0).astype(jnp.int32)


def dot_nt(a, b):
    return lax.dot_general(a, b, (((1,), (1,)), ((), ())), preferred_element_type=jnp.float32)


def dot_nn(a, b):
    return lax.dot_general(a, b, (((1,), (0,)), ((), ())), preferred_element_type=jnp.float32)


def split3(x):
    a = x.astype(jnp.bfloat16)
    r = x - a.astype(jnp.float32)
    b = r.astype(jnp.bfloat16)
    c = (r - b.astype(jnp.float32)).astype(jnp.bfloat16)
    return a, b, c


def fill_bias(diag_ref, bias, pairs):
    for p in range(pairs):
        for d in range(NEAR):
            tiles = []
            for h in (2 * p, 2 * p + 1):
                row = diag_ref[h : h + 1, :]
                if d in (0, NEAR - 1):
                    col = row[:, 511:512] if d == 0 else row[:, 0:1]
                    tiles.append(jnp.broadcast_to(col, (BLOCK, BLOCK)))
                else:
                    base = (3 - d) * BLOCK
                    wide = jnp.broadcast_to(row[:, base : base + 2 * BLOCK], (BLOCK, 2 * BLOCK))
                    tiles.append(pltpu.roll(wide, BLOCK, 1, stride=1, stride_axis=0)[:, :BLOCK])
            bias[p, d] = jnp.concatenate(tiles, 1)


def heads_apart(block, low, extra=None):
    zero = jnp.zeros_like(block)
    first, second = jnp.where(low, block, zero), jnp.where(low, zero, block)
    if extra is not None:
        first, second = jnp.concatenate([first, extra], 1), jnp.concatenate([second, extra], 1)
    return jnp.concatenate([first, second], 0)


def by_count(lo, hi, most, body):
    for n in range(1, most + 1):
        pl.when(hi - lo == n)(functools.partial(body, n))


def own_heads(wide):
    return jnp.concatenate([wide[:64, :LANES], wide[64:128, LANES:]], 0)


def attend(lo_ref, hi_ref, q_ref, k_ref, vt_ref, qm_ref, km_ref, bias, o_ref, lse_ref):
    pairs = q_ref.shape[1] // LANES
    length = q_ref.shape[0]
    nblk = length // BLOCK
    f32, bf16 = jnp.float32, jnp.bfloat16
    low = lax.broadcasted_iota(jnp.int32, (1, LANES), 1) < 64

    def q_block(i, _):
        lo, hi = lo_ref[i], hi_ref[i]
        rows = pl.ds(pl.multiple_of(i * BLOCK, BLOCK), BLOCK)
        start = pl.multiple_of(lo * BLOCK, BLOCK)
        qm = qm_ref[rows, :]

        def body(n):
            span = pl.ds(start, n * BLOCK)
            km = km_ref[span, :]

            def lanes_of(p):
                return pl.ds(pl.multiple_of(p * LANES, LANES), LANES)

            def scores(p):
                qs = heads_apart(q_ref[rows, lanes_of(p)], low, qm)
                return dot_nt(jnp.concatenate([k_ref[span, lanes_of(p)], km], 1), qs)

            def soften(p, st):
                parts = []
                top = None
                for b in range(n):
                    d = jnp.clip(lo + b - i, -2, 2) + 2
                    s = st[b * BLOCK : (b + 1) * BLOCK] + bias[p, d]
                    parts.append(s)
                    top = s if top is None else jnp.maximum(top, s)
                top = jnp.max(top, 0, keepdims=True)
                return jnp.concatenate([jnp.exp(s - top).astype(bf16) for s in parts], 0), top

            def mix(p, probs):
                values = jnp.concatenate([vt_ref[lanes_of(p), span], jnp.ones((16, n * BLOCK), bf16)], 0)
                return dot_nn(values, probs)

            def finish(p, acc, top):
                total = acc[LANES : LANES + 1]
                inv = 1.0 / total
                ot = own_heads(acc)
                ot = jnp.concatenate([ot[:64] * inv[:, :LANES], ot[64:] * inv[:, LANES:]], 0)
                o_ref[rows, lanes_of(p)] = ot.T.astype(bf16)
                lse_ref[i, pl.ds(p, 1), :] = top + jnp.log(total)

            def some(g, _):
                ps = [g * UF + u for u in range(UF)]
                sts = [scores(p) for p in ps]
                soft = [soften(p, st) for p, st in zip(ps, sts)]
                accs = [mix(p, x[0]) for p, x in zip(ps, soft)]
                for p, acc, x in zip(ps, accs, soft):
                    finish(p, acc, x[1])
                return 0
            lax.fori_loop(0, pairs // UF, some, 0)

        by_count(lo, hi, nblk, body)
        return 0
    lax.fori_loop(0, nblk, q_block, 0)


def attend_back(
    lo_ref, hi_ref, q_ref, k_ref, kt_ref, v_ref, lse_ref, do_ref, o_ref, qm_ref, km_ref, bias,
    dq_ref, dk_ref, dv_ref, gsum_ref, gacc, dkacc, dvacc, scale,
):
    length, width = q_ref.shape
    pairs = width // LANES
    nblk = length // BLOCK
    f32, bf16 = jnp.float32, jnp.bfloat16
    low = lax.broadcasted_iota(jnp.int32, (1, LANES), 1) < 64
    pick = (
        lax.broadcasted_iota(jnp.int32, (16, LANES), 0) == lax.broadcasted_iota(jnp.int32, (16, LANES), 1) // 64
    ).astype(f32).astype(bf16)
    gacc[...] = jnp.zeros_like(gacc)
    dkacc[...] = jnp.zeros_like(dkacc)
    dvacc[...] = jnp.zeros_like(dvacc)

    def q_block(i, _):
        lo, hi = lo_ref[i], hi_ref[i]
        rows = pl.ds(pl.multiple_of(i * BLOCK, BLOCK), BLOCK)
        start = pl.multiple_of(lo * BLOCK, BLOCK)
        qm = qm_ref[rows, :]

        def body(n):
            span = pl.ds(start, n * BLOCK)
            km = km_ref[span, :]

            def lanes_of(p):
                return pl.ds(pl.multiple_of(p * LANES, LANES), LANES)

            def products(p):
                cols = lanes_of(p)
                qs = heads_apart(q_ref[rows, cols], low, qm)
                dd = do_ref[rows, cols]
                dos = heads_apart(dd, low)
                prod = dd.astype(f32) * o_ref[rows, cols].astype(f32)
                prod_hi = prod.astype(bf16)
                prod_lo = (prod - prod_hi.astype(f32)).astype(bf16)
                inner = dot_nt(pick, prod_hi) + dot_nt(pick, prod_lo)
                inner = jnp.concatenate([inner[0:1], inner[1:2]], 1)
                st = dot_nt(jnp.concatenate([k_ref[span, cols], km], 1), qs)
                dpt = dot_nt(v_ref[span, cols], dos)
                return qs, dos, inner, st, dpt

            def pointwise(p, inner, st, dpt):
                lse = lse_ref[i, pl.ds(p, 1), :]
                probs, grads = [], []
                for b in range(n):
                    d = jnp.clip(lo + b - i, -2, 2) + 2
                    part = slice(b * BLOCK, (b + 1) * BLOCK)
                    prob = jnp.exp(st[part] + bias[p, d] - lse)
                    grad = prob * (dpt[part] - inner)
                    gacc[p, d] += grad
                    probs.append(prob.astype(bf16))
                    grads.append(grad.astype(bf16))
                return jnp.concatenate(probs, 0), jnp.concatenate(grads, 0)

            def back(p, qs, dos, probs, grads):
                cols = lanes_of(p)
                return (
                    dot_nn(probs, dos), dot_nn(grads, qs[:, :LANES]), dot_nn(kt_ref[cols, span], grads)
                )

            def finish(p, dv, dk, dqt):
                cols = lanes_of(p)
                dvacc[span, cols] += dv
                dkacc[span, cols] += dk
                dq_ref[rows, cols] = (own_heads(dqt).T * scale).astype(bf16)

            def some(g, _):
                ps = [g * UB + u for u in range(UB)]
                first = [products(p) for p in ps]
                points = [pointwise(p, *x[2:]) for p, x in zip(ps, first)]
                last = [back(p, *x[:2], *y) for p, x, y in zip(ps, first, points)]
                for p, x in zip(ps, last):
                    finish(p, *x)
                return 0
            lax.fori_loop(0, pairs // UB, some, 0)

        by_count(lo, hi, nblk, body)
        return 0
    lax.fori_loop(0, nblk, q_block, 0)
    dk_ref[...] = dkacc[...].astype(bf16)
    dv_ref[...] = dvacc[...].astype(bf16)
    turn = (
        lax.broadcasted_iota(jnp.int32, (BLOCK, BLOCK), 0) + lax.broadcasted_iota(jnp.int32, (BLOCK, BLOCK), 1)
        == BLOCK - 1
    ).astype(f32).astype(bf16)
    for p in range(pairs):
        for d in range(NEAR):
            t = gacc[p, d]
            if 0 < d < NEAR - 1:
                hi = t.astype(bf16)
                t = dot_nn(turn, hi) + dot_nn(turn, (t - hi.astype(f32)).astype(bf16))
            for u in range(2):
                s = jnp.concatenate([t[:, u * LANES : (u + 1) * LANES], jnp.zeros((BLOCK, LANES), f32)], 1)
                if 0 < d < NEAR - 1:
                    s = pltpu.roll(s, 0, 1, stride=1, stride_axis=0)
                at = (2 * p + u) * NEAR + d
                gsum_ref[at : at + 1, :] = jnp.sum(s, 0, keepdims=True)


def two(x):
    a = x.astype(jnp.bfloat16)
    return a, (x - a.astype(jnp.float32)).astype(jnp.bfloat16)


def row_pieces(row):
    place = lax.broadcasted_iota(jnp.int32, (16, row.shape[1]), 0)
    a, b, c = [x.astype(jnp.float32) for x in split3(row)]
    return jnp.where(place == 0, a, jnp.where(place == 1, b, jnp.where(place == 2, c, 0.0))).astype(jnp.bfloat16)


def each(count, body):
    if count <= 8:
        for e in range(count):
            body(e)
    else:
        def step(e, _):
            body(e)
            return 0
        lax.fori_loop(0, count, step, 0)


def slot_hot(slot_row, e, slot_rows):
    place = lax.broadcasted_iota(jnp.int32, (slot_rows, slot_row.shape[1]), 0) + e * slot_rows
    return (place == slot_row).astype(jnp.float32).astype(jnp.bfloat16)


def slots_kernel(routes_ref, rows_ref, slot_ref, out_ref, *, experts, capacity, slot_rows):
    f32, bf16 = jnp.float32, jnp.bfloat16
    tokens = routes_ref.shape[1]
    routes = routes_ref[...]
    pad = max(experts, 16)
    hot = (lax.broadcasted_iota(jnp.int32, (pad, tokens), 0) == routes).astype(f32)
    earlier = (
        lax.broadcasted_iota(jnp.int32, (tokens, tokens), 0) < lax.broadcasted_iota(jnp.int32, (tokens, tokens), 1)
    ).astype(f32).astype(bf16)
    ranks = dot_nn(hot.astype(bf16), earlier)
    rank = jnp.sum(ranks * hot, 0, keepdims=True).astype(jnp.int32)
    slot = jnp.where(rank < capacity, routes * slot_rows + rank, -1)
    slot_ref[...] = jnp.broadcast_to(slot, slot_ref.shape)

    def one(e):
        out_ref[e] = dot_nn(slot_hot(slot, e, slot_rows), rows_ref[...]).astype(bf16)
    each(experts, one)


def first_slots(routes_row, rows, experts, capacity, slot_rows):
    tokens, width = rows.shape
    vmem = pl.BlockSpec(memory_space=pltpu.VMEM)
    return pl.pallas_call(
        functools.partial(slots_kernel, experts=experts, capacity=capacity, slot_rows=slot_rows),
        out_shape=(
            jax.ShapeDtypeStruct((8, tokens), jnp.int32),
            jax.ShapeDtypeStruct((experts, slot_rows, width), jnp.bfloat16),
        ),
        in_specs=[vmem] * 2,
        out_specs=(vmem,) * 2,
        compiler_params=pltpu.CompilerParams(vmem_limit_bytes=60 << 20),
        cost_estimate=pl.CostEstimate(
            flops=2 * experts * slot_rows * tokens * width, bytes_accessed=4 << 20, transcendentals=0
        ),
    )(routes_row, rows)


def fill_masks(segment_row, qm, km):
    f32, bf16 = jnp.float32, jnp.bfloat16
    lane = lax.broadcasted_iota(jnp.int32, (1, LANES), 1)
    for b in range(qm.shape[0] // BLOCK):
        span = slice(b * BLOCK, (b + 1) * BLOCK)
        hot = (lax.broadcasted_iota(jnp.int32, (LANES, BLOCK), 0) == segment_row[:, span]).astype(f32).T
        qm[span, :] = (hot * masked_score).astype(bf16)
        km[span, :] = jnp.where(lane < 8, 1.0 - hot, 0.0).astype(bf16)


def fill_diag(grid_ref, diag, heads):
    bf16 = jnp.bfloat16
    buckets = grid_ref.shape[0]
    relative = 256 - lax.broadcasted_iota(jnp.int32, (buckets, 4 * LANES), 1)
    hot = (lax.broadcasted_iota(jnp.int32, (buckets, 4 * LANES), 0) == bucket_of(relative))
    hot = hot.astype(jnp.float32).astype(bf16)
    grid = jnp.concatenate(
        [grid_ref[...], jnp.zeros((buckets, LANES - heads), jnp.float32)], 1
    ).T[:16]
    total = None
    for piece in split3(grid):
        term = dot_nn(piece, hot)
        total = term if total is None else total + term
    diag[...] = total


def front_kernel(
    lo_ref, hi_ref, tokens, segment_row, slot_ref, routes_ref, gain_one, gain_two, wq, wk, wv, wo, grid_ref, router_t,
    q_ref, k_ref, kt_ref, v_ref, o_ref, lse_ref, middle_ref, probs_ref, xs_ref, gs_ref,
    vt_ref, qm_ref, km_ref, diag, bias, hidden, *, experts, slot_rows, scale,
):
    f32, bf16 = jnp.float32, jnp.bfloat16
    length, width = tokens.shape
    pairs = width // LANES
    nblk = length // BLOCK
    heads = grid_ref.shape[1]
    low = lax.broadcasted_iota(jnp.int32, (1, LANES), 1) < 64
    step = 256

    for b in range(length // step):
        span = slice(b * step, (b + 1) * step)
        x = tokens[span, :].astype(f32)
        inverse = lax.rsqrt(jnp.mean(x * x, 1, keepdims=True) + epsilon)
        normed = (x * inverse * gain_one[...]).astype(bf16)
        q_ref[span, :] = (dot_nn(normed, wq[...]).astype(bf16).astype(f32) * scale).astype(bf16)
        k = dot_nn(normed, wk[...]).astype(bf16)
        k_ref[span, :] = k
        kt_ref[:, span] = k.T
        v = dot_nn(normed, wv[...]).astype(bf16)
        v_ref[span, :] = v
        vt_ref[:, span] = v.T
    fill_masks(segment_row[...], qm_ref, km_ref)
    fill_diag(grid_ref, diag, heads)
    fill_bias(diag, bias, pairs)
    attend(lo_ref, hi_ref, q_ref, k_ref, vt_ref, qm_ref, km_ref, bias, o_ref, lse_ref)

    rw = two(router_t[...])
    routes = routes_ref[...]
    pad = router_t.shape[0]
    place = lax.broadcasted_iota(jnp.int32, (pad, step), 0)
    gates = []
    for b in range(length // step):
        span = slice(b * step, (b + 1) * step)
        middle = tokens[span, :].astype(f32) + dot_nn(o_ref[span, :], wo[...])
        middle_ref[span, :] = middle
        inverse = lax.rsqrt(jnp.mean(middle * middle, 1, keepdims=True) + epsilon)
        parts = two(middle * inverse * gain_two[...])
        hidden[span, :] = parts[0]
        logits = dot_nt(rw[0], parts[0]) + dot_nt(rw[0], parts[1]) + dot_nt(rw[1], parts[0])
        logits = jnp.where(place < experts, logits, -1e30)
        powers = jnp.exp(logits - jnp.max(logits, 0, keepdims=True))
        probs = powers / jnp.sum(powers, 0, keepdims=True)
        probs_ref[:, span] = probs
        gates.append(jnp.sum(jnp.where(place == routes[:, span], probs, 0.0), 0, keepdims=True))
    gates = row_pieces(jnp.concatenate(gates, 1))
    slot = slot_ref[0:1, :]
    lanes = gs_ref.shape[2]

    def one(e):
        hot = slot_hot(slot, e, slot_rows)
        xs_ref[e] = dot_nn(hot, hidden[...]).astype(bf16)
        if lanes > slot_rows:
            hot = jnp.concatenate([hot, jnp.zeros((lanes - slot_rows, length), bf16)], 0)
        row = jnp.sum(dot_nt(gates, hot), 0, keepdims=True)
        gs_ref[e] = jnp.broadcast_to(row, gs_ref.shape[1:])
    each(experts, one)


def front(lo, hi, tokens, segments, slot, routes_row, gain_one, gain_two, wq, wk, wv, wo, grid, router_t, experts, slot_rows, scale):
    length, width = tokens.shape
    heads = grid.shape[1]
    pairs = width // LANES
    nblk = length // BLOCK
    lanes = (slot_rows + LANES - 1) // LANES * LANES
    smem = pl.BlockSpec(memory_space=pltpu.SMEM)
    vmem = pl.BlockSpec(memory_space=pltpu.VMEM)
    f32, bf16 = jnp.float32, jnp.bfloat16
    shape = jax.ShapeDtypeStruct
    act = shape((length, width), bf16)
    return pl.pallas_call(
        functools.partial(front_kernel, experts=experts, slot_rows=slot_rows, scale=scale),
        out_shape=(
            act, act, shape((width, length), bf16), act, act,
            shape((nblk, 8, 2 * LANES), f32), shape((length, width), f32),
            shape((router_t.shape[0], length), f32),
            shape((experts, slot_rows, width), bf16), shape((experts, 8, lanes), f32),
        ),
        in_specs=[smem] * 2 + [vmem] * 12,
        out_specs=(vmem,) * 10,
        scratch_shapes=[
            pltpu.VMEM((width, length), bf16),
            pltpu.VMEM((length, LANES), bf16),
            pltpu.VMEM((length, LANES), bf16),
            pltpu.VMEM((16, 4 * LANES), f32),
            pltpu.VMEM((pairs, NEAR, BLOCK, 2 * LANES), f32),
            pltpu.VMEM((length, width), bf16),
        ],
        compiler_params=pltpu.CompilerParams(vmem_limit_bytes=60 << 20),
        cost_estimate=pl.CostEstimate(
            flops=4 * length * length * width + 12 * length * width * width, bytes_accessed=20 << 20,
            transcendentals=length * length * heads,
        ),
    )(lo, hi, tokens, segments, slot, routes_row, gain_one, gain_two, wq, wk, wv, wo, grid, router_t)


def back_kernel(
    lo_ref, hi_ref, home, home_gate, slot_ref, routes_ref, probs_ref, middle_ref, cotangent, segment_row, gain_two,
    wo, router_t, grid_ref, q_ref, k_ref, kt_ref, v_ref, lse_ref, o_ref,
    dq_ref, dk_ref, dv_ref, gsum_ref, middle_grad, router_grad, gain_grad,
    do_ref, qm_ref, km_ref, diag, bias, gacc, dkacc, dvacc, logit, *, experts, slot_rows, scale,
):
    f32, bf16 = jnp.float32, jnp.bfloat16
    length, width = middle_ref.shape
    pairs = width // LANES
    pad = router_t.shape[0]
    heads = grid_ref.shape[1]
    slot = slot_ref[0:1, :]
    lanes = home_gate.shape[2]

    gate_grad = [jnp.zeros((16, length), f32)]
    if experts <= 8:
        total = jnp.zeros((16, length), f32)
        for e in range(experts):
            total = total + dot_nn(row_pieces(home_gate[e, 0:1, :])[:, :slot_rows], slot_hot(slot, e, slot_rows))
    else:
        def add(e, total):
            return total + dot_nn(row_pieces(home_gate[e, 0:1, :])[:, :slot_rows], slot_hot(slot, e, slot_rows))
        total = lax.fori_loop(0, experts, add, jnp.zeros((16, length), f32))
    gate_grad = jnp.sum(total, 0, keepdims=True)
    place = lax.broadcasted_iota(jnp.int32, (pad, length), 0)
    hot = place == routes_ref[...]
    probs = probs_ref[...]
    gate = jnp.sum(jnp.where(hot, probs, 0.0), 0, keepdims=True)
    logit[...] = probs * (jnp.where(hot, gate_grad, 0.0) - gate * gate_grad)
    rw = two(router_t[...])
    slots = experts * slot_rows
    router_sum = jnp.zeros((pad, width), f32)
    gain_sum = jnp.zeros((1, width), f32)
    step = 256
    for b in range(length // step):
        span = slice(b * step, (b + 1) * step)
        hots = []
        for c in range(b * step, (b + 1) * step, BLOCK):
            column = jnp.broadcast_to(slot[:, c : c + BLOCK].astype(f32), (BLOCK, BLOCK)).T
            first = lax.broadcasted_iota(jnp.int32, (BLOCK, LANES), 1).astype(f32)
            hots.append(jnp.concatenate(
                [(column == first + float(s)).astype(f32).astype(bf16) for s in range(0, slots, LANES)], 1))
        spread = jnp.concatenate(hots, 0)
        hidden_grad = dot_nn(spread, home[...].reshape(slots, width))
        lg = two(logit[:, span])
        hidden_grad = hidden_grad + (
            matmul_tn(lg[0], rw[0]) + matmul_tn(lg[0], rw[1]) + matmul_tn(lg[1], rw[0])
        )
        middle = middle_ref[span, :]
        inverse = lax.rsqrt(jnp.mean(middle * middle, 1, keepdims=True) + epsilon)
        unit = middle * inverse
        hidden = two(unit * gain_two[...])
        router_sum = router_sum + (dot_nn(lg[0], hidden[0]) + dot_nn(lg[0], hidden[1]) + dot_nn(lg[1], hidden[0]))
        gain_sum = gain_sum + jnp.sum(hidden_grad * unit, 0, keepdims=True)
        scaled = hidden_grad * gain_two[...]
        mean = jnp.mean(scaled * middle, 1, keepdims=True)
        grad = cotangent[span, :].astype(f32) + inverse * (scaled - unit * (inverse * mean))
        middle_grad[span, :] = grad
        do_ref[span, :] = matmul_nt(grad.astype(bf16), wo[...]).astype(bf16)
    router_grad[...] = router_sum
    gain_grad[...] = gain_sum

    fill_masks(segment_row[...], qm_ref, km_ref)
    fill_diag(grid_ref, diag, heads)
    fill_bias(diag, bias, pairs)
    attend_back(
        lo_ref, hi_ref, q_ref, k_ref, kt_ref, v_ref, lse_ref, do_ref, o_ref, qm_ref, km_ref, bias,
        dq_ref, dk_ref, dv_ref, gsum_ref, gacc, dkacc, dvacc, scale,
    )


def back(lo, hi, home, home_gate, slot, routes_row, probs, middle, cotangent, segments, gain_two, wo, router_t, grid,
         q, k, kt, v, lse, o, experts, slot_rows, scale):
    length, width = middle.shape
    heads = grid.shape[1]
    pairs = width // LANES
    smem = pl.BlockSpec(memory_space=pltpu.SMEM)
    vmem = pl.BlockSpec(memory_space=pltpu.VMEM)
    f32, bf16 = jnp.float32, jnp.bfloat16
    shape = jax.ShapeDtypeStruct
    act = shape((length, width), bf16)
    return pl.pallas_call(
        functools.partial(back_kernel, experts=experts, slot_rows=slot_rows, scale=scale),
        out_shape=(
            act, act, act, shape((heads * NEAR, 2 * LANES), f32), shape((length, width), f32),
            shape((router_t.shape[0], width), f32), shape((1, width), f32),
        ),
        in_specs=[smem] * 2 + [vmem] * 18,
        out_specs=(vmem,) * 7,
        scratch_shapes=[
            pltpu.VMEM((length, width), bf16),
            pltpu.VMEM((length, LANES), bf16),
            pltpu.VMEM((length, LANES), bf16),
            pltpu.VMEM((16, 4 * LANES), f32),
            pltpu.VMEM((pairs, NEAR, BLOCK, 2 * LANES), f32),
            pltpu.VMEM((pairs, NEAR, BLOCK, 2 * LANES), f32),
            pltpu.VMEM((length, width), f32),
            pltpu.VMEM((length, width), f32),
            pltpu.VMEM((router_t.shape[0], length), f32),
        ],
        compiler_params=pltpu.CompilerParams(vmem_limit_bytes=60 << 20),
        cost_estimate=pl.CostEstimate(
            flops=10 * length * length * width + 6 * length * width * width, bytes_accessed=30 << 20,
            transcendentals=length * length * heads,
        ),
    )(lo, hi, home, home_gate, slot, routes_row, probs, middle, cotangent, segments, gain_two, wo, router_t, grid,
      q, k, kt, v, lse, o)


def gelu_parts(v):
    mag = jnp.abs(v)
    t = 1.0 / (1.0 + (0.3275911 * 0.7071067811865476) * mag)
    poly = t * (0.127414796 + t * (-0.142248368 + t * (0.7107068705 + t * (-0.7265760135 + t * 0.5307027145))))
    gauss = jnp.exp(-0.5 * v * v)
    tail = poly * gauss
    phi = jnp.where(v < 0, tail, 1.0 - tail)
    return v * phi, phi + v * gauss * 0.3989422804014327


def flip_bits(index, mask, count):
    out = 0
    bit = 1
    while bit < count:
        a, b = (index // bit) % 2, (mask // bit) % 2
        out = out + bit * (a + b - 2 * a * b)
        bit *= 2
    return out


def ffn_kernel(
    xs, gs, g, win_hbm, wout_hbm,
    home, home_gate, produced, keep, give,
    win, wout, xr, gr, act, pg, gated, igs, ggs, dws, dwr, stage,
    wsem, own_sem, psem, ksem, xsend, xrecv, gsend, grecv, isend, irecv, qsend, qrecv, dsend, drecv,
    *, groups, dp_size, tiles,
):
    f32, bf16 = jnp.float32, jnp.bfloat16
    me = lax.axis_index("expert")
    dp = lax.axis_index("dp")
    core = dp % 2
    sibling = dp + 1 - 2 * core
    rows = xs.shape[1]
    width = xs.shape[2]
    hidden = win.shape[1]
    tile = hidden // tiles
    lanes = gs.shape[2]

    def there(peer):
        return (dp, peer)

    load_in = pltpu.make_async_copy(win_hbm, win, wsem.at[0])
    load_out = pltpu.make_async_copy(wout_hbm, wout, wsem.at[1])
    load_in.start()
    load_out.start()
    load_g = pltpu.make_async_copy(g, gated, wsem.at[2])
    load_g.start()

    barrier = pltpu.get_barrier_semaphore()

    def greet(s, _):
        pl.semaphore_signal(
            barrier, inc=1, device_id=there(flip_bits(me, s, groups)), device_id_type=pl.DeviceIdType.MESH
        )
        return 0
    lax.fori_loop(1, groups, greet, 0)
    pl.semaphore_signal(barrier, inc=1, device_id=(sibling, me), device_id_type=pl.DeviceIdType.MESH)
    pl.semaphore_wait(barrier, groups)

    def x_copy(peer, slot):
        return pltpu.make_async_remote_copy(
            src_ref=xs.at[peer], dst_ref=xr.at[slot], send_sem=xsend.at[peer], recv_sem=xrecv.at[slot],
            device_id=there(peer), device_id_type=pl.DeviceIdType.MESH)

    def g_copy(peer, slot):
        return pltpu.make_async_remote_copy(
            src_ref=gs.at[peer], dst_ref=gr.at[slot], send_sem=gsend.at[peer], recv_sem=grecv.at[slot],
            device_id=there(peer), device_id_type=pl.DeviceIdType.MESH)

    def i_copy(peer, slot):
        return pltpu.make_async_remote_copy(
            src_ref=igs.at[peer], dst_ref=home.at[slot], send_sem=isend.at[peer], recv_sem=irecv.at[slot],
            device_id=there(peer), device_id_type=pl.DeviceIdType.MESH)

    def q_copy(peer, slot):
        return pltpu.make_async_remote_copy(
            src_ref=ggs.at[peer], dst_ref=home_gate.at[slot], send_sem=qsend.at[peer], recv_sem=qrecv.at[slot],
            device_id=there(peer), device_id_type=pl.DeviceIdType.MESH)

    def send(s, _):
        peer = flip_bits(me, s, groups)
        x_copy(peer, me).start()
        g_copy(peer, me).start()
        return 0
    lax.fori_loop(1, groups, send, 0)
    own_x = pltpu.make_async_copy(xs.at[me], xr.at[me], own_sem.at[0])
    own_g = pltpu.make_async_copy(gs.at[me], gr.at[me], own_sem.at[1])
    own_x.start()
    own_g.start()
    load_in.wait()
    load_out.wait()
    load_g.wait()

    spot = (
        lax.broadcasted_iota(jnp.int32, (rows, lanes), 0)
        == lax.broadcasted_iota(jnp.int32, (rows, lanes), 1)
    )

    def work(p):
        x = xr[p]
        place = pl.ds(pl.multiple_of(p * rows, rows), rows)
        gg = gated[place, :]
        gate = jnp.sum(jnp.where(spot, gr[p, 0:1, :], 0.0), 1, keepdims=True)
        gated[place, :] = (gate * gg.astype(f32)).astype(bf16)
        total = jnp.zeros((rows, width), f32)
        gate_grad = jnp.zeros((rows, 1), f32)
        for t in range(tiles):
            cols = slice(t * tile, (t + 1) * tile)
            pre = matmul(x, win[:, cols])
            out_grad = matmul_nt(gg, wout[cols, :])
            value, slope = gelu_parts(pre)
            act[place, cols] = value.astype(bf16)
            gate_grad = gate_grad + jnp.sum(value * out_grad, 1, keepdims=True)
            low = (gate * out_grad * slope).astype(bf16)
            pg[place, cols] = low
            total = total + matmul_nt(low, win[:, cols])
        igs[p] = total.astype(bf16)
        row = jnp.sum(jnp.where(spot, gate_grad, 0.0), 0, keepdims=True)
        ggs[p] = jnp.broadcast_to(row, ggs.shape[1:])

    own_x.wait()
    own_g.wait()
    work(me)
    own_i = pltpu.make_async_copy(igs.at[me], home.at[me], own_sem.at[0])
    own_q = pltpu.make_async_copy(ggs.at[me], home_gate.at[me], own_sem.at[1])
    own_i.start()
    own_q.start()

    def chunk(s, _):
        peer = flip_bits(me, s, groups)
        x_copy(peer, peer).wait_recv()
        g_copy(peer, peer).wait_recv()
        work(peer)
        i_copy(peer, me).start()
        q_copy(peer, me).start()
        return 0
    lax.fori_loop(1, groups, chunk, 0)

    def d_copy(k):
        return pltpu.make_async_remote_copy(
            src_ref=dws.at[k % 2], dst_ref=dwr.at[k], send_sem=dsend.at[k], recv_sem=drecv.at[k],
            device_id=(sibling, me), device_id_type=pl.DeviceIdType.MESH)

    part = hidden // dp_size
    flat = groups * rows
    items = [(which, half) for half in range(dp_size // 2) for which in range(2)]

    def grad(which, quarter):
        span = pl.ds(pl.multiple_of(quarter * part, part), part)
        if which == 0:
            return matmul_tn(xr[...].reshape(flat, width), pg[:, span])
        return matmul_tn(act[:, span], gated[...])

    half_of = dp // 2
    for k, (which, half) in enumerate(items):
        if k >= 2:
            d_copy(k - 2).wait_send()
        dws[k % 2] = grad(which, 2 * half + 1 - core).astype(bf16)
        d_copy(k).start()

    span = stage.shape[1]
    copies = []
    for b in range(flat // span):
        if b >= 2:
            copies[b - 2].wait()
        stage[b % 2] = matmul(act[b * span : (b + 1) * span, :], wout[...]).astype(bf16)
        copy = pltpu.make_async_copy(stage.at[b % 2], produced.at[pl.ds(b * span, span)], psem.at[b % 2])
        copy.start()
        copies.append(copy)
    for copy in copies[-2:]:
        copy.wait()
    for k, (which, half) in enumerate(items):
        local = grad(which, 2 * half + core)
        d_copy(k).wait_recv()
        both = (local + dwr[k].astype(f32)).astype(bf16)
        dwr[k] = both
    outs = []
    for which in range(2):
        outs.append(pltpu.make_async_copy(dwr.at[half_of * 2 + which], keep.at[which], ksem.at[which]))
        outs.append(pltpu.make_async_copy(dwr.at[(1 - half_of) * 2 + which], give.at[which], ksem.at[2 + which]))
    for copy in outs:
        copy.start()
    for copy in outs:
        copy.wait()
    own_i.wait()
    own_q.wait()
    for k in (2, 3):
        d_copy(k).wait_send()

    def finish(s, _):
        peer = flip_bits(me, s, groups)
        x_copy(peer, me).wait_send()
        g_copy(peer, me).wait_send()
        i_copy(peer, me).wait_send()
        q_copy(peer, me).wait_send()
        i_copy(peer, peer).wait_recv()
        q_copy(peer, peer).wait_recv()
        return 0
    lax.fori_loop(1, groups, finish, 0)


def ffn(xs, gs, g, weight_in, weight_out, groups, dp_size, tiles=6):
    f32, bf16 = jnp.float32, jnp.bfloat16
    _, rows, width = xs.shape
    hidden = weight_in.shape[1]
    lanes = gs.shape[2]
    part = hidden // dp_size
    anywhere = pl.BlockSpec(memory_space=pl.ANY)
    sem = pltpu.SemaphoreType.DMA
    flat = groups * rows
    shape = jax.ShapeDtypeStruct
    return pl.pallas_call(
        functools.partial(ffn_kernel, groups=groups, dp_size=dp_size, tiles=tiles),
        out_shape=(
            shape((groups, rows, width), bf16),
            shape((groups, 8, lanes), f32),
            shape((flat, width), bf16),
            shape((2, width, part), bf16),
            shape((2, width, part), bf16),
        ),
        in_specs=[anywhere] * 5,
        out_specs=(anywhere,) * 5,
        scratch_shapes=[
            pltpu.VMEM((width, hidden), bf16),
            pltpu.VMEM((hidden, width), bf16),
            pltpu.VMEM((groups, rows, width), bf16),
            pltpu.VMEM((groups, 8, lanes), f32),
            pltpu.VMEM((flat, hidden), bf16),
            pltpu.VMEM((flat, hidden), bf16),
            pltpu.VMEM((flat, width), bf16),
            pltpu.VMEM((groups, rows, width), bf16),
            pltpu.VMEM((groups, 8, lanes), f32),
            pltpu.VMEM((2, width, part), bf16),
            pltpu.VMEM((4, width, part), bf16),
            pltpu.VMEM((2, flat // 8, width), bf16),
            sem((3,)), sem((2,)), sem((2,)), sem((4,)),
            sem((groups,)), sem((groups,)), sem((groups,)), sem((groups,)),
            sem((groups,)), sem((groups,)), sem((groups,)), sem((groups,)),
            sem((4,)), sem((4,)),
        ],
        compiler_params=pltpu.CompilerParams(
            collective_id=1, has_side_effects=True, vmem_limit_bytes=62 << 20
        ),
        cost_estimate=pl.CostEstimate(
            flops=12 * flat * width * hidden, bytes_accessed=40 << 20, transcendentals=flat * hidden
        ),
    )(xs, gs, g, weight_in, weight_out)


def fold_steps(rows, cols, bits):
    steps = []
    for bit in bits:
        if rows % 32 == 0:
            rows = rows // 2
            steps.append((bit, "rows", rows, cols))
        elif cols % 256 == 0:
            cols = cols // 2
            steps.append((bit, "cols", rows, cols))
        else:
            steps.append((bit, "whole", rows, cols))
    return steps


def reduce_kernel(
    tokens, attended, middle_grad, dq, dk, dv, wq, wk, wv, gain, small_in,
    returned, slot_ref, routes_ref, probs_ref, middle,
    sums, token_grad, small_out, mixed,
    normed, branch, acc, outbox, inbox, small_box, small_sent,
    ssend, srecv, tsend, trecv,
    *, dp_bits, expert_bits,
):
    f32, bf16 = jnp.float32, jnp.bfloat16
    dp = lax.axis_index("dp")
    ex = lax.axis_index("expert")
    MESH = pl.DeviceIdType.MESH
    length, width = tokens.shape

    def own_bit(bit):
        axis, place = bit
        return (dp // 2 ** place) % 2 if axis == "dp" else (ex // 2 ** place) % 2

    def partner(bit):
        axis, place = bit
        flip = (1 - 2 * own_bit(bit)) * 2 ** place
        return (dp + flip, ex) if axis == "dp" else (dp, ex + flip)

    dpb = [("dp", i) for i in range(dp_bits)]
    exb = [("expert", i) for i in range(expert_bits)]
    orders = [
        [dpb[0], dpb[1], exb[0]] + dpb[2:] + exb[1:],
        [dpb[0], exb[0], dpb[1]] + dpb[2:] + exb[1:],
    ]
    every = dpb + exb
    count = len(every)

    barrier = pltpu.get_barrier_semaphore()
    for bit in every:
        pl.semaphore_signal(barrier, inc=1, device_id=partner(bit), device_id_type=MESH)
    pl.semaphore_wait(barrier, count)

    def prepare(i, _):
        span = pl.ds(pl.multiple_of(i * 256, 256), 256)
        x = tokens[span, :].astype(f32)
        inv = lax.rsqrt(jnp.mean(x * x, 1, keepdims=True) + epsilon)
        normed[span, :] = (x * inv * gain[...]).astype(bf16)
        branch[span, :] = middle_grad[span, :].astype(bf16)
        return 0
    lax.fori_loop(0, length // 256, prepare, 0)

    lefts = (attended, normed, normed, normed)
    rights = (branch, dv, dk, dq)
    streams = []
    for s in range(4):
        steps = fold_steps(width, width, orders[s % 2])
        row, col = 0, 0
        at = 0
        plan = []
        for bit, kind, r, c in steps:
            mine = own_bit(bit)
            if kind == "rows":
                keep_at, send_at = (row + mine * r, col), (row + (1 - mine) * r, col)
            elif kind == "cols":
                keep_at, send_at = (row, col + mine * c), (row, col + (1 - mine) * c)
            else:
                keep_at, send_at = (row, col), (row, col)
            plan.append((bit, kind, r, c, at, keep_at, send_at))
            row, col = keep_at
            at += r
        streams.append(plan)

    def rs_copy(s, k):
        bit, kind, r, c, at, _, _ = streams[s][k]
        return pltpu.make_async_remote_copy(
            src_ref=outbox.at[s, pl.ds(at, r), pl.ds(0, c)],
            dst_ref=inbox.at[s, pl.ds(at, r), pl.ds(0, c)],
            send_sem=ssend.at[s, k], recv_sem=srecv.at[s, k],
            device_id=partner(bit), device_id_type=MESH)

    def block(s, at, r, c):
        row, col = at
        row = pl.multiple_of(row, 16) if not isinstance(row, int) else row
        col = pl.multiple_of(col, 128) if not isinstance(col, int) else col
        return sums.at[s, pl.ds(row, r), pl.ds(col, c)]

    def ag_copy(s, k, incoming):
        bit, kind, r, c, _, keep_at, send_at = streams[s][k]
        ref = block(s, send_at if incoming else keep_at, r, c)
        return pltpu.make_async_remote_copy(
            src_ref=ref, dst_ref=ref,
            send_sem=ssend.at[s, count + k], recv_sem=srecv.at[s, count + k],
            device_id=partner(bit), device_id_type=MESH)

    half = width // 2
    core = own_bit(dpb[0])

    def grad(s, which):
        span = pl.ds(pl.multiple_of(which * half, half), half)
        return matmul_tn(lefts[s][:, span], rights[s][...])

    def local(s, k, at):
        base = streams[s][0][5][0]
        row, col = at
        row = row - base
        row = pl.multiple_of(row, 16) if not isinstance(row, int) else row
        col = pl.multiple_of(col, 128) if not isinstance(col, int) else col
        return row, col

    def phase(s, k):
        plan = streams[s]
        if k == 0:
            outbox[s, 0:half, :] = grad(s, 1 - core).astype(bf16)
            rs_copy(s, 0).start()
            acc[s] = grad(s, core)
            return
        if k <= count:
            bit, kind, r, c, at, keep_at, _ = plan[k - 1]
            rs_copy(s, k - 1).wait_recv()
            row, col = local(s, k - 1, keep_at)
            view = acc.at[s, pl.ds(row, r), pl.ds(col, c)]
            own = outbox[s, at : at + r, 0:c].astype(f32) if kind == "whole" else view[...]
            view[...] = own + inbox[s, at : at + r, 0:c].astype(f32)
            if k < count:
                bit, kind, r, c, at, keep_at, send_at = plan[k]
                row, col = local(s, k, send_at)
                outbox[s, at : at + r, 0:c] = acc[s, pl.ds(row, r), pl.ds(col, c)].astype(bf16)
                rs_copy(s, k).start()
                return
            block(s, keep_at, r, c)[...] = view[...].astype(bf16)
        g = 2 * count - 1 - k
        if k > count:
            prev = g + 1
            if plan[prev][1] != "whole":
                ag_copy(s, prev, True).wait_recv()
        if g >= 0 and plan[g][1] != "whole":
            ag_copy(s, g, False).start()

    gain_row = gain[...]
    rows = 256

    def norm_block(i, gain_grad):
        span = pl.ds(pl.multiple_of(i * rows, rows), rows)
        grads = (
            matmul_nt(dq[span, :], wq[...]) + matmul_nt(dk[span, :], wk[...]) + matmul_nt(dv[span, :], wv[...])
        )
        x = tokens[span, :].astype(f32)
        inv = lax.rsqrt(jnp.mean(x * x, 1, keepdims=True) + epsilon)
        scaled = grads * gain_row
        mean = jnp.sum(scaled * x, 1, keepdims=True) * (1.0 / width)
        part = inv * (scaled - x * (inv * inv * mean))
        token_grad[span, :] = (middle_grad[span, :] + part).astype(bf16)
        return gain_grad + jnp.sum(grads * (x * inv), 0, keepdims=True)

    slots = returned.shape[0]
    routes = routes_ref[...]
    pad = probs_ref.shape[0]
    hot = lax.broadcasted_iota(jnp.int32, (pad, length), 0) == routes
    gate_row = jnp.sum(jnp.where(hot, probs_ref[...], 0.0), 0, keepdims=True)

    def mix(c):
        at = slice(c, c + BLOCK)
        column = jnp.broadcast_to(slot_ref[0:1, at].astype(f32), (BLOCK, BLOCK)).T
        first = lax.broadcasted_iota(jnp.int32, (BLOCK, LANES), 1).astype(f32)
        spread = jnp.concatenate(
            [(column == first + float(s)).astype(f32).astype(bf16) for s in range(0, slots, LANES)], 1)
        rows_back = dot_nn(spread, returned[...])
        gate = jnp.broadcast_to(gate_row[:, at], (BLOCK, BLOCK)).T
        gate = jnp.concatenate([gate] * (width // LANES), 1)
        mixed[at, :] = (middle[at, :] + gate * rows_back).astype(bf16)

    def small_copy(k):
        return pltpu.make_async_remote_copy(
            src_ref=small_sent.at[k], dst_ref=small_box.at[k],
            send_sem=tsend.at[k], recv_sem=trecv.at[k],
            device_id=partner(every[k]), device_id_type=MESH)

    def small_phase(k):
        if k == 0:
            gain_grad = lax.fori_loop(0, length // rows, norm_block, jnp.zeros((1, width), f32))
            small_out[...] = small_in[...]
            for i in range(width // LANES):
                small_out[i : i + 1, :] = gain_grad[:, i * LANES : (i + 1) * LANES]
        else:
            small_copy(k - 1).wait_recv()
            small_out[...] = small_out[...] + small_box[k - 1]
        if k < count:
            small_sent[k] = small_out[...]
            small_copy(k).start()

    last = 2 * count
    for t in range(last + 4):
        for s in range(4):
            if 0 <= t - s <= last:
                phase(s, t - s)
        if 4 <= t and t - 4 <= count:
            small_phase(t - 4)
        if 5 <= t and t - 5 < length // BLOCK:
            mix((t - 5) * BLOCK)
    for s in range(4):
        for k in range(count):
            rs_copy(s, k).wait_send()
            if streams[s][k][1] != "whole":
                ag_copy(s, k, False).wait_send()
    for k in range(count):
        small_copy(k).wait_send()


def reduce_grads(tokens, attended, middle_grad, dq, dk, dv, wq, wk, wv, gain, small,
                 returned, slot, routes_row, probs, middle, dp_size, groups):
    f32, bf16 = jnp.float32, jnp.bfloat16
    length, width = tokens.shape
    dp_bits, expert_bits = dp_size.bit_length() - 1, groups.bit_length() - 1
    count = dp_bits + expert_bits
    box = sum(step[2] for step in fold_steps(width, width, range(count)))
    vmem = pl.BlockSpec(memory_space=pltpu.VMEM)
    sem = pltpu.SemaphoreType.DMA
    shape = jax.ShapeDtypeStruct
    return pl.pallas_call(
        functools.partial(reduce_kernel, dp_bits=dp_bits, expert_bits=expert_bits),
        out_shape=(shape((4, width, width), bf16), shape((length, width), bf16), shape(small.shape, f32),
                   shape((length, width), bf16)),
        in_specs=[vmem] * 16,
        out_specs=(vmem,) * 4,
        scratch_shapes=[
            pltpu.VMEM((length, width), bf16),
            pltpu.VMEM((length, width), bf16),
            pltpu.VMEM((4, width // 2, width), f32),
            pltpu.VMEM((4, box, width), bf16),
            pltpu.VMEM((4, box, width), bf16),
            pltpu.VMEM((count,) + small.shape, f32),
            pltpu.VMEM((count,) + small.shape, f32),
            sem((4, 2 * count)), sem((4, 2 * count)), sem((count,)), sem((count,)),
        ],
        compiler_params=pltpu.CompilerParams(
            collective_id=2, has_side_effects=True, vmem_limit_bytes=62 << 20
        ),
        cost_estimate=pl.CostEstimate(
            flops=14 * length * width * width, bytes_accessed=30 << 20, transcendentals=0
        ),
    )(tokens, attended, middle_grad, dq, dk, dv, wq, wk, wv, gain, small, returned, slot, routes_row, probs, middle)


def key_ranges(segment_row):
    first, last = segment_row[::BLOCK], segment_row[BLOCK - 1 :: BLOCK]
    lo = jnp.sum(segment_row[None, :] < first[:, None], 1) // BLOCK
    hi = (jnp.sum(segment_row[None, :] <= last[:, None], 1) + BLOCK - 1) // BLOCK
    return lo.astype(jnp.int32), hi.astype(jnp.int32)


def bias_grad(sums, heads, bucket_count):
    near = lax.broadcasted_iota(jnp.int32, (NEAR, 2 * LANES), 0)
    place = lax.broadcasted_iota(jnp.int32, (NEAR, 2 * LANES), 1)
    bucket = bucket_of((near - 2) * BLOCK + BLOCK - 1 - place)
    bucket = jnp.where(near == 0, 15, jnp.where(near == NEAR - 1, 31, bucket))
    hot = (bucket.reshape(-1)[:, None] == lax.iota(jnp.int32, bucket_count)[None, :]).astype(jnp.float32)
    return jnp.dot(sums.reshape(heads, -1), hot, precision=precise_setting).T


def per_device(
    tokens,
    segments,
    routes,
    cotangent,
    attn_gain,
    ffn_gain,
    query_weight,
    key_weight,
    value_weight,
    output_weight,
    position_bias_grid,
    router_weight,
    expert_in,
    expert_out,
):
    f32, bf16 = jnp.float32, jnp.bfloat16
    token_count, model_width = tokens.shape
    bucket_count, head_count = position_bias_grid.shape
    score_scale = (model_width // head_count) ** (-0.5)
    experts_all = router_weight.shape[1]
    capacity = (5 * token_count + 4 * experts_all - 1) // (4 * experts_all)
    slot_rows = (capacity + 15) // 16 * 16
    slots = experts_all * slot_rows
    groups = lax.axis_size("expert")
    dp_size = lax.axis_size("dp")

    def exchange(rows):
        return lax.all_to_all(rows, "expert", split_axis=0, concat_axis=0, tiled=True)

    routes_row = routes.reshape(1, token_count)
    token_slot, grad_slots = first_slots(routes_row, cotangent, experts_all, capacity, slot_rows)
    grad_arrived = exchange(grad_slots)
    lo, hi = key_ranges(segments[0])
    router_pad = max(experts_all, 16)
    router_t = jnp.pad(router_weight.T, ((0, router_pad - experts_all), (0, 0)))
    gain_one, gain_two = attn_gain[None, :], ffn_gain[None, :]
    queries, key_rows, keys_t, value_rows, attended, log_sums, middle, router_probs, sent, gate_slots = front(
        lo, hi, tokens, segments, token_slot, routes_row, gain_one, gain_two,
        query_weight, key_weight, value_weight, output_weight, position_bias_grid, router_t,
        experts_all, slot_rows, score_scale,
    )
    home_grad, home_gate, produced, keep, give = ffn(
        sent, gate_slots, grad_arrived.reshape(slots, model_width), expert_in[0], expert_out[0], groups, dp_size,
    )
    passed = lax.ppermute(give, "dp", [(i, (i + dp_size // 2) % dp_size) for i in range(dp_size)])
    weight_grads = keep.astype(f32) + passed.astype(f32)
    in_weight_grad, out_weight_grad = weight_grads[0], weight_grads[1]
    returned = exchange(produced.reshape(experts_all, slot_rows, model_width)).reshape(slots, model_width)
    query_grad, key_grad, value_grad, diag_sums, middle_grad, router_grad, ffn_gain_grad = back(
        lo, hi, home_grad, home_gate, token_slot, routes_row, router_probs, middle, cotangent, segments, gain_two,
        output_weight, router_t, position_bias_grid, queries, key_rows, keys_t, value_rows, log_sums, attended,
        experts_all, slot_rows, score_scale,
    )
    table_grad = bias_grad(diag_sums, head_count, bucket_count)
    router_grad = router_grad[:experts_all]
    flat = jnp.concatenate(
        [jnp.zeros((model_width,), f32), ffn_gain_grad.reshape(-1), router_grad.reshape(-1), table_grad.reshape(-1)]
    )
    small_rows = -(-flat.shape[0] // (8 * LANES)) * 8
    small = jnp.pad(flat, (0, small_rows * LANES - flat.shape[0])).reshape(small_rows, LANES)
    weights, token_grad, small, mixed = reduce_grads(
        tokens, attended, middle_grad, query_grad, key_grad, value_grad,
        query_weight, key_weight, value_weight, gain_one, small,
        returned, token_slot, routes_row, router_probs, middle, dp_size, groups,
    )
    weights = weights.astype(f32)
    flat = small.reshape(-1)
    ends = [model_width, 2 * model_width]
    ends.append(ends[-1] + router_grad.size)
    ends.append(ends[-1] + table_grad.size)
    return (
        mixed,
        token_grad,
        flat[: ends[0]],
        flat[ends[0] : ends[1]],
        weights[3],
        weights[2],
        weights[1],
        weights[0],
        flat[ends[2] : ends[3]].reshape(table_grad.shape),
        flat[ends[1] : ends[2]].reshape(experts_all, model_width).T,
        in_weight_grad[None],
        out_weight_grad[None],
    )


def solution(mesh):
    rows = P(("dp", "expert"), None)
    return jax.shard_map(
        per_device,
        mesh=mesh,
        in_specs=(rows,) * 4 + (P(),) * 8 + (P("expert", None, None),) * 2,
        out_specs=(rows,) * 2 + (P(),) * 8 + (P("expert", None, "dp"), P("expert", "dp", None)),
        check_vma=False,
    )
```

time: 436 us -> 342 us (0.78)
  matrix products: 54.2 us -> 0.72 us
  Pallas kernels: 303 us -> 276 us
  starting transfers between devices: 35 us -> 21.8 us
  waiting for transfers between devices: 0.01 us -> 10.9 us
  other arithmetic: 15.2 us -> 7.53 us
    dot_general x16 -> x0, matrix products: 53.5 us -> none  [the longest x8 25.6 us: matmul(): return jnp.dot(left, right, preferred_element_type=jnp.float32)]
    pallas_call x2 -> x3, Pallas kernels: 113 us -> 76.2 us  [the longest x1 40.7 us: back(): pl.pallas_call(functools.partial(back_kernel, experts=experts, slot_rows=...]
    all_to_all x2, waiting for transfers between devices: 0.01 us -> 10.9 us  [exchange(): lax.all_to_all(rows, 'expert', split_axis=0, concat_axis=0, tiled=True)]
    ppermute x1, starting transfers between devices: 11.1 us -> 1.2 us  [per_device(): lax.ppermute(give, 'dp', [(i, (i + dp_size // 2) % dp_size) for i in rang...]
    pallas_call x1, Pallas kernels: 106 us -> 116 us  [reduce_grads(): pl.pallas_call(functools.partial(reduce_kernel, dp_bits=dp_bits, expert_b...]
    convert_element_type x8 -> x0, other arithmetic: 6.51 us -> none  [the longest x1 3.1 us: per_device(): branch_grad = middle_grad.astype(bf16)]
  transfers between devices with their start and end apart: 3 -> 3, of which waited for: 0 -> 1; matrix products, arithmetic and copies ran while one was open for 17% -> 4% of each run, Pallas kernels for 51% -> 21%
where the time goes in v4:
time: 342 us; the launch traced here: 336 us
  Pallas kernels  276 us (81%)
  starting transfers between devices  21.8 us (6%)
  local copies, waits for them, and re-layouts  18.6 us (5%)
  waiting for transfers between devices  10.9 us (3%)
  other arithmetic  7.53 us (2%)
    pallas_call x1, Pallas kernels, reduce_grads(): pl.pallas_call(functools.partial(reduce_kernel, dp_bits=dp_bits, expert_b...  116 us
    pallas_call x1, Pallas kernels, ffn(): pl.pallas_call(functools.partial(ffn_kernel, groups=groups, dp_size=dp_si...  84 us
    pallas_call x1, Pallas kernels, back(): pl.pallas_call(functools.partial(back_kernel, experts=experts, slot_rows=...  40.7 us
    pallas_call x1, Pallas kernels, front(): pl.pallas_call(functools.partial(front_kernel, experts=experts, slot_rows...  30.2 us
    all_to_all x2, starting transfers between devices, exchange(): lax.all_to_all(rows, 'expert', split_axis=0, concat_axis=0, tiled=True)  20.6 us
    all_to_all x2, waiting for transfers between devices, exchange(): lax.all_to_all(rows, 'expert', split_axis=0, concat_axis=0, tiled=True)  10.9 us
  transfers between devices with their start and end apart: 3, of which 1 were waited for; matrix products, arithmetic and copies ran while one was open for 4% of the time, Pallas kernels for 21%

profile of v4, /device:TPU:1, one launch (start us, length us, event | category | flops | bytes accessed | tf_op | source)
XLA Modules:
  0.0 336.4 jit_solution(9387511472437021195)
XLA Ops:
  0.6 5.3 %shard_map.229 = (s32[8,1024]{1,0:T(8,128)}, bf16[8,160,768]{2,1,0:T(8,128)(2,1)}) custom-call(s32[1,1024]{1,0:T(1,128)} %bitcast.33, bf16[1024,768]{1,0:T(8,128)(2,1)} %cotangent.1), custom_call_target="tpu_custom_call" | custom-call | flops 2013265920 | bytes 4194304 | tf_op jit(solution)/shard_map/pallas_call | solution.py:303
  5.9 0.0 copy-start.4
  5.9 6.5 %all-to-all-start = ((bf16[8,160,768]{2,1,0:T(8,128)(2,1)}), bf16[8,160,768]{2,1,0:T(8,128)(2,1)S(1)}, u32[]{:S(2)}, u32[]{:S(2)}) async-start(bf16[8,160,768]{2,1,0:T(8,128)(2,1)} %get-tuple-element.44), calls=%async_computation | async-start | bytes 3932160 | tf_op jit(solution)/shard_map/all_to_all | solution.py:1097
  12.5 0.0 copy-done.8
  12.5 0.1 slice.47
  12.6 0.1 slice.48
  12.7 0.0 copy-done.5
  12.7 0.7 copy.33.grid_ref
  13.4 0.0 copy-done.6
  13.4 0.6 broadcast_in_dim.19.gain_one.gain
  13.9 0.0 copy-done.7
  13.9 0.6 broadcast_in_dim.20.gain_two
  14.5 0.0 copy-done.4
  14.5 0.6 pad.8.router_t
  15.2 0.2 convert_reduce_fusion
  15.4 0.6 and_select_fusion
  16.0 30.2 %shard_map.230 = (bf16[1024,768]{1,0:T(8,128)(2,1)}, bf16[1024,768]{1,0:T(8,128)(2,1)}, bf16[768,1024]{1,0:T(8,128)(2,1)}, bf16[1024,768]{1,0:T(8,128)(2,1)}, bf...) custom-call(s32[8]{0:T(128)} %get-tuple-element.117.lo_ref, ...), custom_call_target="tpu_custom_call" | custom-call | flops 10468982784 | bytes 20971520 | tf_op jit(solution)/shard_map/pallas_call | solution.py:417
  46.2 10.9 %all-to-all-done = bf16[8,160,768]{2,1,0:T(8,128)(2,1)S(1)} async-done(((bf16[8,160,768]{2,1,0:T(8,128)(2,1)}), bf16[8,160,768]{2,1,0:T(8,128)(2,1)S(1)}, u32[]{:S(2)}, u32[]{:S(2)}) %all-to-all-start) | async-done | bytes 1966112 | tf_op jit(solution)/shard_map/all_to_all | solution.py:1097
  57.0 1.3 copy-done.1
  58.3 84.0 %shard_map.231 = (bf16[8,160,768]{2,1,0:T(8,128)(2,1)}, f32[8,8,256]{2,1,0:T(8,128)}, bf16[1280,768]{1,0:T(8,128)(2,1)}, bf16[2,768,768]{2,1,0:T(8,128)(2,1)}, bf16[2,768,768]{2,1,0:T(8,128)(2,1)}) custom-call(bf16[8,160,768]{2,1,0:T(8,128)(2,1)} %get-tuple-element.42.xs, f32[8,8,256]{2,1,0:T(8,128)} %get-tuple-element.43.gs, bf16[1280,768]{1,0:T(8,128)(2,1)} %bitcast.25, ...), custom_call_target="tpu_custom_call" | custom-call | flops 36238786560 | bytes 41943040 | tf_op jit(solution)/shard_map/pallas_call | solution.py:763
  142.3 14.1 %all-to-all-start.1 = ((bf16[8,160,768]{2,1,0:T(8,128)(2,1)}), bf16[8,160,768]{2,1,0:T(8,128)(2,1)}, u32[]{:S(2)}, u32[]{:S(2)}) async-start(bf16[8,160,768]{2,1,0:T(8,128)(2,1)} %bitcast.24), calls=%async_computation.1 | async-start | bytes 3932160 | tf_op jit(solution)/shard_map/all_to_all | solution.py:1097
  156.4 1.2 collective-permute-start
  157.6 0.1 fusion.9
  157.7 0.1 iota.26
  157.8 0.1 iota.28
  157.9 40.7 %shard_map.232 = (bf16[1024,768]{1,0:T(8,128)(2,1)}, bf16[1024,768]{1,0:T(8,128)(2,1)}, bf16[1024,768]{1,0:T(8,128)(2,1)}, f32[60,256]{1,0:T(8,128)}, f32[1024,7...) custom-call(s32[8]{0:T(128)} %get-tuple-element.117.lo_ref, s32[8]{0:T(128)} %get-tuple-element.116.hi_ref, ...), custom_call_target="tpu_custom_call" | custom-call | flops 11676942336 | bytes 31457280 | tf_op jit(solution)/shard_map/pallas_call | solution.py:524
  198.6 0.9 reshape.134
  199.5 0.7 fusion.1
  200.2 0.1 reshape.135
  200.3 0.7 slice.49
  201.1 0.7 reduce
  201.8 0.6 fusion.4.small_in
  202.4 0.0 collective-permute-done
  202.4 0.0 copy-done
  202.4 2.1 convert_add_fusion
  204.6 2.5 fusion.13
  207.0 0.0 all-to-all-done.1
  207.0 115.6 %shard_map.233 = (bf16[4,768,768]{2,1,0:T(8,128)(2,1)}, bf16[1024,768]{1,0:T(8,128)(2,1)}, f32[64,128]{1,0:T(8,128)}, bf16[1024,768]{1,0:T(8,128)(2,1)}) custom-call(bf16[1024,768]{1,0:T(8,128)(2,1)} %tokens.3, bf16[1024,768]{1,0:T(8,128)(2,1)} %get-tuple-element.41.o_ref.attended, f32[1024,768]{1,0:T(8,128)} %get-tuple-element.54.middle_grad, ...), custom_call_target="tpu_custom_call" | custom-call | flops 8455716864 | bytes 31457280 | tf_op jit(solution)/shard_map/pallas_call | solution.py:1028
  322.7 0.8 slice.59
  323.4 0.7 slice.58
  324.1 1.4 slice_bitcast_fusion.4
  325.5 3.2 convert_element_type.79
  328.7 3.8 %slice_bitcast_fusion = (f32[768,768]{1,0:T(8,128)}, f32[768,768]{1,0:T(8,128)}, f32[768,768]{1,0:T(8,128)}, f32[768,768]{1,0:T(8,128)}) fusion(f32[4,768,768]{2,1,0:T(8,128)S(1)} %convert_element_type.79), kind=kLoop, calls=%fused_computation.1 | loop fusion | bytes 18874368 | tf_op jit(solution)/shard_map/squeeze | solution.py:1148
  332.5 0.6 reshape.140
  333.1 0.1 reshape.139
  333.2 0.7 copy.36
  333.9 1.1 copy.40
  335.0 1.1 copy.41
  (20 shorter events, 0.1 us)
Async XLA Ops:
  5.9 6.6 %copy-start.8 = (s32[1,1024]{1,0:T(1,128)S(1)}, s32[1,1024]{1,0:T(1,128)}, u32[]{:S(2)}) copy-start(s32[1,1024]{1,0:T(1,128)} %segment_row.3) | copy-start | bytes 12292
  5.9 6.7 %copy-start.5 = (f32[32,12]{0,1:T(8,128)S(1)}, f32[32,12]{0,1:T(8,128)}, u32[]{:S(2)}) copy-start(f32[32,12]{0,1:T(8,128)} %param.24) | copy-start | bytes 4612
  5.9 7.4 %copy-start.6 = (f32[768]{0:T(1024)S(1)}, f32[768]{0:T(1024)}, u32[]{:S(2)}) copy-start(f32[768]{0:T(1024)} %param.18) | copy-start | bytes 9220
  5.9 8.0 %copy-start.7 = (f32[768]{0:T(1024)S(1)}, f32[768]{0:T(1024)}, u32[]{:S(2)}) copy-start(f32[768]{0:T(1024)} %param.19) | copy-start | bytes 9220
  5.9 8.6 %copy-start.4 = (f32[768,8]{0,1:T(8,128)S(1)}, f32[768,8]{0,1:T(8,128)}, u32[]{:S(2)}) copy-start(f32[768,8]{0,1:T(8,128)} %param.25) | copy-start | bytes 73732
  5.9 51.1 %all-to-all-start = ((bf16[8,160,768]{2,1,0:T(8,128)(2,1)}), bf16[8,160,768]{2,1,0:T(8,128)(2,1)S(1)}, u32[]{:S(2)}, u32[]{:S(2)}) async-start(bf16[8,160,768]{2,1,0:T(8,128)(2,1)} %get-tuple-element.44), calls=%async_computation | async-start | bytes 3932160 | tf_op jit(solution)/shard_map/all_to_all | solution.py:1097
  57.0 1.3 copy-start.1
  142.3 64.7 %all-to-all-start.1 = ((bf16[8,160,768]{2,1,0:T(8,128)(2,1)}), bf16[8,160,768]{2,1,0:T(8,128)(2,1)}, u32[]{:S(2)}, u32[]{:S(2)}) async-start(bf16[8,160,768]{2,1,0:T(8,128)(2,1)} %bitcast.24), calls=%async_computation.1 | async-start | bytes 3932160 | tf_op jit(solution)/shard_map/all_to_all | solution.py:1097
  156.4 46.0 %collective-permute-start = (bf16[2,768,768]{2,1,0:T(8,128)(2,1)}, bf16[2,768,768]{2,1,0:T(8,128)(2,1)}, u32[]{:S(2)}, u32[]{:S(2)}) collective-permute-start(bf16[2,768,768]{2,1,0:T(8,128)(2,1)} %get-tuple-element.67), channel_id=1, source_target_pairs={{0,16},{8,24},{16,0},{24,8},{1,17},{9,25},{17,1},{25,9},{2,18},{10... | collective-permute-start | bytes 7077896 | tf_op jit(solution)/shard_map/ppermute | solution.py:1114
  157.9 44.5 %copy-start = (bf16[2,768,768]{2,1,0:T(8,128)(2,1)S(1)}, bf16[2,768,768]{2,1,0:T(8,128)(2,1)}, u32[]{:S(2)}) copy-start(bf16[2,768,768]{2,1,0:T(8,128)(2,1)} %get-tuple-element.66) | copy-start | bytes 7077892
  328.6 5.2 %copy-start.3 = (bf16[1024,768]{1,0:T(8,128)(2,1)S(1)}, bf16[1024,768]{1,0:T(8,128)(2,1)}, u32[]{:S(2)}) copy-start(bf16[1024,768]{1,0:T(8,128)(2,1)} %get-tuple-element.130) | copy-start | bytes 4718596
  332.5 2.5 copy-start.2
